TPU v7x, 32 devices: a whole 2x2x4 slice. The times are simulated.
32 devices in a mesh: clip: 4 (over y, x), frame: 4 (over z), tile: 2 (over core).
Axes of the slice: x: 2, y: 2, z: 4, core: 2. Of those that a mesh axis runs over, the one named last changes fastest.
Arguments:
- clip_feats: bfloat16 [128, 8, 16, 256], P(('clip', 'frame'), 'tile'), parts along dimension 0, may hold values from -6 to 6
- out_grad: bfloat16 [128, 8, 16, 256], P(('clip', 'frame'), 'tile'), parts along dimension 0, may hold values from -6 to 6
- spatial_weight: bfloat16 [2304, 256], replicated, may hold values from -0.125 to 0.125
- temporal_weight: bfloat16 [2304, 256], replicated, may hold values from -0.125 to 0.125
Outputs:
- block_out: bfloat16 [128, 8, 16, 256], P(('clip', 'frame'), 'tile'), parts along dimension 0
- input_grad: bfloat16 [128, 8, 16, 256], P(('clip', 'frame'), 'tile'), parts along dimension 0
- weight_grad: float32 [9216, 256], P(('clip', 'frame', 'tile')), parts along dimension 0
There are 4 independent parts, one for each index of `clip`. A program takes and returns all parts, laid end to end along the dimension named above; an argument that names none is the same for every part. Nothing has to cross between parts.
All inputs are finite; a program needn't handle non-finite values.
Results may differ from a plain program's by a relative error of at most 0.009.
Values may be sent and summed in bfloat16 or wider, within the bound.
No kernel may reach another device: no remote copies, remote signals or barrier semaphores. Data moves between devices by JAX's collectives and lax.ppermute only.
A program may use at most 64 MiB of HBM per device.

v0:
```python
import functools
import math

import jax
import jax.numpy as jnp
from jax import lax
from jax.experimental import pallas as pl
from jax.experimental.pallas import tpu as pltpu
from jax.sharding import PartitionSpec as P

TAP_DILATION = 2
VMEM_LIMIT = 32 * 1024 * 1024


def padded_2(block, sides, width):
    for axis, dim in sides:
        count = lax.axis_size(axis)
        forward = [(i, i + 1) for i in range(count - 1)]
        backward = [(target, source) for source, target in forward]
        low = lax.ppermute(
            lax.slice_in_dim(block, block.shape[dim] - width, None, axis=dim), axis, forward
        )
        high = lax.ppermute(lax.slice_in_dim(block, 0, width, axis=dim), axis, backward)
        block = jnp.concatenate([low, block, high], axis=dim)
    return block


def tile_columns(extended, tile_rows, width_cells, backward_pass):
    padded = jnp.pad(extended, ((0, 0), (0, 0), (1, 1), (0, 0)))
    pieces = []
    for row_shift in range(3):
        for col_shift in range(3):
            row_start = 2 - row_shift if backward_pass else row_shift
            col_start = 2 - col_shift if backward_pass else col_shift
            pieces.append(
                padded[:, row_start : row_start + tile_rows, col_start : col_start + width_cells, :]
            )
    channels = extended.shape[3]
    return jnp.concatenate(pieces, axis=-1).reshape(-1, 9 * channels)


def temporal_taps(padded_seq, weight, frame_count, backward_pass):
    pieces = []
    for temporal_tap_index in range(9):
        first_frame_index = (
            (8 - temporal_tap_index) * TAP_DILATION
            if backward_pass
            else temporal_tap_index * TAP_DILATION
        )
        pieces.append(padded_seq[first_frame_index : first_frame_index + frame_count])
    channels = padded_seq.shape[2]
    columns = jnp.concatenate(pieces, axis=-1).reshape(-1, 9 * channels)
    return jnp.dot(columns, weight, preferred_element_type=jnp.float32)


def per_device_any(clip_feats, out_grad, spatial_weight, temporal_weight):
    slab_frames, tile_rows, width_cells, channels = clip_feats.shape
    row_count = slab_frames * tile_rows * width_cells
    frame_devs = lax.axis_size("frame")
    tile_devs = lax.axis_size("tile")
    grad_scale = jnp.float32(
        1.0 / math.sqrt(slab_frames * frame_devs * tile_rows * tile_devs * width_cells)
    )
    spatial_back = (
        spatial_weight.reshape(9, channels, channels)
        .transpose(0, 2, 1)
        .reshape(9 * channels, channels)
    )
    temporal_back = (
        temporal_weight.reshape(9, channels, channels)
        .transpose(0, 2, 1)
        .reshape(9 * channels, channels)
    )
    feat_ext = padded_2(clip_feats, (("tile", 1),), 1)
    feat_columns = tile_columns(feat_ext, tile_rows, width_cells, False)
    pre = jnp.dot(feat_columns, spatial_weight, preferred_element_type=jnp.float32)
    act = jax.nn.silu(pre).astype(jnp.bfloat16)
    temporal_reach = 4 * TAP_DILATION
    per_group = tile_rows * width_cells // frame_devs
    grouped = (slab_frames, frame_devs, per_group, channels)
    act_part = lax.all_to_all(
        act.reshape(grouped), "frame", split_axis=1, concat_axis=0, tiled=True
    )
    grad_part = lax.all_to_all(out_grad, "frame", split_axis=1, concat_axis=0, tiled=True)
    feat_part = lax.all_to_all(clip_feats, "frame", split_axis=1, concat_axis=0, tiled=True)
    frame_count = act_part.shape[0]
    item_count = act_part.shape[2]
    act_pad = jnp.pad(
        act_part.reshape(frame_count, item_count, channels),
        ((temporal_reach, temporal_reach), (0, 0), (0, 0)),
    )
    grad_pad = jnp.pad(
        grad_part.reshape(frame_count, item_count, channels),
        ((temporal_reach, temporal_reach), (0, 0), (0, 0)),
    )
    mixed = temporal_taps(act_pad, temporal_weight, frame_count, False)
    out_part = (feat_part.reshape(-1, channels).astype(jnp.float32) + mixed).astype(jnp.bfloat16)
    back_part = temporal_taps(grad_pad, temporal_back, frame_count, True).astype(jnp.bfloat16)
    out_part = out_part.reshape(frame_count, 1, item_count, channels)
    back_part = back_part.reshape(frame_count, 1, item_count, channels)
    out_slab = lax.all_to_all(out_part, "frame", split_axis=0, concat_axis=1, tiled=True)
    grad_slab = lax.all_to_all(back_part, "frame", split_axis=0, concat_axis=1, tiled=True)
    act_grad = grad_slab.reshape(row_count, channels)
    sig = jax.nn.sigmoid(pre)
    pre_grad = (act_grad.astype(jnp.float32) * (sig * (1.0 + pre * (1.0 - sig)))).astype(
        jnp.bfloat16
    )
    full_term = lax.dot_general(
        feat_columns, pre_grad, (((0,), (0,)), ((), ())), preferred_element_type=jnp.float32
    )
    summed = lax.psum_scatter(full_term, ("frame", "tile"), scatter_dimension=0, tiled=True)
    weight_grad = summed * grad_scale
    grad_ext = padded_2(
        pre_grad.reshape(slab_frames, tile_rows, width_cells, channels), (("tile", 1),), 1
    )
    grad_columns = tile_columns(grad_ext, tile_rows, width_cells, True)
    local_back = jnp.dot(grad_columns, spatial_back, preferred_element_type=jnp.float32)
    input_grad = (out_grad.reshape(row_count, channels).astype(jnp.float32) + local_back).astype(
        jnp.bfloat16
    )
    input_grad = input_grad.reshape(slab_frames, tile_rows, width_cells, channels)
    return (out_slab, input_grad, weight_grad)


def kernel_call(body, outs, scratch, flops, *args, anywhere=0):
    moved = sum(a.size * a.dtype.itemsize for a in args)
    moved += sum(math.prod(shape) * jnp.dtype(kind).itemsize for shape, kind in outs)
    spaces = [pltpu.VMEM] * (len(args) - anywhere) + [pl.ANY] * anywhere
    return pl.pallas_call(
        body,
        out_shape=tuple(jax.ShapeDtypeStruct(shape, kind) for shape, kind in outs),
        in_specs=[pl.BlockSpec(memory_space=space) for space in spaces],
        out_specs=tuple(pl.BlockSpec(memory_space=pltpu.VMEM) for _ in outs),
        scratch_shapes=[pltpu.VMEM(shape, kind) for shape, kind in scratch],
        compiler_params=pltpu.CompilerParams(vmem_limit_bytes=VMEM_LIMIT),
        cost_estimate=pl.CostEstimate(flops=flops, bytes_accessed=moved, transcendentals=0),
    )(*args)


def shifted(values, width, step):
    rows = values.shape[0]
    at = lax.broadcasted_iota(jnp.int32, values.shape, 0) % width
    moved = pltpu.roll(values, step % rows, 0)
    inside = at >= step if step > 0 else at < width + step
    return jnp.where(inside, moved, 0.0)


def column_shifts(values, width):
    wide = values.astype(jnp.float32)
    return (
        shifted(wide, width, 1).astype(values.dtype),
        values,
        shifted(wide, width, -1).astype(values.dtype),
    )


def with_edges(own, other, ext):
    rows = own.shape[1]
    tile = lax.axis_index("tile")
    ext[:, 1 : rows + 1] = own[...]
    above, below = other[:, rows - 1], other[:, 0]
    ext[:, 0] = jnp.where(tile == 1, above, jnp.zeros_like(above))
    ext[:, rows + 1] = jnp.where(tile == 0, below, jnp.zeros_like(below))


def whole_image(own, other, image):
    rows = own.shape[1]
    tile = lax.axis_index("tile")
    image[:, 0] = jnp.zeros_like(image[:, 0])
    image[:, 2 * rows + 1] = jnp.zeros_like(image[:, 2 * rows + 1])
    image[:, pl.ds(1 + tile * rows, rows)] = own[...]
    image[:, pl.ds(1 + (1 - tile) * rows, rows)] = other[...]


def order_kernel(*refs):
    refs[-1][...] = jnp.zeros_like(refs[-1])


def spatial_kernel(own, weight, other, _, pre_ref, act_ref, image, pre_all):
    frames, rows, width, channels = own.shape
    whole_image(own, other, image)
    shifts = column_shifts(image[...].reshape(-1, channels), width)
    shifts = [piece.reshape(image.shape) for piece in shifts]
    for half in range(2):
        columns = jnp.concatenate(
            [
                shifts[s][:, half * rows + r : half * rows + r + rows].reshape(-1, channels)
                for r in range(3)
                for s in range(3)
            ],
            axis=1,
        )
        pre = jnp.dot(columns, weight[...], preferred_element_type=jnp.float32)
        pre_all[half] = pre
        act_ref[half] = (pre * jax.nn.sigmoid(pre)).astype(jnp.bfloat16)
    pre_ref[...] = pre_all[lax.axis_index("tile")]


def split_kernel(arrived, _, mine_ref, other_ref):
    tile = lax.axis_index("tile")
    mine_ref[...] = arrived[tile]
    other_ref[...] = arrived[1 - tile]


def forward_sum_kernel(partial, arrived, *rest, first):
    sum_ref = rest[-1]
    rows = partial[first : first + sum_ref.shape[0]]
    came = arrived[: sum_ref.shape[0]].astype(jnp.float32)
    sum_ref[...] = (rows + came).astype(sum_ref.dtype)


def last_sum_kernel(keep, near, last_a, last_b, _, out_ref, *, scale):
    half = last_a.shape[0]
    for first, last in ((0, last_a), (half, last_b)):
        total = keep[first : first + half] + near[first : first + half].astype(jnp.float32)
        out_ref[first : first + half] = (total + last[...].astype(jnp.float32)) * scale


def transpose_kernel(own, other, _, out_ref, image):
    frames, rows, width, channels = own.shape
    tile = lax.axis_index("tile")
    whole_image(own, other, image)
    for which, first in enumerate((tile * rows, (1 - tile) * rows)):
        for r in range(3):
            block = image[:, pl.ds(first + r, rows)].reshape(-1, channels)
            out_ref[which, r * channels : (r + 1) * channels] = block.T


def slabs(own, first, second, ext):
    tile = lax.axis_index("tile")
    ext[2 * tile] = first[...]
    ext[1] = own[...]
    ext[2 - 2 * tile] = second[...]
    chip = lax.axis_index("frame")

    @pl.when(chip == 0)
    def _():
        ext[0] = jnp.zeros_like(ext[0])

    @pl.when(chip == lax.axis_size("frame") - 1)
    def _():
        ext[2] = jnp.zeros_like(ext[2])

    return ext[...].reshape(-1, own.shape[1])


def act_grad_kernel(own, first_in, second_in, weight, pre_ref, _, out_ref, ext):
    count, channels = own.shape
    frames = slabs(own, first_in, second_in, ext)
    hop = count // 4
    total = None
    for k in range(9):
        first = (8 - k) * hop
        term = lax.dot_general(
            frames[first : first + count],
            weight[k * channels : (k + 1) * channels],
            (((1,), (1,)), ((), ())),
            preferred_element_type=jnp.float32,
        )
        total = term if total is None else total + term
    act_grad = total.astype(jnp.bfloat16).astype(jnp.float32)
    pre = pre_ref[...]
    sig = jax.nn.sigmoid(pre)
    out_ref[...] = (act_grad * (sig * (1.0 + pre * (1.0 - sig)))).astype(jnp.bfloat16)


def temporal_kernel(feats, act, first_in, second_in, weight, _, out_ref, done_ref, ext):
    count, channels = feats.shape
    own = act.at[lax.axis_index("tile")]
    frames = slabs(own, first_in, second_in, ext)
    hop = count // 4
    columns = jnp.concatenate([frames[k * hop : k * hop + count] for k in range(9)], axis=1)
    mixed = jnp.dot(columns, weight[...], preferred_element_type=jnp.float32)
    out_ref[...] = (feats[...].astype(jnp.float32) + mixed).astype(jnp.bfloat16)
    done_ref[...] = jnp.zeros_like(done_ref)


def own_term_kernel(feats_t, own, total_ref):
    channels = own.shape[3]
    after, same, before = column_shifts(own[...].reshape(-1, channels), own.shape[2])
    left = feats_t[0]
    for s, right in enumerate((before, same, after)):
        total_ref[s] = jnp.dot(left, right, preferred_element_type=jnp.float32)


def kernel_grad_kernel(
    feats_t, other, term, far_a_ref, far_b_ref, pass_ref, near_ref, keep_ref, total
):
    frames, rows, width, channels = other.shape
    tile = lax.axis_index("tile")
    chip = lax.axis_index("frame")
    after, same, before = column_shifts(other[...].reshape(-1, channels), width)
    left = feats_t[1]
    for s, right in enumerate((before, same, after)):
        both = term[s] + jnp.dot(left, right, preferred_element_type=jnp.float32)
        for r in range(3):
            tap = 3 * r + s
            total[tap * channels : (tap + 1) * channels] = both[r * channels : (r + 1) * channels]
    share = keep_ref.shape[0]
    half = share // 2
    for distance, skip, ref in (
        (3, 0, far_a_ref),
        (3, half, far_b_ref),
        (2, 0, pass_ref),
        (1, 0, near_ref),
        (0, 0, keep_ref),
    ):
        first = (2 * (chip ^ distance) + tile) * share + skip
        ref[...] = total[pl.ds(pl.multiple_of(first, 16), ref.shape[0])].astype(ref.dtype)


def input_grad_kernel(out_grad, own, other, weight, _, out_ref, done_ref, ext):
    frames, rows, width, channels = own.shape
    with_edges(own, other, ext)
    after, same, before = column_shifts(ext[...].reshape(-1, channels), width)
    shifts = [piece.reshape(ext.shape) for piece in (before, same, after)]
    total = out_grad[...].astype(jnp.float32)
    for r in range(3):
        for s in range(3):
            tap = 3 * r + s
            total = total + lax.dot_general(
                shifts[s][:, 2 - r : 2 - r + rows].reshape(-1, channels),
                weight[tap * channels : (tap + 1) * channels],
                (((1,), (1,)), ((), ())),
                preferred_element_type=jnp.float32,
            )
    out_ref[...] = total.astype(jnp.bfloat16)
    done_ref[...] = jnp.zeros_like(done_ref)


def per_device_pair(clip_feats, out_grad, spatial_weight, temporal_weight):
    frames, rows, width, channels = clip_feats.shape
    count = frames * rows * width
    chips = lax.axis_size("frame")
    cores = lax.axis_size("tile")
    scale = 1.0 / math.sqrt(frames * chips * rows * cores * width)
    outward = [(2 * z, 2 * z + 2) for z in range(chips - 1)]
    outward += [(2 * z + 3, 2 * z + 1) for z in range(chips - 1)]
    outward += [(2 * chips - 2, 2 * chips - 1), (1, 0)]
    inward = [(target, source) for source, target in outward]
    both = ("frame", "tile")
    swap = [(0, 1), (1, 0)]
    bf16, f32 = jnp.bfloat16, jnp.float32
    product = 2 * count * 9 * channels * channels
    flat = (count, channels)
    ext = ((frames, rows + 2, width, channels), bf16)
    image = ((frames, 2 * rows + 2, width, channels), bf16)
    three = ((3, count, channels), bf16)

    grad_flat = out_grad.reshape(flat)
    feat_flat = clip_feats.reshape(flat)
    grad_first = lax.ppermute(grad_flat, both, outward)
    grad_second = lax.ppermute(grad_flat, both, inward)
    feat_other = lax.ppermute(clip_feats, "tile", swap)

    (first,) = kernel_call(order_kernel, [((8, 128), f32)], [], 2 * product)
    pre, act = kernel_call(
        spatial_kernel,
        [(flat, f32), ((2, *flat), bf16)],
        [image, ((2, *flat), f32)],
        2 * product,
        clip_feats, spatial_weight, feat_other, first, anywhere=1,
    )
    act_in = lax.ppermute(act, both, inward)
    (feats_t,) = kernel_call(
        transpose_kernel,
        [((2, 3 * channels, count), bf16)],
        [image],
        0,
        clip_feats, feat_other, pre, anywhere=1,
    )
    (pre_grad,) = kernel_call(
        act_grad_kernel,
        [(flat, bf16)],
        [three],
        product,
        grad_flat, grad_first, grad_second, temporal_weight, pre, feats_t, anywhere=1,
    )
    pre_grad = pre_grad.reshape(clip_feats.shape)
    pre_other = lax.ppermute(pre_grad, "tile", swap)

    share = (9 * channels // (chips * cores), channels)
    (term,) = kernel_call(
        own_term_kernel,
        [((3, 3 * channels, channels), f32)],
        [],
        product,
        feats_t, pre_grad,
    )
    half = (share[0] // 2, channels)
    far_a, far_b, onward, near, keep = kernel_call(
        kernel_grad_kernel,
        [(half, bf16), (half, bf16), (share, f32), (share, bf16), (share, f32)],
        [((9 * channels, channels), f32)],
        product,
        feats_t, pre_other, term,
    )
    beside = [(z, z ^ 1) for z in range(chips)]
    across = [(z, z ^ 2) for z in range(chips)]
    far_in_a = lax.ppermute(far_a, "frame", beside)
    far_in_b = lax.ppermute(far_b, "frame", beside)
    near_in = lax.ppermute(near, "frame", beside)
    (sum_a,) = kernel_call(
        functools.partial(forward_sum_kernel, first=0),
        [(half, bf16)],
        [],
        4 * product,
        onward, far_in_a, act_in, anywhere=1,
    )
    last_a = lax.ppermute(sum_a, "frame", across)
    (sum_b,) = kernel_call(
        functools.partial(forward_sum_kernel, first=half[0]),
        [(half, bf16)],
        [],
        0,
        onward, far_in_b, sum_a, anywhere=1,
    )
    last_b = lax.ppermute(sum_b, "frame", across)
    act_second, act_pass = kernel_call(
        split_kernel, [(flat, bf16)] * 2, [], 0, act_in, sum_b, anywhere=1
    )
    act_first = lax.ppermute(act_pass, "tile", swap)

    input_grad, done = kernel_call(
        input_grad_kernel,
        [(flat, bf16), ((8, 128), f32)],
        [ext],
        product,
        grad_flat, pre_grad, pre_other, spatial_weight, sum_b, anywhere=1,
    )
    (arrived,) = kernel_call(
        order_kernel, [((8, 128), f32)], [], 20 * product, last_a, near_in, done, anywhere=3
    )
    block_out, done = kernel_call(
        temporal_kernel,
        [(flat, bf16), ((8, 128), f32)],
        [three],
        product,
        feat_flat, act, act_first, act_second, temporal_weight, arrived, anywhere=1,
    )
    (weight_grad,) = kernel_call(
        functools.partial(last_sum_kernel, scale=scale),
        [(share, f32)],
        [],
        0,
        keep, near_in, last_a, last_b, done, anywhere=1,
    )
    return (
        block_out.reshape(clip_feats.shape),
        input_grad.reshape(clip_feats.shape),
        weight_grad,
    )


def per_device(clip_feats, *rest):
    pairs = lax.axis_size("tile") == 2 and lax.axis_size("frame") == 4
    if pairs and clip_feats.shape[0] == 4 * TAP_DILATION:
        return per_device_pair(clip_feats, *rest)
    return per_device_any(clip_feats, *rest)


def solution(mesh):
    return jax.shard_map(
        per_device,
        mesh=mesh,
        in_specs=(
            P(("clip", "frame"), "tile", None, None),
            P(("clip", "frame"), "tile", None, None),
            P(),
            P(),
        ),
        out_specs=(
            P(("clip", "frame"), "tile", None, None),
            P(("clip", "frame"), "tile", None, None),
            P(("clip", "frame", "tile"), None),
        ),
        check_vma=False,
    )
```

profile of v0, /device:TPU:0, one launch (start us, length us, event | category | flops | bytes accessed | tf_op | source)
XLA Modules:
  0.0 30.9 jit_solution(3052587908984970341)
XLA Ops:
  0.6 0.5 %collective-permute-start = (bf16[8,4,16,256]{3,2,1,0:T(8,128)(2,1)}, bf16[8,4,16,256]{3,2,1,0:T(8,128)(2,1)S(1)}, u32[]{:S(2)}, u32[]{:S(2)}) collective-permute-start(bf16[8,4,16,256]{3,2,1,0:T(8,128)(2,1)} %own.3), channel_id=1, source_target_pairs={{0,1},{1,0},{2,3},{3,2},{4,5},{5,4},{6,7},{7,6},{8,9},{9,8},{10,11... | collective-permute-start | bytes 786440 | tf_op jit(solution)/shard_map/ppermute | solution.py:354
  1.1 0.0 copy-start.1
  1.1 0.0 copy-start.3
  1.2 2.6 %collective-permute-start.2 = (bf16[512,256]{1,0:T(8,128)(2,1)}, bf16[512,256]{1,0:T(8,128)(2,1)S(1)}, u32[]{:S(2)}, u32[]{:S(2)}) collective-permute-start(bf16[512,256]{1,0:T(8,128)(2,1)} %bitcast.9), channel_id=1, source_target_pairs={{0,2},{2,4},{4,6},{3,1},{5,3},{7,5},{6,7},{1,0},{8,10},{10,12},{12... | collective-permute-start | bytes 786440 | tf_op jit(solution)/shard_map/ppermute | solution.py:352
  3.8 0.0 collective-permute-start.3
  3.8 0.0 collective-permute-done.other
  3.8 0.0 copy-done.1
  3.8 0.0 copy-done.3
  3.8 1.7 %shard_map.68 = (f32[512,256]{1,0:T(8,128)S(1)}, bf16[2,512,256]{2,1,0:T(8,128)(2,1)S(1)}) custom-call(bf16[8,4,16,256]{3,2,1,0:T(8,128)(2,1)S(1)} %copy-done.1, bf16[2304,256]{1,0:T(8,128)(2,1)S(1)} %copy-done.3, bf16[8,4,16,256]{3,2,1,0:T(8,128)(2,1)S(1)} %collective-permute-done.other, f32[8,128]{1,0:T(8,128)S(1)} %shard_map.67._), custom_call_target="tpu_custom_call" | custom-call | flops 1207959552 | bytes 2756608 | tf_op jit(solution)/shard_map/pallas_call | solution.py:129
  5.5 0.0 copy-start
  5.5 0.0 copy-start.2
  5.6 0.2 collective-permute-start.1
  5.8 0.5 %shard_map.69._.feats_t = bf16[2,768,512]{2,1,0:T(8,128)(2,1)S(1)} custom-call(bf16[8,4,16,256]{3,2,1,0:T(8,128)(2,1)S(1)} %copy-done.1, bf16[8,4,16,256]{3,2,1,0:T(8,128)(2,1)S(1)} %collective-permute-done.other, f32[512,256]{1,0:T(8,128)S(1)} %get-tuple-element.17._.pre_ref), custom_call_target="tpu_custom_call" | custom-call | bytes 2621440 | tf_op jit(solution)/shard_map/pallas_call | solution.py:129
  6.3 4.4 %collective-permute-done.2.first_in = bf16[512,256]{1,0:T(8,128)(2,1)S(1)} collective-permute-done((bf16[512,256]{1,0:T(8,128)(2,1)}, bf16[512,256]{1,0:T(8,128)(2,1)S(1)}, u32[]{:S(2)}, u32[]{:S(2)}) %collective-permute-start.2) | collective-permute-done | bytes 262176 | tf_op jit(solution)/shard_map/ppermute | solution.py:352
  10.7 0.2 collective-permute-done.3.second_in
  10.9 0.0 copy-done
  10.9 0.0 copy-done.2
  10.9 0.9 %shard_map.70 = bf16[512,256]{1,0:T(8,128)(2,1)S(1)} custom-call(bf16[512,256]{1,0:T(8,128)(2,1)S(1)} %bitcast.11, bf16[512,256]{1,0:T(8,128)(2,1)S(1)} %collective-permute-done.2.first_in, bf16[512,256]{1,0:T(8,128)(2,1)S(1)} %collective-permute-done.3.second_in, bf16[2304,256]{1,0:T(8,128)(2,1)S(1)} %copy-done, ...), custom_call_target="tpu_custom_call" | custom-call | flops 603979776 | bytes 4325376 | tf_op jit(solution)/shard_map/pallas_call | solution.py:129
  11.8 0.1 collective-permute-start.4
  11.9 0.8 %shard_map.71.term = f32[3,768,256]{2,1,0:T(8,128)S(1)} custom-call(bf16[2,768,512]{2,1,0:T(8,128)(2,1)S(1)} %shard_map.69._.feats_t, bf16[8,4,16,256]{3,2,1,0:T(8,128)(2,1)S(1)} %bitcast.7), custom_call_target="tpu_custom_call" | custom-call | flops 603979776 | bytes 4194304 | tf_op jit(solution)/shard_map/pallas_call | solution.py:129
  12.7 0.7 %collective-permute-done.4.other = bf16[8,4,16,256]{3,2,1,0:T(8,128)(2,1)S(1)} collective-permute-done((bf16[8,4,16,256]{3,2,1,0:T(8,128)(2,1)S(1)}, bf16[8,4,16,256]{3,2,1,0:T(8,128)(2,1)S(1)}, u32[]{:S(2)}, u32[]{:S(2)}) %collective-permute-start.4) | collective-permute-done | bytes 262176 | tf_op jit(solution)/shard_map/ppermute | solution.py:380
  13.4 0.9 %shard_map.72 = (bf16[144,256]{1,0:T(8,128)(2,1)S(1)}, bf16[144,256]{1,0:T(8,128)(2,1)S(1)}, f32[288,256]{1,0:T(8,128)S(1)}, bf16[288,256]{1,0:T(8,128)(2,1)S(1)}, f32[288,256]{1,0:T(8,128)S(1)}) custom-call(bf16[2,768,512]{2,1,0:T(8,128)(2,1)S(1)} %shard_map.69._.feats_t, bf16[8,4,16,256]{3,2,1,0:T(8,128)(2,1)S(1)} %collective-permute-done.4.other, ...), custom_call_target="tpu_custom_call" | custom-call | flops 603979776 | bytes 5079040 | tf_op jit(solution)/shard_map/pallas_call | solution.py:129
  14.3 2.2 %collective-permute-start.6 = (bf16[144,256]{1,0:T(8,128)(2,1)S(1)}, bf16[144,256]{1,0:T(8,128)(2,1)S(1)}, u32[]{:S(2)}, u32[]{:S(2)}) collective-permute-start(bf16[144,256]{1,0:T(8,128)(2,1)S(1)} %get-tuple-element.20), channel_id=1, source_target_pairs={{0,2},{2,0},{4,6},{6,4},{1,3},{3,1},{5,7},{7,5},{8,10},{10,8},{12,... | collective-permute-start | bytes 221192 | tf_op jit(solution)/shard_map/ppermute | solution.py:400
  16.5 0.1 collective-permute-start.5
  16.6 1.9 %collective-permute-start.9 = (bf16[288,256]{1,0:T(8,128)(2,1)S(1)}, bf16[288,256]{1,0:T(8,128)(2,1)S(1)}, u32[]{:S(2)}, u32[]{:S(2)}) collective-permute-start(bf16[288,256]{1,0:T(8,128)(2,1)S(1)} %get-tuple-element.23), channel_id=1, source_target_pairs={{0,2},{2,0},{4,6},{6,4},{1,3},{3,1},{5,7},{7,5},{8,10},{10,8},{12,... | collective-permute-start | bytes 442376 | tf_op jit(solution)/shard_map/ppermute | solution.py:402
  18.6 0.7 %collective-permute-done.6.arrived = bf16[144,256]{1,0:T(8,128)(2,1)S(1)} collective-permute-done((bf16[144,256]{1,0:T(8,128)(2,1)S(1)}, bf16[144,256]{1,0:T(8,128)(2,1)S(1)}, u32[]{:S(2)}, u32[]{:S(2)}) %collective-permute-start.6) | collective-permute-done | bytes 73760 | tf_op jit(solution)/shard_map/ppermute | solution.py:400
  19.2 0.0 collective-permute-done.1.rest_0_.arrived
  19.3 3.2 %collective-permute-start.8 = (bf16[144,256]{1,0:T(8,128)(2,1)S(1)}, bf16[144,256]{1,0:T(8,128)(2,1)S(1)}, u32[]{:S(2)}, u32[]{:S(2)}) collective-permute-start(bf16[144,256]{1,0:T(8,128)(2,1)S(1)} %shard_map.73.rest_0_), channel_id=1, source_target_pairs={{0,4},{2,6},{4,0},{6,2},{1,5},{3,7},{5,1},{7,3},{8,12},{10,14},{12... | collective-permute-start | bytes 221192 | tf_op jit(solution)/shard_map/ppermute | solution.py:410
  22.5 0.0 collective-permute-done.5.arrived
  22.5 2.0 %collective-permute-start.10 = (bf16[144,256]{1,0:T(8,128)(2,1)S(1)}, bf16[144,256]{1,0:T(8,128)(2,1)S(1)}, u32[]{:S(2)}, u32[]{:S(2)}) collective-permute-start(bf16[144,256]{1,0:T(8,128)(2,1)S(1)} %shard_map.74._), channel_id=1, source_target_pairs={{0,4},{2,6},{4,0},{6,2},{1,5},{3,7},{5,1},{7,3},{8,12},{10,14},{12... | collective-permute-start | bytes 221192 | tf_op jit(solution)/shard_map/ppermute | solution.py:418
  24.5 0.1 collective-permute-start.7
  24.6 1.5 %shard_map.76 = (bf16[512,256]{1,0:T(8,128)(2,1)}, f32[8,128]{1,0:T(8,128)S(1)}) custom-call(bf16[512,256]{1,0:T(8,128)(2,1)S(1)} %bitcast.12, bf16[8,4,16,256]{3,2,1,0:T(8,128)(2,1)S(1)} %bitcast.8, bf16[8,4,16,256]{3,2,1,0:T(8,128)(2,1)S(1)} %collective-permute-done.4.other, bf16[2304,256]{1,0:T(8,128)(2,1)S(1)} %copy-done.3, bf16[144,256]{1,0:T(8,128)(2,1)S(1)} %shard_map.74._), custom_call_target="tpu_custom_call" | custom-call | flops 603979776 | bytes 2306048 | tf_op jit(solution)/shard_map/pallas_call | solution.py:129
  26.1 0.1 collective-permute-done.9.refs_1_.near
  26.2 0.0 collective-permute-done.8.refs_0_.last_a
  26.2 0.0 collective-permute-done.7.first_in
  26.2 1.6 %shard_map.78 = (bf16[512,256]{1,0:T(8,128)(2,1)}, f32[8,128]{1,0:T(8,128)S(1)}) custom-call(bf16[512,256]{1,0:T(8,128)(2,1)S(1)} %bitcast.5, bf16[2,512,256]{2,1,0:T(8,128)(2,1)S(1)} %get-tuple-element.16.act, bf16[512,256]{1,0:T(8,128)(2,1)S(1)} %collective-permute-done.7.first_in, bf16[512,256]{1,0:T(8,128)(2,1)S(1)} %get-tuple-element.22.second_in, ...), custom_call_target="tpu_custom_call" | custom-call | flops 603979776 | bytes 2760704 | tf_op jit(solution)/shard_map/pallas_call | solution.py:129
  27.8 2.3 %collective-permute-done.10.last_b = bf16[144,256]{1,0:T(8,128)(2,1)S(1)} collective-permute-done((bf16[144,256]{1,0:T(8,128)(2,1)S(1)}, bf16[144,256]{1,0:T(8,128)(2,1)S(1)}, u32[]{:S(2)}, u32[]{:S(2)}) %collective-permute-start.10) | collective-permute-done | bytes 73760 | tf_op jit(solution)/shard_map/ppermute | solution.py:418
  30.1 0.8 %shard_map.79 = f32[288,256]{1,0:T(8,128)} custom-call(f32[288,256]{1,0:T(8,128)S(1)} %get-tuple-element.27.keep, bf16[288,256]{1,0:T(8,128)(2,1)S(1)} %collective-permute-done.9.refs_1_.near, bf16[144,256]{1,0:T(8,128)(2,1)S(1)} %collective-permute-done.8.refs_0_.last_a, bf16[144,256]{1,0:T(8,128)(2,1)S(1)} %collective-permute-done.10.last_b, ...), custom_call_target="tpu_custom_call" | custom-call | bytes 888832 | tf_op jit(solution)/shard_map/pallas_call | solution.py:129
  (5 shorter events, 0.1 us)
Async XLA Ops:
  0.6 3.1 %collective-permute-start = (bf16[8,4,16,256]{3,2,1,0:T(8,128)(2,1)}, bf16[8,4,16,256]{3,2,1,0:T(8,128)(2,1)S(1)}, u32[]{:S(2)}, u32[]{:S(2)}) collective-permute-start(bf16[8,4,16,256]{3,2,1,0:T(8,128)(2,1)} %own.3), channel_id=1, source_target_pairs={{0,1},{1,0},{2,3},{3,2},{4,5},{5,4},{6,7},{7,6},{8,9},{9,8},{10,11... | collective-permute-start | bytes 786440 | tf_op jit(solution)/shard_map/ppermute | solution.py:354
  1.1 2.6 %copy-start.1 = (bf16[8,4,16,256]{3,2,1,0:T(8,128)(2,1)S(1)}, bf16[8,4,16,256]{3,2,1,0:T(8,128)(2,1)}, u32[]{:S(2)}) copy-start(bf16[8,4,16,256]{3,2,1,0:T(8,128)(2,1)} %own.3) | copy-start | bytes 786436
  1.1 2.6 %copy-start.3 = (bf16[2304,256]{1,0:T(8,128)(2,1)S(1)}, bf16[2304,256]{1,0:T(8,128)(2,1)}, u32[]{:S(2)}) copy-start(bf16[2304,256]{1,0:T(8,128)(2,1)} %weight.6) | copy-start | bytes 3538948
  1.2 9.6 %collective-permute-start.2 = (bf16[512,256]{1,0:T(8,128)(2,1)}, bf16[512,256]{1,0:T(8,128)(2,1)S(1)}, u32[]{:S(2)}, u32[]{:S(2)}) collective-permute-start(bf16[512,256]{1,0:T(8,128)(2,1)} %bitcast.9), channel_id=1, source_target_pairs={{0,2},{2,4},{4,6},{3,1},{5,3},{7,5},{6,7},{1,0},{8,10},{10,12},{12... | collective-permute-start | bytes 786440 | tf_op jit(solution)/shard_map/ppermute | solution.py:352
  3.8 7.1 %collective-permute-start.3 = (bf16[512,256]{1,0:T(8,128)(2,1)}, bf16[512,256]{1,0:T(8,128)(2,1)S(1)}, u32[]{:S(2)}, u32[]{:S(2)}) collective-permute-start(bf16[512,256]{1,0:T(8,128)(2,1)} %bitcast.10), channel_id=1, source_target_pairs={{2,0},{4,2},{6,4},{1,3},{3,5},{5,7},{7,6},{0,1},{10,8},{12,10},{14... | collective-permute-start | bytes 786440 | tf_op jit(solution)/shard_map/ppermute | solution.py:353
  5.5 5.4 %copy-start = (bf16[2304,256]{1,0:T(8,128)(2,1)S(1)}, bf16[2304,256]{1,0:T(8,128)(2,1)}, u32[]{:S(2)}) copy-start(bf16[2304,256]{1,0:T(8,128)(2,1)} %weight.7) | copy-start | bytes 3538948
  5.5 5.4 %copy-start.2 = (bf16[8,4,16,256]{3,2,1,0:T(8,128)(2,1)S(1)}, bf16[8,4,16,256]{3,2,1,0:T(8,128)(2,1)}, u32[]{:S(2)}) copy-start(bf16[8,4,16,256]{3,2,1,0:T(8,128)(2,1)} %param.5) | copy-start | bytes 786436
  5.6 13.7 %collective-permute-start.1 = (bf16[2,512,256]{2,1,0:T(8,128)(2,1)S(1)}, bf16[2,512,256]{2,1,0:T(8,128)(2,1)S(1)}, u32[]{:S(2)}, u32[]{:S(2)}) collective-permute-start(bf16[2,512,256]{2,1,0:T(8,128)(2,1)S(1)} %get-tuple-element.16.act), channel_id=1, source_target_pairs={{2,0},{4,2},{6,4},{1,3},{3,5},{5,7},{7,6},{0,1},{10,8},{12,10},{14... | collective-permute-start | bytes 1572872 | tf_op jit(solution)/shard_map/ppermute | solution.py:364
  11.8 1.6 %collective-permute-start.4 = (bf16[8,4,16,256]{3,2,1,0:T(8,128)(2,1)S(1)}, bf16[8,4,16,256]{3,2,1,0:T(8,128)(2,1)S(1)}, u32[]{:S(2)}, u32[]{:S(2)}) collective-permute-start(bf16[8,4,16,256]{3,2,1,0:T(8,128)(2,1)S(1)} %bitcast.6), channel_id=1, source_target_pairs={{0,1},{1,0},{2,3},{3,2},{4,5},{5,4},{6,7},{7,6},{8,9},{9,8},{10,11... | collective-permute-start | bytes 786440 | tf_op jit(solution)/shard_map/ppermute | solution.py:380
  14.3 4.9 %collective-permute-start.6 = (bf16[144,256]{1,0:T(8,128)(2,1)S(1)}, bf16[144,256]{1,0:T(8,128)(2,1)S(1)}, u32[]{:S(2)}, u32[]{:S(2)}) collective-permute-start(bf16[144,256]{1,0:T(8,128)(2,1)S(1)} %get-tuple-element.20), channel_id=1, source_target_pairs={{0,2},{2,0},{4,6},{6,4},{1,3},{3,1},{5,7},{7,5},{8,10},{10,8},{12,... | collective-permute-start | bytes 221192 | tf_op jit(solution)/shard_map/ppermute | solution.py:400
  16.5 5.9 %collective-permute-start.5 = (bf16[144,256]{1,0:T(8,128)(2,1)S(1)}, bf16[144,256]{1,0:T(8,128)(2,1)S(1)}, u32[]{:S(2)}, u32[]{:S(2)}) collective-permute-start(bf16[144,256]{1,0:T(8,128)(2,1)S(1)} %get-tuple-element.19), channel_id=1, source_target_pairs={{0,2},{2,0},{4,6},{6,4},{1,3},{3,1},{5,7},{7,5},{8,10},{10,8},{12,... | collective-permute-start | bytes 221192 | tf_op jit(solution)/shard_map/ppermute | solution.py:401
  16.6 9.6 %collective-permute-start.9 = (bf16[288,256]{1,0:T(8,128)(2,1)S(1)}, bf16[288,256]{1,0:T(8,128)(2,1)S(1)}, u32[]{:S(2)}, u32[]{:S(2)}) collective-permute-start(bf16[288,256]{1,0:T(8,128)(2,1)S(1)} %get-tuple-element.23), channel_id=1, source_target_pairs={{0,2},{2,0},{4,6},{6,4},{1,3},{3,1},{5,7},{7,5},{8,10},{10,8},{12,... | collective-permute-start | bytes 442376 | tf_op jit(solution)/shard_map/ppermute | solution.py:402
  19.3 7.0 %collective-permute-start.8 = (bf16[144,256]{1,0:T(8,128)(2,1)S(1)}, bf16[144,256]{1,0:T(8,128)(2,1)S(1)}, u32[]{:S(2)}, u32[]{:S(2)}) collective-permute-start(bf16[144,256]{1,0:T(8,128)(2,1)S(1)} %shard_map.73.rest_0_), channel_id=1, source_target_pairs={{0,4},{2,6},{4,0},{6,2},{1,5},{3,7},{5,1},{7,3},{8,12},{10,14},{12... | collective-permute-start | bytes 221192 | tf_op jit(solution)/shard_map/ppermute | solution.py:410
  22.5 7.6 %collective-permute-start.10 = (bf16[144,256]{1,0:T(8,128)(2,1)S(1)}, bf16[144,256]{1,0:T(8,128)(2,1)S(1)}, u32[]{:S(2)}, u32[]{:S(2)}) collective-permute-start(bf16[144,256]{1,0:T(8,128)(2,1)S(1)} %shard_map.74._), channel_id=1, source_target_pairs={{0,4},{2,6},{4,0},{6,2},{1,5},{3,7},{5,1},{7,3},{8,12},{10,14},{12... | collective-permute-start | bytes 221192 | tf_op jit(solution)/shard_map/ppermute | solution.py:418
  24.5 1.7 %collective-permute-start.7 = (bf16[512,256]{1,0:T(8,128)(2,1)S(1)}, bf16[512,256]{1,0:T(8,128)(2,1)S(1)}, u32[]{:S(2)}, u32[]{:S(2)}) collective-permute-start(bf16[512,256]{1,0:T(8,128)(2,1)S(1)} %get-tuple-element.21), channel_id=1, source_target_pairs={{0,1},{1,0},{2,3},{3,2},{4,5},{5,4},{6,7},{7,6},{8,9},{9,8},{10,11... | collective-permute-start | bytes 786440 | tf_op jit(solution)/shard_map/ppermute | solution.py:422
where the time goes:
time: 31 us; the launch traced here: 30.9 us
  starting transfers between devices  12.9 us (42%)
  Pallas kernels  8.79 us (28%)
  waiting for transfers between devices  8.44 us (27%)
  between operations  0.74 us (2%)
    pallas_call x13, Pallas kernels, kernel_call(): pl.pallas_call(body, out_shape=tuple((jax.ShapeDtypeStruct(shape, kind) f...  8.79 us
    ppermute x1, waiting for transfers between devices, per_device_pair(): grad_first = lax.ppermute(grad_flat, both, outward)  4.44 us
    ppermute x1, starting transfers between devices, per_device_pair(): last_a = lax.ppermute(sum_a, 'frame', across)  3.2 us
    ppermute x1, starting transfers between devices, per_device_pair(): grad_first = lax.ppermute(grad_flat, both, outward)  2.62 us
    ppermute x1, waiting for transfers between devices, per_device_pair(): last_b = lax.ppermute(sum_b, 'frame', across)  2.31 us
    ppermute x1, starting transfers between devices, per_device_pair(): far_in_a = lax.ppermute(far_a, 'frame', beside)  2.24 us
    ppermute x1, starting transfers between devices, per_device_pair(): last_b = lax.ppermute(sum_b, 'frame', across)  1.97 us
    ppermute x1, starting transfers between devices, per_device_pair(): near_in = lax.ppermute(near, 'frame', beside)  1.95 us
  transfers between devices with their start and end apart: 11, of which 6 were waited for; matrix products, arithmetic and copies ran while one was open for 0% of the time, Pallas kernels for 26%

commit v1 on v0

--- a/solution.py
+++ b/solution.py
@@ -353,7 +353,7 @@
     grad_second = lax.ppermute(grad_flat, both, inward)
     feat_other = lax.ppermute(clip_feats, "tile", swap)
 
-    (first,) = kernel_call(order_kernel, [((8, 128), f32)], [], 2 * product)
+    (first,) = kernel_call(order_kernel, [((8, 128), f32)], [], 5 * product)
     pre, act = kernel_call(
         spatial_kernel,
         [(flat, f32), ((2, *flat), bf16)],

time: 31 us -> 30.1 us (0.971)
  waiting for transfers between devices: 8.44 us -> 7.91 us
  starting transfers between devices: 12.9 us -> 12.5 us
    ppermute x1, waiting for transfers between devices: 4.44 us -> 1.48 us  [per_device_pair(): grad_first = lax.ppermute(grad_flat, both, outward)]
    ppermute x1, waiting for transfers between devices: 0.01 us -> 1.74 us  [per_device_pair(): feat_other = lax.ppermute(clip_feats, 'tile', swap)]
    ppermute x1, starting transfers between devices: 0.52 us -> 0.01 us  [per_device_pair(): feat_other = lax.ppermute(clip_feats, 'tile', swap)]
    ppermute x1, starting transfers between devices: 2.24 us -> 1.76 us  [per_device_pair(): far_in_a = lax.ppermute(far_a, 'frame', beside)]
    ppermute x1, waiting for transfers between devices: 0.2 us -> 0.67 us  [per_device_pair(): grad_second = lax.ppermute(grad_flat, both, inward)]
    ppermute x1, starting transfers between devices: 2.62 us -> 3.04 us  [per_device_pair(): grad_first = lax.ppermute(grad_flat, both, outward)]
  transfers between devices with their start and end apart: 11 -> 11, of which waited for: 6 -> 7; matrix products, arithmetic and copies ran while one was open for 0% -> 0% of each run, Pallas kernels for 26% -> 27%
where the time goes in v1:
time: 30.1 us; the launch traced here: 29.9 us
  starting transfers between devices  12.5 us (42%)
  Pallas kernels  8.79 us (29%)
  waiting for transfers between devices  7.91 us (26%)
  between operations  0.74 us (2%)
    pallas_call x13, Pallas kernels, kernel_call(): pl.pallas_call(body, out_shape=tuple((jax.ShapeDtypeStruct(shape, kind) f...  8.79 us
    ppermute x1, starting transfers between devices, per_device_pair(): last_a = lax.ppermute(sum_a, 'frame', across)  3.12 us
    ppermute x1, starting transfers between devices, per_device_pair(): grad_first = lax.ppermute(grad_flat, both, outward)  3.04 us
    ppermute x1, waiting for transfers between devices, per_device_pair(): last_b = lax.ppermute(sum_b, 'frame', across)  2.36 us
    ppermute x1, starting transfers between devices, per_device_pair(): last_b = lax.ppermute(sum_b, 'frame', across)  1.96 us
    ppermute x1, starting transfers between devices, per_device_pair(): far_in_a = lax.ppermute(far_a, 'frame', beside)  1.76 us
    ppermute x1, waiting for transfers between devices, per_device_pair(): feat_other = lax.ppermute(clip_feats, 'tile', swap)  1.74 us
    ppermute x1, starting transfers between devices, per_device_pair(): near_in = lax.ppermute(near, 'frame', beside)  1.7 us
  transfers between devices with their start and end apart: 11, of which 7 were waited for; matrix products, arithmetic and copies ran while one was open for 0% of the time, Pallas kernels for 27%

profile of v1, /device:TPU:0, one launch (start us, length us, event | category | flops | bytes accessed | tf_op | source)
XLA Modules:
  0.0 29.9 jit_solution(2690180539041707686)
XLA Ops:
  0.6 0.0 copy-start.1
  0.6 0.0 copy-start.3
  0.6 3.0 %collective-permute-start.2 = (bf16[512,256]{1,0:T(8,128)(2,1)}, bf16[512,256]{1,0:T(8,128)(2,1)S(1)}, u32[]{:S(2)}, u32[]{:S(2)}) collective-permute-start(bf16[512,256]{1,0:T(8,128)(2,1)} %bitcast.9), channel_id=1, source_target_pairs={{0,2},{2,4},{4,6},{3,1},{5,3},{7,5},{6,7},{1,0},{8,10},{10,12},{12... | collective-permute-start | bytes 786440 | tf_op jit(solution)/shard_map/ppermute | solution.py:352
  3.7 0.0 collective-permute-start.3
  3.7 0.0 collective-permute-start
  3.7 1.7 %collective-permute-done.other = bf16[8,4,16,256]{3,2,1,0:T(8,128)(2,1)S(1)} collective-permute-done((bf16[8,4,16,256]{3,2,1,0:T(8,128)(2,1)}, bf16[8,4,16,256]{3,2,1,0:T(8,128)(2,1)S(1)}, u32[]{:S(2)}, u32[]{:S(2)}) %collective-permute-start) | collective-permute-done | bytes 262176 | tf_op jit(solution)/shard_map/ppermute | solution.py:354
  5.4 0.0 copy-done.1
  5.4 0.0 copy-done.3
  5.4 1.7 %shard_map.68 = (f32[512,256]{1,0:T(8,128)S(1)}, bf16[2,512,256]{2,1,0:T(8,128)(2,1)S(1)}) custom-call(bf16[8,4,16,256]{3,2,1,0:T(8,128)(2,1)S(1)} %copy-done.1, bf16[2304,256]{1,0:T(8,128)(2,1)S(1)} %copy-done.3, bf16[8,4,16,256]{3,2,1,0:T(8,128)(2,1)S(1)} %collective-permute-done.other, f32[8,128]{1,0:T(8,128)S(1)} %shard_map.67._), custom_call_target="tpu_custom_call" | custom-call | flops 1207959552 | bytes 2756608 | tf_op jit(solution)/shard_map/pallas_call | solution.py:129
  7.2 0.0 copy-start
  7.2 0.0 copy-start.2
  7.2 0.4 %collective-permute-start.1 = (bf16[2,512,256]{2,1,0:T(8,128)(2,1)S(1)}, bf16[2,512,256]{2,1,0:T(8,128)(2,1)S(1)}, u32[]{:S(2)}, u32[]{:S(2)}) collective-permute-start(bf16[2,512,256]{2,1,0:T(8,128)(2,1)S(1)} %get-tuple-element.16.act), channel_id=1, source_target_pairs={{2,0},{4,2},{6,4},{1,3},{3,5},{5,7},{7,6},{0,1},{10,8},{12,10},{14... | collective-permute-start | bytes 1572872 | tf_op jit(solution)/shard_map/ppermute | solution.py:364
  7.6 0.5 %shard_map.69._.feats_t = bf16[2,768,512]{2,1,0:T(8,128)(2,1)S(1)} custom-call(bf16[8,4,16,256]{3,2,1,0:T(8,128)(2,1)S(1)} %copy-done.1, bf16[8,4,16,256]{3,2,1,0:T(8,128)(2,1)S(1)} %collective-permute-done.other, f32[512,256]{1,0:T(8,128)S(1)} %get-tuple-element.17._.pre_ref), custom_call_target="tpu_custom_call" | custom-call | bytes 2621440 | tf_op jit(solution)/shard_map/pallas_call | solution.py:129
  8.1 1.5 %collective-permute-done.2.first_in = bf16[512,256]{1,0:T(8,128)(2,1)S(1)} collective-permute-done((bf16[512,256]{1,0:T(8,128)(2,1)}, bf16[512,256]{1,0:T(8,128)(2,1)S(1)}, u32[]{:S(2)}, u32[]{:S(2)}) %collective-permute-start.2) | collective-permute-done | bytes 262176 | tf_op jit(solution)/shard_map/ppermute | solution.py:352
  9.6 0.7 %collective-permute-done.3.second_in = bf16[512,256]{1,0:T(8,128)(2,1)S(1)} collective-permute-done((bf16[512,256]{1,0:T(8,128)(2,1)}, bf16[512,256]{1,0:T(8,128)(2,1)S(1)}, u32[]{:S(2)}, u32[]{:S(2)}) %collective-permute-start.3) | collective-permute-done | bytes 262176 | tf_op jit(solution)/shard_map/ppermute | solution.py:353
  10.3 0.0 copy-done
  10.3 0.0 copy-done.2
  10.3 0.9 %shard_map.70 = bf16[512,256]{1,0:T(8,128)(2,1)S(1)} custom-call(bf16[512,256]{1,0:T(8,128)(2,1)S(1)} %bitcast.11, bf16[512,256]{1,0:T(8,128)(2,1)S(1)} %collective-permute-done.2.first_in, bf16[512,256]{1,0:T(8,128)(2,1)S(1)} %collective-permute-done.3.second_in, bf16[2304,256]{1,0:T(8,128)(2,1)S(1)} %copy-done, ...), custom_call_target="tpu_custom_call" | custom-call | flops 603979776 | bytes 4325376 | tf_op jit(solution)/shard_map/pallas_call | solution.py:129
  11.2 0.1 collective-permute-start.4
  11.3 0.8 %shard_map.71.term = f32[3,768,256]{2,1,0:T(8,128)S(1)} custom-call(bf16[2,768,512]{2,1,0:T(8,128)(2,1)S(1)} %shard_map.69._.feats_t, bf16[8,4,16,256]{3,2,1,0:T(8,128)(2,1)S(1)} %bitcast.7), custom_call_target="tpu_custom_call" | custom-call | flops 603979776 | bytes 4194304 | tf_op jit(solution)/shard_map/pallas_call | solution.py:129
  12.1 0.7 %collective-permute-done.4.other = bf16[8,4,16,256]{3,2,1,0:T(8,128)(2,1)S(1)} collective-permute-done((bf16[8,4,16,256]{3,2,1,0:T(8,128)(2,1)S(1)}, bf16[8,4,16,256]{3,2,1,0:T(8,128)(2,1)S(1)}, u32[]{:S(2)}, u32[]{:S(2)}) %collective-permute-start.4) | collective-permute-done | bytes 262176 | tf_op jit(solution)/shard_map/ppermute | solution.py:380
  12.8 0.9 %shard_map.72 = (bf16[144,256]{1,0:T(8,128)(2,1)S(1)}, bf16[144,256]{1,0:T(8,128)(2,1)S(1)}, f32[288,256]{1,0:T(8,128)S(1)}, bf16[288,256]{1,0:T(8,128)(2,1)S(1)}, f32[288,256]{1,0:T(8,128)S(1)}) custom-call(bf16[2,768,512]{2,1,0:T(8,128)(2,1)S(1)} %shard_map.69._.feats_t, bf16[8,4,16,256]{3,2,1,0:T(8,128)(2,1)S(1)} %collective-permute-done.4.other, ...), custom_call_target="tpu_custom_call" | custom-call | flops 603979776 | bytes 5079040 | tf_op jit(solution)/shard_map/pallas_call | solution.py:129
  13.7 1.8 %collective-permute-start.6 = (bf16[144,256]{1,0:T(8,128)(2,1)S(1)}, bf16[144,256]{1,0:T(8,128)(2,1)S(1)}, u32[]{:S(2)}, u32[]{:S(2)}) collective-permute-start(bf16[144,256]{1,0:T(8,128)(2,1)S(1)} %get-tuple-element.20), channel_id=1, source_target_pairs={{0,2},{2,0},{4,6},{6,4},{1,3},{3,1},{5,7},{7,5},{8,10},{10,8},{12,... | collective-permute-start | bytes 221192 | tf_op jit(solution)/shard_map/ppermute | solution.py:400
  15.4 0.3 %collective-permute-start.5 = (bf16[144,256]{1,0:T(8,128)(2,1)S(1)}, bf16[144,256]{1,0:T(8,128)(2,1)S(1)}, u32[]{:S(2)}, u32[]{:S(2)}) collective-permute-start(bf16[144,256]{1,0:T(8,128)(2,1)S(1)} %get-tuple-element.19), channel_id=1, source_target_pairs={{0,2},{2,0},{4,6},{6,4},{1,3},{3,1},{5,7},{7,5},{8,10},{10,8},{12,... | collective-permute-start | bytes 221192 | tf_op jit(solution)/shard_map/ppermute | solution.py:401
  15.8 1.7 %collective-permute-start.9 = (bf16[288,256]{1,0:T(8,128)(2,1)S(1)}, bf16[288,256]{1,0:T(8,128)(2,1)S(1)}, u32[]{:S(2)}, u32[]{:S(2)}) collective-permute-start(bf16[288,256]{1,0:T(8,128)(2,1)S(1)} %get-tuple-element.23), channel_id=1, source_target_pairs={{0,2},{2,0},{4,6},{6,4},{1,3},{3,1},{5,7},{7,5},{8,10},{10,8},{12,... | collective-permute-start | bytes 442376 | tf_op jit(solution)/shard_map/ppermute | solution.py:402
  17.5 0.9 %collective-permute-done.6.arrived = bf16[144,256]{1,0:T(8,128)(2,1)S(1)} collective-permute-done((bf16[144,256]{1,0:T(8,128)(2,1)S(1)}, bf16[144,256]{1,0:T(8,128)(2,1)S(1)}, u32[]{:S(2)}, u32[]{:S(2)}) %collective-permute-start.6) | collective-permute-done | bytes 73760 | tf_op jit(solution)/shard_map/ppermute | solution.py:400
  18.4 0.0 collective-permute-done.1.rest_0_.arrived
  18.4 3.1 %collective-permute-start.8 = (bf16[144,256]{1,0:T(8,128)(2,1)S(1)}, bf16[144,256]{1,0:T(8,128)(2,1)S(1)}, u32[]{:S(2)}, u32[]{:S(2)}) collective-permute-start(bf16[144,256]{1,0:T(8,128)(2,1)S(1)} %shard_map.73.rest_0_), channel_id=1, source_target_pairs={{0,4},{2,6},{4,0},{6,2},{1,5},{3,7},{5,1},{7,3},{8,12},{10,14},{12... | collective-permute-start | bytes 221192 | tf_op jit(solution)/shard_map/ppermute | solution.py:410
  21.5 0.0 collective-permute-done.5.arrived
  21.5 2.0 %collective-permute-start.10 = (bf16[144,256]{1,0:T(8,128)(2,1)S(1)}, bf16[144,256]{1,0:T(8,128)(2,1)S(1)}, u32[]{:S(2)}, u32[]{:S(2)}) collective-permute-start(bf16[144,256]{1,0:T(8,128)(2,1)S(1)} %shard_map.74._), channel_id=1, source_target_pairs={{0,4},{2,6},{4,0},{6,2},{1,5},{3,7},{5,1},{7,3},{8,12},{10,14},{12... | collective-permute-start | bytes 221192 | tf_op jit(solution)/shard_map/ppermute | solution.py:418
  23.5 0.1 collective-permute-start.7
  23.6 1.5 %shard_map.76 = (bf16[512,256]{1,0:T(8,128)(2,1)}, f32[8,128]{1,0:T(8,128)S(1)}) custom-call(bf16[512,256]{1,0:T(8,128)(2,1)S(1)} %bitcast.12, bf16[8,4,16,256]{3,2,1,0:T(8,128)(2,1)S(1)} %bitcast.8, bf16[8,4,16,256]{3,2,1,0:T(8,128)(2,1)S(1)} %collective-permute-done.4.other, bf16[2304,256]{1,0:T(8,128)(2,1)S(1)} %copy-done.3, bf16[144,256]{1,0:T(8,128)(2,1)S(1)} %shard_map.74._), custom_call_target="tpu_custom_call" | custom-call | flops 603979776 | bytes 2306048 | tf_op jit(solution)/shard_map/pallas_call | solution.py:129
  25.1 0.1 collective-permute-done.9.refs_1_.near
  25.2 0.0 collective-permute-done.8.refs_0_.last_a
  25.2 0.0 collective-permute-done.7.first_in
  25.2 1.6 %shard_map.78 = (bf16[512,256]{1,0:T(8,128)(2,1)}, f32[8,128]{1,0:T(8,128)S(1)}) custom-call(bf16[512,256]{1,0:T(8,128)(2,1)S(1)} %bitcast.5, bf16[2,512,256]{2,1,0:T(8,128)(2,1)S(1)} %get-tuple-element.16.act, bf16[512,256]{1,0:T(8,128)(2,1)S(1)} %collective-permute-done.7.first_in, bf16[512,256]{1,0:T(8,128)(2,1)S(1)} %get-tuple-element.22.second_in, ...), custom_call_target="tpu_custom_call" | custom-call | flops 603979776 | bytes 2760704 | tf_op jit(solution)/shard_map/pallas_call | solution.py:129
  26.8 2.4 %collective-permute-done.10.last_b = bf16[144,256]{1,0:T(8,128)(2,1)S(1)} collective-permute-done((bf16[144,256]{1,0:T(8,128)(2,1)S(1)}, bf16[144,256]{1,0:T(8,128)(2,1)S(1)}, u32[]{:S(2)}, u32[]{:S(2)}) %collective-permute-start.10) | collective-permute-done | bytes 73760 | tf_op jit(solution)/shard_map/ppermute | solution.py:418
  29.1 0.8 %shard_map.79 = f32[288,256]{1,0:T(8,128)} custom-call(f32[288,256]{1,0:T(8,128)S(1)} %get-tuple-element.27.keep, bf16[288,256]{1,0:T(8,128)(2,1)S(1)} %collective-permute-done.9.refs_1_.near, bf16[144,256]{1,0:T(8,128)(2,1)S(1)} %collective-permute-done.8.refs_0_.last_a, bf16[144,256]{1,0:T(8,128)(2,1)S(1)} %collective-permute-done.10.last_b, ...), custom_call_target="tpu_custom_call" | custom-call | bytes 888832 | tf_op jit(solution)/shard_map/pallas_call | solution.py:129
  (5 shorter events, 0.1 us)
Async XLA Ops:
  0.6 4.8 %copy-start.1 = (bf16[8,4,16,256]{3,2,1,0:T(8,128)(2,1)S(1)}, bf16[8,4,16,256]{3,2,1,0:T(8,128)(2,1)}, u32[]{:S(2)}) copy-start(bf16[8,4,16,256]{3,2,1,0:T(8,128)(2,1)} %own.3) | copy-start | bytes 786436
  0.6 4.8 %copy-start.3 = (bf16[2304,256]{1,0:T(8,128)(2,1)S(1)}, bf16[2304,256]{1,0:T(8,128)(2,1)}, u32[]{:S(2)}) copy-start(bf16[2304,256]{1,0:T(8,128)(2,1)} %weight.6) | copy-start | bytes 3538948
  0.6 9.0 %collective-permute-start.2 = (bf16[512,256]{1,0:T(8,128)(2,1)}, bf16[512,256]{1,0:T(8,128)(2,1)S(1)}, u32[]{:S(2)}, u32[]{:S(2)}) collective-permute-start(bf16[512,256]{1,0:T(8,128)(2,1)} %bitcast.9), channel_id=1, source_target_pairs={{0,2},{2,4},{4,6},{3,1},{5,3},{7,5},{6,7},{1,0},{8,10},{10,12},{12... | collective-permute-start | bytes 786440 | tf_op jit(solution)/shard_map/ppermute | solution.py:352
  3.7 6.6 %collective-permute-start.3 = (bf16[512,256]{1,0:T(8,128)(2,1)}, bf16[512,256]{1,0:T(8,128)(2,1)S(1)}, u32[]{:S(2)}, u32[]{:S(2)}) collective-permute-start(bf16[512,256]{1,0:T(8,128)(2,1)} %bitcast.10), channel_id=1, source_target_pairs={{2,0},{4,2},{6,4},{1,3},{3,5},{5,7},{7,6},{0,1},{10,8},{12,10},{14... | collective-permute-start | bytes 786440 | tf_op jit(solution)/shard_map/ppermute | solution.py:353
  3.7 1.7 %collective-permute-start = (bf16[8,4,16,256]{3,2,1,0:T(8,128)(2,1)}, bf16[8,4,16,256]{3,2,1,0:T(8,128)(2,1)S(1)}, u32[]{:S(2)}, u32[]{:S(2)}) collective-permute-start(bf16[8,4,16,256]{3,2,1,0:T(8,128)(2,1)} %own.3), channel_id=1, source_target_pairs={{0,1},{1,0},{2,3},{3,2},{4,5},{5,4},{6,7},{7,6},{8,9},{9,8},{10,11... | collective-permute-start | bytes 786440 | tf_op jit(solution)/shard_map/ppermute | solution.py:354
  7.2 3.1 %copy-start = (bf16[2304,256]{1,0:T(8,128)(2,1)S(1)}, bf16[2304,256]{1,0:T(8,128)(2,1)}, u32[]{:S(2)}) copy-start(bf16[2304,256]{1,0:T(8,128)(2,1)} %weight.7) | copy-start | bytes 3538948
  7.2 3.1 %copy-start.2 = (bf16[8,4,16,256]{3,2,1,0:T(8,128)(2,1)S(1)}, bf16[8,4,16,256]{3,2,1,0:T(8,128)(2,1)}, u32[]{:S(2)}) copy-start(bf16[8,4,16,256]{3,2,1,0:T(8,128)(2,1)} %param.5) | copy-start | bytes 786436
  7.2 11.2 %collective-permute-start.1 = (bf16[2,512,256]{2,1,0:T(8,128)(2,1)S(1)}, bf16[2,512,256]{2,1,0:T(8,128)(2,1)S(1)}, u32[]{:S(2)}, u32[]{:S(2)}) collective-permute-start(bf16[2,512,256]{2,1,0:T(8,128)(2,1)S(1)} %get-tuple-element.16.act), channel_id=1, source_target_pairs={{2,0},{4,2},{6,4},{1,3},{3,5},{5,7},{7,6},{0,1},{10,8},{12,10},{14... | collective-permute-start | bytes 1572872 | tf_op jit(solution)/shard_map/ppermute | solution.py:364
  11.2 1.6 %collective-permute-start.4 = (bf16[8,4,16,256]{3,2,1,0:T(8,128)(2,1)S(1)}, bf16[8,4,16,256]{3,2,1,0:T(8,128)(2,1)S(1)}, u32[]{:S(2)}, u32[]{:S(2)}) collective-permute-start(bf16[8,4,16,256]{3,2,1,0:T(8,128)(2,1)S(1)} %bitcast.6), channel_id=1, source_target_pairs={{0,1},{1,0},{2,3},{3,2},{4,5},{5,4},{6,7},{7,6},{8,9},{9,8},{10,11... | collective-permute-start | bytes 786440 | tf_op jit(solution)/shard_map/ppermute | solution.py:380
  13.7 4.7 %collective-permute-start.6 = (bf16[144,256]{1,0:T(8,128)(2,1)S(1)}, bf16[144,256]{1,0:T(8,128)(2,1)S(1)}, u32[]{:S(2)}, u32[]{:S(2)}) collective-permute-start(bf16[144,256]{1,0:T(8,128)(2,1)S(1)} %get-tuple-element.20), channel_id=1, source_target_pairs={{0,2},{2,0},{4,6},{6,4},{1,3},{3,1},{5,7},{7,5},{8,10},{10,8},{12,... | collective-permute-start | bytes 221192 | tf_op jit(solution)/shard_map/ppermute | solution.py:400
  15.4 6.1 %collective-permute-start.5 = (bf16[144,256]{1,0:T(8,128)(2,1)S(1)}, bf16[144,256]{1,0:T(8,128)(2,1)S(1)}, u32[]{:S(2)}, u32[]{:S(2)}) collective-permute-start(bf16[144,256]{1,0:T(8,128)(2,1)S(1)} %get-tuple-element.19), channel_id=1, source_target_pairs={{0,2},{2,0},{4,6},{6,4},{1,3},{3,1},{5,7},{7,5},{8,10},{10,8},{12,... | collective-permute-start | bytes 221192 | tf_op jit(solution)/shard_map/ppermute | solution.py:401
  15.8 9.4 %collective-permute-start.9 = (bf16[288,256]{1,0:T(8,128)(2,1)S(1)}, bf16[288,256]{1,0:T(8,128)(2,1)S(1)}, u32[]{:S(2)}, u32[]{:S(2)}) collective-permute-start(bf16[288,256]{1,0:T(8,128)(2,1)S(1)} %get-tuple-element.23), channel_id=1, source_target_pairs={{0,2},{2,0},{4,6},{6,4},{1,3},{3,1},{5,7},{7,5},{8,10},{10,8},{12,... | collective-permute-start | bytes 442376 | tf_op jit(solution)/shard_map/ppermute | solution.py:402
  18.4 6.8 %collective-permute-start.8 = (bf16[144,256]{1,0:T(8,128)(2,1)S(1)}, bf16[144,256]{1,0:T(8,128)(2,1)S(1)}, u32[]{:S(2)}, u32[]{:S(2)}) collective-permute-start(bf16[144,256]{1,0:T(8,128)(2,1)S(1)} %shard_map.73.rest_0_), channel_id=1, source_target_pairs={{0,4},{2,6},{4,0},{6,2},{1,5},{3,7},{5,1},{7,3},{8,12},{10,14},{12... | collective-permute-start | bytes 221192 | tf_op jit(solution)/shard_map/ppermute | solution.py:410
  21.5 7.6 %collective-permute-start.10 = (bf16[144,256]{1,0:T(8,128)(2,1)S(1)}, bf16[144,256]{1,0:T(8,128)(2,1)S(1)}, u32[]{:S(2)}, u32[]{:S(2)}) collective-permute-start(bf16[144,256]{1,0:T(8,128)(2,1)S(1)} %shard_map.74._), channel_id=1, source_target_pairs={{0,4},{2,6},{4,0},{6,2},{1,5},{3,7},{5,1},{7,3},{8,12},{10,14},{12... | collective-permute-start | bytes 221192 | tf_op jit(solution)/shard_map/ppermute | solution.py:418
  23.5 1.7 %collective-permute-start.7 = (bf16[512,256]{1,0:T(8,128)(2,1)S(1)}, bf16[512,256]{1,0:T(8,128)(2,1)S(1)}, u32[]{:S(2)}, u32[]{:S(2)}) collective-permute-start(bf16[512,256]{1,0:T(8,128)(2,1)S(1)} %get-tuple-element.21), channel_id=1, source_target_pairs={{0,1},{1,0},{2,3},{3,2},{4,5},{5,4},{6,7},{7,6},{8,9},{9,8},{10,11... | collective-permute-start | bytes 786440 | tf_op jit(solution)/shard_map/ppermute | solution.py:422

commit v2 on v1

--- a/solution.py
+++ b/solution.py
@@ -299,9 +299,9 @@
     share = keep_ref.shape[0]
     half = share // 2
     for distance, skip, ref in (
-        (3, 0, far_a_ref),
-        (3, half, far_b_ref),
-        (2, 0, pass_ref),
+        (2, 0, far_a_ref),
+        (2, half, far_b_ref),
+        (3, 0, pass_ref),
         (1, 0, near_ref),
         (0, 0, keep_ref),
     ):
@@ -396,7 +396,7 @@
         feats_t, pre_other, term,
     )
     beside = [(z, z ^ 1) for z in range(chips)]
-    across = [(z, z ^ 2) for z in range(chips)]
+    across = [(z, z ^ 3) for z in range(chips)]
     far_in_a = lax.ppermute(far_a, "frame", beside)
     far_in_b = lax.ppermute(far_b, "frame", beside)
     near_in = lax.ppermute(near, "frame", beside)

time: 30.1 us -> 30.2 us (level)
  starting transfers between devices: 12.5 us -> 13.4 us
  waiting for transfers between devices: 7.91 us -> 7.03 us
    ppermute x1, waiting for transfers between devices: 2.36 us -> 0.01 us  [per_device_pair(): last_b = lax.ppermute(sum_b, 'frame', across)]
    ppermute x1, waiting for transfers between devices: 0.01 us -> 1.54 us  [per_device_pair(): last_a = lax.ppermute(sum_a, 'frame', across)]
    ppermute x1, starting transfers between devices: 3.12 us -> 4.51 us  [per_device_pair(): last_a = lax.ppermute(sum_a, 'frame', across)]
    ppermute x1, starting transfers between devices: 1.96 us -> 1.55 us  [per_device_pair(): last_b = lax.ppermute(sum_b, 'frame', across)]
  transfers between devices with their start and end apart: 11 -> 11, of which waited for: 7 -> 6; matrix products, arithmetic and copies ran while one was open for 0% -> 0% of each run, Pallas kernels for 27% -> 27%
where the time goes in v2:
time: 30.2 us; the launch traced here: 30 us
  starting transfers between devices  13.4 us (44%)
  Pallas kernels  8.78 us (29%)
  waiting for transfers between devices  7.03 us (23%)
  between operations  0.74 us (2%)
    pallas_call x13, Pallas kernels, kernel_call(): pl.pallas_call(body, out_shape=tuple((jax.ShapeDtypeStruct(shape, kind) f...  8.78 us
    ppermute x1, starting transfers between devices, per_device_pair(): last_a = lax.ppermute(sum_a, 'frame', across)  4.51 us
    ppermute x1, starting transfers between devices, per_device_pair(): grad_first = lax.ppermute(grad_flat, both, outward)  3.04 us
    ppermute x1, starting transfers between devices, per_device_pair(): far_in_a = lax.ppermute(far_a, 'frame', beside)  1.76 us
    ppermute x1, waiting for transfers between devices, per_device_pair(): feat_other = lax.ppermute(clip_feats, 'tile', swap)  1.74 us
    ppermute x1, starting transfers between devices, per_device_pair(): near_in = lax.ppermute(near, 'frame', beside)  1.7 us
    ppermute x1, starting transfers between devices, per_device_pair(): last_b = lax.ppermute(sum_b, 'frame', across)  1.55 us
    ppermute x1, waiting for transfers between devices, per_device_pair(): last_a = lax.ppermute(sum_a, 'frame', across)  1.54 us
  transfers between devices with their start and end apart: 11, of which 6 were waited for; matrix products, arithmetic and copies ran while one was open for 0% of the time, Pallas kernels for 27%

profile of v2, /device:TPU:0, one launch (start us, length us, event | category | flops | bytes accessed | tf_op | source)
XLA Modules:
  0.0 30.0 jit_solution(15095353479634090103)
XLA Ops:
  0.6 0.0 copy-start.1
  0.6 0.0 copy-start.3
  0.6 3.0 %collective-permute-start.2 = (bf16[512,256]{1,0:T(8,128)(2,1)}, bf16[512,256]{1,0:T(8,128)(2,1)S(1)}, u32[]{:S(2)}, u32[]{:S(2)}) collective-permute-start(bf16[512,256]{1,0:T(8,128)(2,1)} %bitcast.9), channel_id=1, source_target_pairs={{0,2},{2,4},{4,6},{3,1},{5,3},{7,5},{6,7},{1,0},{8,10},{10,12},{12... | collective-permute-start | bytes 786440 | tf_op jit(solution)/shard_map/ppermute | solution.py:352
  3.7 0.0 collective-permute-start.3
  3.7 0.0 collective-permute-start
  3.7 1.7 %collective-permute-done.other = bf16[8,4,16,256]{3,2,1,0:T(8,128)(2,1)S(1)} collective-permute-done((bf16[8,4,16,256]{3,2,1,0:T(8,128)(2,1)}, bf16[8,4,16,256]{3,2,1,0:T(8,128)(2,1)S(1)}, u32[]{:S(2)}, u32[]{:S(2)}) %collective-permute-start) | collective-permute-done | bytes 262176 | tf_op jit(solution)/shard_map/ppermute | solution.py:354
  5.4 0.0 copy-done.1
  5.4 0.0 copy-done.3
  5.4 1.7 %shard_map.68 = (f32[512,256]{1,0:T(8,128)S(1)}, bf16[2,512,256]{2,1,0:T(8,128)(2,1)S(1)}) custom-call(bf16[8,4,16,256]{3,2,1,0:T(8,128)(2,1)S(1)} %copy-done.1, bf16[2304,256]{1,0:T(8,128)(2,1)S(1)} %copy-done.3, bf16[8,4,16,256]{3,2,1,0:T(8,128)(2,1)S(1)} %collective-permute-done.other, f32[8,128]{1,0:T(8,128)S(1)} %shard_map.67._), custom_call_target="tpu_custom_call" | custom-call | flops 1207959552 | bytes 2756608 | tf_op jit(solution)/shard_map/pallas_call | solution.py:129
  7.2 0.0 copy-start
  7.2 0.0 copy-start.2
  7.2 0.4 %collective-permute-start.1 = (bf16[2,512,256]{2,1,0:T(8,128)(2,1)S(1)}, bf16[2,512,256]{2,1,0:T(8,128)(2,1)S(1)}, u32[]{:S(2)}, u32[]{:S(2)}) collective-permute-start(bf16[2,512,256]{2,1,0:T(8,128)(2,1)S(1)} %get-tuple-element.16.act), channel_id=1, source_target_pairs={{2,0},{4,2},{6,4},{1,3},{3,5},{5,7},{7,6},{0,1},{10,8},{12,10},{14... | collective-permute-start | bytes 1572872 | tf_op jit(solution)/shard_map/ppermute | solution.py:364
  7.6 0.5 %shard_map.69._.feats_t = bf16[2,768,512]{2,1,0:T(8,128)(2,1)S(1)} custom-call(bf16[8,4,16,256]{3,2,1,0:T(8,128)(2,1)S(1)} %copy-done.1, bf16[8,4,16,256]{3,2,1,0:T(8,128)(2,1)S(1)} %collective-permute-done.other, f32[512,256]{1,0:T(8,128)S(1)} %get-tuple-element.17._.pre_ref), custom_call_target="tpu_custom_call" | custom-call | bytes 2621440 | tf_op jit(solution)/shard_map/pallas_call | solution.py:129
  8.1 1.5 %collective-permute-done.2.first_in = bf16[512,256]{1,0:T(8,128)(2,1)S(1)} collective-permute-done((bf16[512,256]{1,0:T(8,128)(2,1)}, bf16[512,256]{1,0:T(8,128)(2,1)S(1)}, u32[]{:S(2)}, u32[]{:S(2)}) %collective-permute-start.2) | collective-permute-done | bytes 262176 | tf_op jit(solution)/shard_map/ppermute | solution.py:352
  9.6 0.7 %collective-permute-done.3.second_in = bf16[512,256]{1,0:T(8,128)(2,1)S(1)} collective-permute-done((bf16[512,256]{1,0:T(8,128)(2,1)}, bf16[512,256]{1,0:T(8,128)(2,1)S(1)}, u32[]{:S(2)}, u32[]{:S(2)}) %collective-permute-start.3) | collective-permute-done | bytes 262176 | tf_op jit(solution)/shard_map/ppermute | solution.py:353
  10.3 0.0 copy-done
  10.3 0.0 copy-done.2
  10.3 0.9 %shard_map.70 = bf16[512,256]{1,0:T(8,128)(2,1)S(1)} custom-call(bf16[512,256]{1,0:T(8,128)(2,1)S(1)} %bitcast.11, bf16[512,256]{1,0:T(8,128)(2,1)S(1)} %collective-permute-done.2.first_in, bf16[512,256]{1,0:T(8,128)(2,1)S(1)} %collective-permute-done.3.second_in, bf16[2304,256]{1,0:T(8,128)(2,1)S(1)} %copy-done, ...), custom_call_target="tpu_custom_call" | custom-call | flops 603979776 | bytes 4325376 | tf_op jit(solution)/shard_map/pallas_call | solution.py:129
  11.2 0.1 collective-permute-start.4
  11.3 0.8 %shard_map.71.term = f32[3,768,256]{2,1,0:T(8,128)S(1)} custom-call(bf16[2,768,512]{2,1,0:T(8,128)(2,1)S(1)} %shard_map.69._.feats_t, bf16[8,4,16,256]{3,2,1,0:T(8,128)(2,1)S(1)} %bitcast.7), custom_call_target="tpu_custom_call" | custom-call | flops 603979776 | bytes 4194304 | tf_op jit(solution)/shard_map/pallas_call | solution.py:129
  12.1 0.7 %collective-permute-done.4.other = bf16[8,4,16,256]{3,2,1,0:T(8,128)(2,1)S(1)} collective-permute-done((bf16[8,4,16,256]{3,2,1,0:T(8,128)(2,1)S(1)}, bf16[8,4,16,256]{3,2,1,0:T(8,128)(2,1)S(1)}, u32[]{:S(2)}, u32[]{:S(2)}) %collective-permute-start.4) | collective-permute-done | bytes 262176 | tf_op jit(solution)/shard_map/ppermute | solution.py:380
  12.8 0.9 %shard_map.72 = (bf16[144,256]{1,0:T(8,128)(2,1)S(1)}, bf16[144,256]{1,0:T(8,128)(2,1)S(1)}, f32[288,256]{1,0:T(8,128)S(1)}, bf16[288,256]{1,0:T(8,128)(2,1)S(1)}, f32[288,256]{1,0:T(8,128)S(1)}) custom-call(bf16[2,768,512]{2,1,0:T(8,128)(2,1)S(1)} %shard_map.69._.feats_t, bf16[8,4,16,256]{3,2,1,0:T(8,128)(2,1)S(1)} %collective-permute-done.4.other, ...), custom_call_target="tpu_custom_call" | custom-call | flops 603979776 | bytes 5079040 | tf_op jit(solution)/shard_map/pallas_call | solution.py:129
  13.7 1.8 %collective-permute-start.6 = (bf16[144,256]{1,0:T(8,128)(2,1)S(1)}, bf16[144,256]{1,0:T(8,128)(2,1)S(1)}, u32[]{:S(2)}, u32[]{:S(2)}) collective-permute-start(bf16[144,256]{1,0:T(8,128)(2,1)S(1)} %get-tuple-element.20), channel_id=1, source_target_pairs={{0,2},{2,0},{4,6},{6,4},{1,3},{3,1},{5,7},{7,5},{8,10},{10,8},{12,... | collective-permute-start | bytes 221192 | tf_op jit(solution)/shard_map/ppermute | solution.py:400
  15.4 0.3 %collective-permute-start.5 = (bf16[144,256]{1,0:T(8,128)(2,1)S(1)}, bf16[144,256]{1,0:T(8,128)(2,1)S(1)}, u32[]{:S(2)}, u32[]{:S(2)}) collective-permute-start(bf16[144,256]{1,0:T(8,128)(2,1)S(1)} %get-tuple-element.19), channel_id=1, source_target_pairs={{0,2},{2,0},{4,6},{6,4},{1,3},{3,1},{5,7},{7,5},{8,10},{10,8},{12,... | collective-permute-start | bytes 221192 | tf_op jit(solution)/shard_map/ppermute | solution.py:401
  15.8 1.7 %collective-permute-start.9 = (bf16[288,256]{1,0:T(8,128)(2,1)S(1)}, bf16[288,256]{1,0:T(8,128)(2,1)S(1)}, u32[]{:S(2)}, u32[]{:S(2)}) collective-permute-start(bf16[288,256]{1,0:T(8,128)(2,1)S(1)} %get-tuple-element.23), channel_id=1, source_target_pairs={{0,2},{2,0},{4,6},{6,4},{1,3},{3,1},{5,7},{7,5},{8,10},{10,8},{12,... | collective-permute-start | bytes 442376 | tf_op jit(solution)/shard_map/ppermute | solution.py:402
  17.5 0.9 %collective-permute-done.6.arrived = bf16[144,256]{1,0:T(8,128)(2,1)S(1)} collective-permute-done((bf16[144,256]{1,0:T(8,128)(2,1)S(1)}, bf16[144,256]{1,0:T(8,128)(2,1)S(1)}, u32[]{:S(2)}, u32[]{:S(2)}) %collective-permute-start.6) | collective-permute-done | bytes 73760 | tf_op jit(solution)/shard_map/ppermute | solution.py:400
  18.3 0.0 collective-permute-done.1.rest_0_.arrived
  18.4 4.5 %collective-permute-start.8 = (bf16[144,256]{1,0:T(8,128)(2,1)S(1)}, bf16[144,256]{1,0:T(8,128)(2,1)S(1)}, u32[]{:S(2)}, u32[]{:S(2)}) collective-permute-start(bf16[144,256]{1,0:T(8,128)(2,1)S(1)} %shard_map.73.rest_0_), channel_id=1, source_target_pairs={{0,6},{2,4},{4,2},{6,0},{1,7},{3,5},{5,3},{7,1},{8,14},{10,12},{12... | collective-permute-start | bytes 221192 | tf_op jit(solution)/shard_map/ppermute | solution.py:410
  22.9 0.0 collective-permute-done.5.arrived
  22.9 1.5 %collective-permute-start.10 = (bf16[144,256]{1,0:T(8,128)(2,1)S(1)}, bf16[144,256]{1,0:T(8,128)(2,1)S(1)}, u32[]{:S(2)}, u32[]{:S(2)}) collective-permute-start(bf16[144,256]{1,0:T(8,128)(2,1)S(1)} %shard_map.74._), channel_id=1, source_target_pairs={{0,6},{2,4},{4,2},{6,0},{1,7},{3,5},{5,3},{7,1},{8,14},{10,12},{12... | collective-permute-start | bytes 221192 | tf_op jit(solution)/shard_map/ppermute | solution.py:418
  24.5 0.1 collective-permute-start.7
  24.6 1.5 %shard_map.76 = (bf16[512,256]{1,0:T(8,128)(2,1)}, f32[8,128]{1,0:T(8,128)S(1)}) custom-call(bf16[512,256]{1,0:T(8,128)(2,1)S(1)} %bitcast.12, bf16[8,4,16,256]{3,2,1,0:T(8,128)(2,1)S(1)} %bitcast.8, bf16[8,4,16,256]{3,2,1,0:T(8,128)(2,1)S(1)} %collective-permute-done.4.other, bf16[2304,256]{1,0:T(8,128)(2,1)S(1)} %copy-done.3, bf16[144,256]{1,0:T(8,128)(2,1)S(1)} %shard_map.74._), custom_call_target="tpu_custom_call" | custom-call | flops 603979776 | bytes 2306048 | tf_op jit(solution)/shard_map/pallas_call | solution.py:129
  26.1 0.0 collective-permute-done.9.refs_1_.near
  26.1 1.5 %collective-permute-done.8.refs_0_.last_a = bf16[144,256]{1,0:T(8,128)(2,1)S(1)} collective-permute-done((bf16[144,256]{1,0:T(8,128)(2,1)S(1)}, bf16[144,256]{1,0:T(8,128)(2,1)S(1)}, u32[]{:S(2)}, u32[]{:S(2)}) %collective-permute-start.8) | collective-permute-done | bytes 73760 | tf_op jit(solution)/shard_map/ppermute | solution.py:410
  27.7 0.0 collective-permute-done.7.first_in
  27.7 1.6 %shard_map.78 = (bf16[512,256]{1,0:T(8,128)(2,1)}, f32[8,128]{1,0:T(8,128)S(1)}) custom-call(bf16[512,256]{1,0:T(8,128)(2,1)S(1)} %bitcast.5, bf16[2,512,256]{2,1,0:T(8,128)(2,1)S(1)} %get-tuple-element.16.act, bf16[512,256]{1,0:T(8,128)(2,1)S(1)} %collective-permute-done.7.first_in, bf16[512,256]{1,0:T(8,128)(2,1)S(1)} %get-tuple-element.22.second_in, ...), custom_call_target="tpu_custom_call" | custom-call | flops 603979776 | bytes 2760704 | tf_op jit(solution)/shard_map/pallas_call | solution.py:129
  29.2 0.0 collective-permute-done.10.last_b
  29.2 0.8 %shard_map.79 = f32[288,256]{1,0:T(8,128)} custom-call(f32[288,256]{1,0:T(8,128)S(1)} %get-tuple-element.27.keep, bf16[288,256]{1,0:T(8,128)(2,1)S(1)} %collective-permute-done.9.refs_1_.near, bf16[144,256]{1,0:T(8,128)(2,1)S(1)} %collective-permute-done.8.refs_0_.last_a, bf16[144,256]{1,0:T(8,128)(2,1)S(1)} %collective-permute-done.10.last_b, ...), custom_call_target="tpu_custom_call" | custom-call | bytes 888832 | tf_op jit(solution)/shard_map/pallas_call | solution.py:129
  (5 shorter events, 0.1 us)
Async XLA Ops:
  0.6 4.8 %copy-start.1 = (bf16[8,4,16,256]{3,2,1,0:T(8,128)(2,1)S(1)}, bf16[8,4,16,256]{3,2,1,0:T(8,128)(2,1)}, u32[]{:S(2)}) copy-start(bf16[8,4,16,256]{3,2,1,0:T(8,128)(2,1)} %own.3) | copy-start | bytes 786436
  0.6 4.8 %copy-start.3 = (bf16[2304,256]{1,0:T(8,128)(2,1)S(1)}, bf16[2304,256]{1,0:T(8,128)(2,1)}, u32[]{:S(2)}) copy-start(bf16[2304,256]{1,0:T(8,128)(2,1)} %weight.6) | copy-start | bytes 3538948
  0.6 9.0 %collective-permute-start.2 = (bf16[512,256]{1,0:T(8,128)(2,1)}, bf16[512,256]{1,0:T(8,128)(2,1)S(1)}, u32[]{:S(2)}, u32[]{:S(2)}) collective-permute-start(bf16[512,256]{1,0:T(8,128)(2,1)} %bitcast.9), channel_id=1, source_target_pairs={{0,2},{2,4},{4,6},{3,1},{5,3},{7,5},{6,7},{1,0},{8,10},{10,12},{12... | collective-permute-start | bytes 786440 | tf_op jit(solution)/shard_map/ppermute | solution.py:352
  3.7 6.6 %collective-permute-start.3 = (bf16[512,256]{1,0:T(8,128)(2,1)}, bf16[512,256]{1,0:T(8,128)(2,1)S(1)}, u32[]{:S(2)}, u32[]{:S(2)}) collective-permute-start(bf16[512,256]{1,0:T(8,128)(2,1)} %bitcast.10), channel_id=1, source_target_pairs={{2,0},{4,2},{6,4},{1,3},{3,5},{5,7},{7,6},{0,1},{10,8},{12,10},{14... | collective-permute-start | bytes 786440 | tf_op jit(solution)/shard_map/ppermute | solution.py:353
  3.7 1.7 %collective-permute-start = (bf16[8,4,16,256]{3,2,1,0:T(8,128)(2,1)}, bf16[8,4,16,256]{3,2,1,0:T(8,128)(2,1)S(1)}, u32[]{:S(2)}, u32[]{:S(2)}) collective-permute-start(bf16[8,4,16,256]{3,2,1,0:T(8,128)(2,1)} %own.3), channel_id=1, source_target_pairs={{0,1},{1,0},{2,3},{3,2},{4,5},{5,4},{6,7},{7,6},{8,9},{9,8},{10,11... | collective-permute-start | bytes 786440 | tf_op jit(solution)/shard_map/ppermute | solution.py:354
  7.2 3.1 %copy-start = (bf16[2304,256]{1,0:T(8,128)(2,1)S(1)}, bf16[2304,256]{1,0:T(8,128)(2,1)}, u32[]{:S(2)}) copy-start(bf16[2304,256]{1,0:T(8,128)(2,1)} %weight.7) | copy-start | bytes 3538948
  7.2 3.1 %copy-start.2 = (bf16[8,4,16,256]{3,2,1,0:T(8,128)(2,1)S(1)}, bf16[8,4,16,256]{3,2,1,0:T(8,128)(2,1)}, u32[]{:S(2)}) copy-start(bf16[8,4,16,256]{3,2,1,0:T(8,128)(2,1)} %param.5) | copy-start | bytes 786436
  7.2 11.2 %collective-permute-start.1 = (bf16[2,512,256]{2,1,0:T(8,128)(2,1)S(1)}, bf16[2,512,256]{2,1,0:T(8,128)(2,1)S(1)}, u32[]{:S(2)}, u32[]{:S(2)}) collective-permute-start(bf16[2,512,256]{2,1,0:T(8,128)(2,1)S(1)} %get-tuple-element.16.act), channel_id=1, source_target_pairs={{2,0},{4,2},{6,4},{1,3},{3,5},{5,7},{7,6},{0,1},{10,8},{12,10},{14... | collective-permute-start | bytes 1572872 | tf_op jit(solution)/shard_map/ppermute | solution.py:364
  11.2 1.6 %collective-permute-start.4 = (bf16[8,4,16,256]{3,2,1,0:T(8,128)(2,1)S(1)}, bf16[8,4,16,256]{3,2,1,0:T(8,128)(2,1)S(1)}, u32[]{:S(2)}, u32[]{:S(2)}) collective-permute-start(bf16[8,4,16,256]{3,2,1,0:T(8,128)(2,1)S(1)} %bitcast.6), channel_id=1, source_target_pairs={{0,1},{1,0},{2,3},{3,2},{4,5},{5,4},{6,7},{7,6},{8,9},{9,8},{10,11... | collective-permute-start | bytes 786440 | tf_op jit(solution)/shard_map/ppermute | solution.py:380
  13.7 4.7 %collective-permute-start.6 = (bf16[144,256]{1,0:T(8,128)(2,1)S(1)}, bf16[144,256]{1,0:T(8,128)(2,1)S(1)}, u32[]{:S(2)}, u32[]{:S(2)}) collective-permute-start(bf16[144,256]{1,0:T(8,128)(2,1)S(1)} %get-tuple-element.20), channel_id=1, source_target_pairs={{0,2},{2,0},{4,6},{6,4},{1,3},{3,1},{5,7},{7,5},{8,10},{10,8},{12,... | collective-permute-start | bytes 221192 | tf_op jit(solution)/shard_map/ppermute | solution.py:400
  15.4 7.4 %collective-permute-start.5 = (bf16[144,256]{1,0:T(8,128)(2,1)S(1)}, bf16[144,256]{1,0:T(8,128)(2,1)S(1)}, u32[]{:S(2)}, u32[]{:S(2)}) collective-permute-start(bf16[144,256]{1,0:T(8,128)(2,1)S(1)} %get-tuple-element.19), channel_id=1, source_target_pairs={{0,2},{2,0},{4,6},{6,4},{1,3},{3,1},{5,7},{7,5},{8,10},{10,8},{12,... | collective-permute-start | bytes 221192 | tf_op jit(solution)/shard_map/ppermute | solution.py:401
  15.8 10.4 %collective-permute-start.9 = (bf16[288,256]{1,0:T(8,128)(2,1)S(1)}, bf16[288,256]{1,0:T(8,128)(2,1)S(1)}, u32[]{:S(2)}, u32[]{:S(2)}) collective-permute-start(bf16[288,256]{1,0:T(8,128)(2,1)S(1)} %get-tuple-element.23), channel_id=1, source_target_pairs={{0,2},{2,0},{4,6},{6,4},{1,3},{3,1},{5,7},{7,5},{8,10},{10,8},{12,... | collective-permute-start | bytes 442376 | tf_op jit(solution)/shard_map/ppermute | solution.py:402
  18.4 9.3 %collective-permute-start.8 = (bf16[144,256]{1,0:T(8,128)(2,1)S(1)}, bf16[144,256]{1,0:T(8,128)(2,1)S(1)}, u32[]{:S(2)}, u32[]{:S(2)}) collective-permute-start(bf16[144,256]{1,0:T(8,128)(2,1)S(1)} %shard_map.73.rest_0_), channel_id=1, source_target_pairs={{0,6},{2,4},{4,2},{6,0},{1,7},{3,5},{5,3},{7,1},{8,14},{10,12},{12... | collective-permute-start | bytes 221192 | tf_op jit(solution)/shard_map/ppermute | solution.py:410
  22.9 6.3 %collective-permute-start.10 = (bf16[144,256]{1,0:T(8,128)(2,1)S(1)}, bf16[144,256]{1,0:T(8,128)(2,1)S(1)}, u32[]{:S(2)}, u32[]{:S(2)}) collective-permute-start(bf16[144,256]{1,0:T(8,128)(2,1)S(1)} %shard_map.74._), channel_id=1, source_target_pairs={{0,6},{2,4},{4,2},{6,0},{1,7},{3,5},{5,3},{7,1},{8,14},{10,12},{12... | collective-permute-start | bytes 221192 | tf_op jit(solution)/shard_map/ppermute | solution.py:418
  24.5 3.2 %collective-permute-start.7 = (bf16[512,256]{1,0:T(8,128)(2,1)S(1)}, bf16[512,256]{1,0:T(8,128)(2,1)S(1)}, u32[]{:S(2)}, u32[]{:S(2)}) collective-permute-start(bf16[512,256]{1,0:T(8,128)(2,1)S(1)} %get-tuple-element.21), channel_id=1, source_target_pairs={{0,1},{1,0},{2,3},{3,2},{4,5},{5,4},{6,7},{7,6},{8,9},{9,8},{10,11... | collective-permute-start | bytes 786440 | tf_op jit(solution)/shard_map/ppermute | solution.py:422

commit v3 on v2

--- a/solution.py
+++ b/solution.py
@@ -209,7 +209,8 @@
     sum_ref[...] = (rows + came).astype(sum_ref.dtype)
 
 
-def last_sum_kernel(keep, near, last_a, last_b, _, out_ref, *, scale):
+def last_sum_kernel(keep, near, last_a, last_b, block, out_ref, block_ref, *, scale):
+    block_ref[...] = block[...]
     half = last_a.shape[0]
     for first, last in ((0, last_a), (half, last_b)):
         total = keep[first : first + half] + near[first : first + half].astype(jnp.float32)
@@ -264,7 +265,7 @@
     out_ref[...] = (act_grad * (sig * (1.0 + pre * (1.0 - sig)))).astype(jnp.bfloat16)
 
 
-def temporal_kernel(feats, act, first_in, second_in, weight, _, out_ref, done_ref, ext):
+def temporal_kernel(feats, act, first_in, second_in, weight, _, out_ref, ext):
     count, channels = feats.shape
     own = act.at[lax.axis_index("tile")]
     frames = slabs(own, first_in, second_in, ext)
@@ -272,7 +273,6 @@
     columns = jnp.concatenate([frames[k * hop : k * hop + count] for k in range(9)], axis=1)
     mixed = jnp.dot(columns, weight[...], preferred_element_type=jnp.float32)
     out_ref[...] = (feats[...].astype(jnp.float32) + mixed).astype(jnp.bfloat16)
-    done_ref[...] = jnp.zeros_like(done_ref)
 
 
 def own_term_kernel(feats_t, own, total_ref):
@@ -431,19 +431,19 @@
     (arrived,) = kernel_call(
         order_kernel, [((8, 128), f32)], [], 20 * product, last_a, near_in, done, anywhere=3
     )
-    block_out, done = kernel_call(
+    (block,) = kernel_call(
         temporal_kernel,
-        [(flat, bf16), ((8, 128), f32)],
+        [(flat, bf16)],
         [three],
         product,
         feat_flat, act, act_first, act_second, temporal_weight, arrived, anywhere=1,
     )
-    (weight_grad,) = kernel_call(
+    weight_grad, block_out = kernel_call(
         functools.partial(last_sum_kernel, scale=scale),
-        [(share, f32)],
+        [(share, f32), (flat, bf16)],
         [],
         0,
-        keep, near_in, last_a, last_b, done, anywhere=1,
+        keep, near_in, last_a, last_b, block,
     )
     return (
         block_out.reshape(clip_feats.shape),

time: 30.2 us -> 30.1 us (level)
  Pallas kernels: 8.78 us -> 8.15 us
  waiting for transfers between devices: 7.03 us -> 7.61 us
    pallas_call x13, Pallas kernels: 8.78 us -> 8.15 us  [kernel_call(): pl.pallas_call(body, out_shape=tuple((jax.ShapeDtypeStruct(shape, kind) f...]
    ppermute x1, waiting for transfers between devices: 0.01 us -> 0.59 us  [per_device_pair(): last_b = lax.ppermute(sum_b, 'frame', across)]
  transfers between devices with their start and end apart: 11 -> 11, of which waited for: 6 -> 7; matrix products, arithmetic and copies ran while one was open for 0% -> 0% of each run, Pallas kernels for 27% -> 24%
where the time goes in v3:
time: 30.1 us; the launch traced here: 30 us
  starting transfers between devices  13.4 us (45%)
  Pallas kernels  8.15 us (27%)
  waiting for transfers between devices  7.61 us (25%)
  between operations  0.74 us (2%)
    pallas_call x13, Pallas kernels, kernel_call(): pl.pallas_call(body, out_shape=tuple((jax.ShapeDtypeStruct(shape, kind) f...  8.15 us
    ppermute x1, starting transfers between devices, per_device_pair(): last_a = lax.ppermute(sum_a, 'frame', across)  4.51 us
    ppermute x1, starting transfers between devices, per_device_pair(): grad_first = lax.ppermute(grad_flat, both, outward)  3.04 us
    ppermute x1, starting transfers between devices, per_device_pair(): far_in_a = lax.ppermute(far_a, 'frame', beside)  1.76 us
    ppermute x1, waiting for transfers between devices, per_device_pair(): feat_other = lax.ppermute(clip_feats, 'tile', swap)  1.74 us
    ppermute x1, starting transfers between devices, per_device_pair(): near_in = lax.ppermute(near, 'frame', beside)  1.7 us
    ppermute x1, starting transfers between devices, per_device_pair(): last_b = lax.ppermute(sum_b, 'frame', across)  1.55 us
    ppermute x1, waiting for transfers between devices, per_device_pair(): last_a = lax.ppermute(sum_a, 'frame', across)  1.55 us
  transfers between devices with their start and end apart: 11, of which 7 were waited for; matrix products, arithmetic and copies ran while one was open for 0% of the time, Pallas kernels for 24%

profile of v3, /device:TPU:0, one launch (start us, length us, event | category | flops | bytes accessed | tf_op | source)
XLA Modules:
  0.0 30.0 jit_solution(232875608296024915)
XLA Ops:
  0.6 0.0 copy-start.1
  0.6 0.0 copy-start.3
  0.6 3.0 %collective-permute-start.1 = (bf16[512,256]{1,0:T(8,128)(2,1)}, bf16[512,256]{1,0:T(8,128)(2,1)S(1)}, u32[]{:S(2)}, u32[]{:S(2)}) collective-permute-start(bf16[512,256]{1,0:T(8,128)(2,1)} %bitcast.9), channel_id=1, source_target_pairs={{0,2},{2,4},{4,6},{3,1},{5,3},{7,5},{6,7},{1,0},{8,10},{10,12},{12... | collective-permute-start | bytes 786440 | tf_op jit(solution)/shard_map/ppermute | solution.py:352
  3.7 0.0 collective-permute-start.2
  3.7 0.0 collective-permute-start
  3.7 1.7 %collective-permute-done.other = bf16[8,4,16,256]{3,2,1,0:T(8,128)(2,1)S(1)} collective-permute-done((bf16[8,4,16,256]{3,2,1,0:T(8,128)(2,1)}, bf16[8,4,16,256]{3,2,1,0:T(8,128)(2,1)S(1)}, u32[]{:S(2)}, u32[]{:S(2)}) %collective-permute-start) | collective-permute-done | bytes 262176 | tf_op jit(solution)/shard_map/ppermute | solution.py:354
  5.4 0.0 copy-done.1
  5.4 0.0 copy-done.3
  5.4 1.7 %shard_map.68 = (f32[512,256]{1,0:T(8,128)S(1)}, bf16[2,512,256]{2,1,0:T(8,128)(2,1)S(1)}) custom-call(bf16[8,4,16,256]{3,2,1,0:T(8,128)(2,1)S(1)} %copy-done.1, bf16[2304,256]{1,0:T(8,128)(2,1)S(1)} %copy-done.3, bf16[8,4,16,256]{3,2,1,0:T(8,128)(2,1)S(1)} %collective-permute-done.other, f32[8,128]{1,0:T(8,128)S(1)} %shard_map.67._), custom_call_target="tpu_custom_call" | custom-call | flops 1207959552 | bytes 2756608 | tf_op jit(solution)/shard_map/pallas_call | solution.py:129
  7.2 0.0 copy-start
  7.2 0.0 copy-start.2
  7.2 0.4 %collective-permute-start.6 = (bf16[2,512,256]{2,1,0:T(8,128)(2,1)S(1)}, bf16[2,512,256]{2,1,0:T(8,128)(2,1)S(1)}, u32[]{:S(2)}, u32[]{:S(2)}) collective-permute-start(bf16[2,512,256]{2,1,0:T(8,128)(2,1)S(1)} %get-tuple-element.21.act), channel_id=1, source_target_pairs={{2,0},{4,2},{6,4},{1,3},{3,5},{5,7},{7,6},{0,1},{10,8},{12,10},{14... | collective-permute-start | bytes 1572872 | tf_op jit(solution)/shard_map/ppermute | solution.py:364
  7.6 0.5 %shard_map.69._.feats_t = bf16[2,768,512]{2,1,0:T(8,128)(2,1)S(1)} custom-call(bf16[8,4,16,256]{3,2,1,0:T(8,128)(2,1)S(1)} %copy-done.1, bf16[8,4,16,256]{3,2,1,0:T(8,128)(2,1)S(1)} %collective-permute-done.other, f32[512,256]{1,0:T(8,128)S(1)} %get-tuple-element.16._.pre_ref), custom_call_target="tpu_custom_call" | custom-call | bytes 2621440 | tf_op jit(solution)/shard_map/pallas_call | solution.py:129
  8.1 1.5 %collective-permute-done.1.first_in = bf16[512,256]{1,0:T(8,128)(2,1)S(1)} collective-permute-done((bf16[512,256]{1,0:T(8,128)(2,1)}, bf16[512,256]{1,0:T(8,128)(2,1)S(1)}, u32[]{:S(2)}, u32[]{:S(2)}) %collective-permute-start.1) | collective-permute-done | bytes 262176 | tf_op jit(solution)/shard_map/ppermute | solution.py:352
  9.6 0.7 %collective-permute-done.2.second_in = bf16[512,256]{1,0:T(8,128)(2,1)S(1)} collective-permute-done((bf16[512,256]{1,0:T(8,128)(2,1)}, bf16[512,256]{1,0:T(8,128)(2,1)S(1)}, u32[]{:S(2)}, u32[]{:S(2)}) %collective-permute-start.2) | collective-permute-done | bytes 262176 | tf_op jit(solution)/shard_map/ppermute | solution.py:353
  10.3 0.0 copy-done
  10.3 0.0 copy-done.2
  10.3 0.9 %shard_map.70 = bf16[512,256]{1,0:T(8,128)(2,1)S(1)} custom-call(bf16[512,256]{1,0:T(8,128)(2,1)S(1)} %bitcast.11, bf16[512,256]{1,0:T(8,128)(2,1)S(1)} %collective-permute-done.1.first_in, bf16[512,256]{1,0:T(8,128)(2,1)S(1)} %collective-permute-done.2.second_in, bf16[2304,256]{1,0:T(8,128)(2,1)S(1)} %copy-done, ...), custom_call_target="tpu_custom_call" | custom-call | flops 603979776 | bytes 4325376 | tf_op jit(solution)/shard_map/pallas_call | solution.py:129
  11.2 0.1 collective-permute-start.3
  11.3 0.8 %shard_map.71.term = f32[3,768,256]{2,1,0:T(8,128)S(1)} custom-call(bf16[2,768,512]{2,1,0:T(8,128)(2,1)S(1)} %shard_map.69._.feats_t, bf16[8,4,16,256]{3,2,1,0:T(8,128)(2,1)S(1)} %bitcast.6), custom_call_target="tpu_custom_call" | custom-call | flops 603979776 | bytes 4194304 | tf_op jit(solution)/shard_map/pallas_call | solution.py:129
  12.1 0.7 %collective-permute-done.3.other = bf16[8,4,16,256]{3,2,1,0:T(8,128)(2,1)S(1)} collective-permute-done((bf16[8,4,16,256]{3,2,1,0:T(8,128)(2,1)S(1)}, bf16[8,4,16,256]{3,2,1,0:T(8,128)(2,1)S(1)}, u32[]{:S(2)}, u32[]{:S(2)}) %collective-permute-start.3) | collective-permute-done | bytes 262176 | tf_op jit(solution)/shard_map/ppermute | solution.py:380
  12.8 0.9 %shard_map.72 = (bf16[144,256]{1,0:T(8,128)(2,1)S(1)}, bf16[144,256]{1,0:T(8,128)(2,1)S(1)}, f32[288,256]{1,0:T(8,128)S(1)}, bf16[288,256]{1,0:T(8,128)(2,1)S(1)}, f32[288,256]{1,0:T(8,128)S(1)}) custom-call(bf16[2,768,512]{2,1,0:T(8,128)(2,1)S(1)} %shard_map.69._.feats_t, bf16[8,4,16,256]{3,2,1,0:T(8,128)(2,1)S(1)} %collective-permute-done.3.other, ...), custom_call_target="tpu_custom_call" | custom-call | flops 603979776 | bytes 5079040 | tf_op jit(solution)/shard_map/pallas_call | solution.py:129
  13.7 1.8 %collective-permute-start.5 = (bf16[144,256]{1,0:T(8,128)(2,1)S(1)}, bf16[144,256]{1,0:T(8,128)(2,1)S(1)}, u32[]{:S(2)}, u32[]{:S(2)}) collective-permute-start(bf16[144,256]{1,0:T(8,128)(2,1)S(1)} %get-tuple-element.20), channel_id=1, source_target_pairs={{0,2},{2,0},{4,6},{6,4},{1,3},{3,1},{5,7},{7,5},{8,10},{10,8},{12,... | collective-permute-start | bytes 221192 | tf_op jit(solution)/shard_map/ppermute | solution.py:400
  15.4 0.3 %collective-permute-start.8 = (bf16[144,256]{1,0:T(8,128)(2,1)S(1)}, bf16[144,256]{1,0:T(8,128)(2,1)S(1)}, u32[]{:S(2)}, u32[]{:S(2)}) collective-permute-start(bf16[144,256]{1,0:T(8,128)(2,1)S(1)} %get-tuple-element.22), channel_id=1, source_target_pairs={{0,2},{2,0},{4,6},{6,4},{1,3},{3,1},{5,7},{7,5},{8,10},{10,8},{12,... | collective-permute-start | bytes 221192 | tf_op jit(solution)/shard_map/ppermute | solution.py:401
  15.8 1.7 %collective-permute-start.4 = (bf16[288,256]{1,0:T(8,128)(2,1)S(1)}, bf16[288,256]{1,0:T(8,128)(2,1)S(1)}, u32[]{:S(2)}, u32[]{:S(2)}) collective-permute-start(bf16[288,256]{1,0:T(8,128)(2,1)S(1)} %get-tuple-element.18), channel_id=1, source_target_pairs={{0,2},{2,0},{4,6},{6,4},{1,3},{3,1},{5,7},{7,5},{8,10},{10,8},{12,... | collective-permute-start | bytes 442376 | tf_op jit(solution)/shard_map/ppermute | solution.py:402
  17.5 0.9 %collective-permute-done.5.arrived = bf16[144,256]{1,0:T(8,128)(2,1)S(1)} collective-permute-done((bf16[144,256]{1,0:T(8,128)(2,1)S(1)}, bf16[144,256]{1,0:T(8,128)(2,1)S(1)}, u32[]{:S(2)}, u32[]{:S(2)}) %collective-permute-start.5) | collective-permute-done | bytes 73760 | tf_op jit(solution)/shard_map/ppermute | solution.py:400
  18.3 0.0 collective-permute-done.6.rest_0_.arrived
  18.4 4.5 %collective-permute-start.7 = (bf16[144,256]{1,0:T(8,128)(2,1)S(1)}, bf16[144,256]{1,0:T(8,128)(2,1)S(1)}, u32[]{:S(2)}, u32[]{:S(2)}) collective-permute-start(bf16[144,256]{1,0:T(8,128)(2,1)S(1)} %shard_map.73.rest_0_), channel_id=1, source_target_pairs={{0,6},{2,4},{4,2},{6,0},{1,7},{3,5},{5,3},{7,1},{8,14},{10,12},{12... | collective-permute-start | bytes 221192 | tf_op jit(solution)/shard_map/ppermute | solution.py:410
  22.9 0.0 collective-permute-done.8.arrived
  22.9 1.6 %collective-permute-start.9 = (bf16[144,256]{1,0:T(8,128)(2,1)S(1)}, bf16[144,256]{1,0:T(8,128)(2,1)S(1)}, u32[]{:S(2)}, u32[]{:S(2)}) collective-permute-start(bf16[144,256]{1,0:T(8,128)(2,1)S(1)} %shard_map.74._), channel_id=1, source_target_pairs={{0,6},{2,4},{4,2},{6,0},{1,7},{3,5},{5,3},{7,1},{8,14},{10,12},{12... | collective-permute-start | bytes 221192 | tf_op jit(solution)/shard_map/ppermute | solution.py:418
  24.5 0.1 collective-permute-start.10
  24.6 1.5 %shard_map.76 = (bf16[512,256]{1,0:T(8,128)(2,1)}, f32[8,128]{1,0:T(8,128)S(1)}) custom-call(bf16[512,256]{1,0:T(8,128)(2,1)S(1)} %bitcast.12, bf16[8,4,16,256]{3,2,1,0:T(8,128)(2,1)S(1)} %bitcast.7, bf16[8,4,16,256]{3,2,1,0:T(8,128)(2,1)S(1)} %collective-permute-done.3.other, bf16[2304,256]{1,0:T(8,128)(2,1)S(1)} %copy-done.3, bf16[144,256]{1,0:T(8,128)(2,1)S(1)} %shard_map.74._), custom_call_target="tpu_custom_call" | custom-call | flops 603979776 | bytes 2306048 | tf_op jit(solution)/shard_map/pallas_call | solution.py:129
  26.1 0.0 collective-permute-done.4.refs_1_.near
  26.1 1.5 %collective-permute-done.7.refs_0_.last_a = bf16[144,256]{1,0:T(8,128)(2,1)S(1)} collective-permute-done((bf16[144,256]{1,0:T(8,128)(2,1)S(1)}, bf16[144,256]{1,0:T(8,128)(2,1)S(1)}, u32[]{:S(2)}, u32[]{:S(2)}) %collective-permute-start.7) | collective-permute-done | bytes 73760 | tf_op jit(solution)/shard_map/ppermute | solution.py:410
  27.7 0.0 collective-permute-done.10.first_in
  27.7 0.9 %shard_map.78.block = bf16[512,256]{1,0:T(8,128)(2,1)S(1)} custom-call(bf16[512,256]{1,0:T(8,128)(2,1)S(1)} %bitcast.8, bf16[2,512,256]{2,1,0:T(8,128)(2,1)S(1)} %get-tuple-element.21.act, bf16[512,256]{1,0:T(8,128)(2,1)S(1)} %collective-permute-done.10.first_in, bf16[512,256]{1,0:T(8,128)(2,1)S(1)} %get-tuple-element.24.second_in, ...), custom_call_target="tpu_custom_call" | custom-call | flops 603979776 | bytes 2756608 | tf_op jit(solution)/shard_map/pallas_call | solution.py:129
  28.5 0.6 %collective-permute-done.9.last_b = bf16[144,256]{1,0:T(8,128)(2,1)S(1)} collective-permute-done((bf16[144,256]{1,0:T(8,128)(2,1)S(1)}, bf16[144,256]{1,0:T(8,128)(2,1)S(1)}, u32[]{:S(2)}, u32[]{:S(2)}) %collective-permute-start.9) | collective-permute-done | bytes 73760 | tf_op jit(solution)/shard_map/ppermute | solution.py:418
  29.1 0.8 %shard_map.79 = (f32[288,256]{1,0:T(8,128)}, bf16[512,256]{1,0:T(8,128)(2,1)}) custom-call(f32[288,256]{1,0:T(8,128)S(1)} %get-tuple-element.17.keep, bf16[288,256]{1,0:T(8,128)(2,1)S(1)} %collective-permute-done.4.refs_1_.near, bf16[144,256]{1,0:T(8,128)(2,1)S(1)} %collective-permute-done.7.refs_0_.last_a, ...), custom_call_target="tpu_custom_call" | custom-call | bytes 1409024 | tf_op jit(solution)/shard_map/pallas_call | solution.py:129
  (5 shorter events, 0.1 us)
Async XLA Ops:
  0.6 4.8 %copy-start.1 = (bf16[8,4,16,256]{3,2,1,0:T(8,128)(2,1)S(1)}, bf16[8,4,16,256]{3,2,1,0:T(8,128)(2,1)}, u32[]{:S(2)}) copy-start(bf16[8,4,16,256]{3,2,1,0:T(8,128)(2,1)} %own.3) | copy-start | bytes 786436
  0.6 4.8 %copy-start.3 = (bf16[2304,256]{1,0:T(8,128)(2,1)S(1)}, bf16[2304,256]{1,0:T(8,128)(2,1)}, u32[]{:S(2)}) copy-start(bf16[2304,256]{1,0:T(8,128)(2,1)} %weight.6) | copy-start | bytes 3538948
  0.6 9.0 %collective-permute-start.1 = (bf16[512,256]{1,0:T(8,128)(2,1)}, bf16[512,256]{1,0:T(8,128)(2,1)S(1)}, u32[]{:S(2)}, u32[]{:S(2)}) collective-permute-start(bf16[512,256]{1,0:T(8,128)(2,1)} %bitcast.9), channel_id=1, source_target_pairs={{0,2},{2,4},{4,6},{3,1},{5,3},{7,5},{6,7},{1,0},{8,10},{10,12},{12... | collective-permute-start | bytes 786440 | tf_op jit(solution)/shard_map/ppermute | solution.py:352
  3.7 6.6 %collective-permute-start.2 = (bf16[512,256]{1,0:T(8,128)(2,1)}, bf16[512,256]{1,0:T(8,128)(2,1)S(1)}, u32[]{:S(2)}, u32[]{:S(2)}) collective-permute-start(bf16[512,256]{1,0:T(8,128)(2,1)} %bitcast.10), channel_id=1, source_target_pairs={{2,0},{4,2},{6,4},{1,3},{3,5},{5,7},{7,6},{0,1},{10,8},{12,10},{14... | collective-permute-start | bytes 786440 | tf_op jit(solution)/shard_map/ppermute | solution.py:353
  3.7 1.7 %collective-permute-start = (bf16[8,4,16,256]{3,2,1,0:T(8,128)(2,1)}, bf16[8,4,16,256]{3,2,1,0:T(8,128)(2,1)S(1)}, u32[]{:S(2)}, u32[]{:S(2)}) collective-permute-start(bf16[8,4,16,256]{3,2,1,0:T(8,128)(2,1)} %own.3), channel_id=1, source_target_pairs={{0,1},{1,0},{2,3},{3,2},{4,5},{5,4},{6,7},{7,6},{8,9},{9,8},{10,11... | collective-permute-start | bytes 786440 | tf_op jit(solution)/shard_map/ppermute | solution.py:354
  7.2 3.1 %copy-start = (bf16[2304,256]{1,0:T(8,128)(2,1)S(1)}, bf16[2304,256]{1,0:T(8,128)(2,1)}, u32[]{:S(2)}) copy-start(bf16[2304,256]{1,0:T(8,128)(2,1)} %weight.7) | copy-start | bytes 3538948
  7.2 3.1 %copy-start.2 = (bf16[8,4,16,256]{3,2,1,0:T(8,128)(2,1)S(1)}, bf16[8,4,16,256]{3,2,1,0:T(8,128)(2,1)}, u32[]{:S(2)}) copy-start(bf16[8,4,16,256]{3,2,1,0:T(8,128)(2,1)} %param.5) | copy-start | bytes 786436
  7.2 11.2 %collective-permute-start.6 = (bf16[2,512,256]{2,1,0:T(8,128)(2,1)S(1)}, bf16[2,512,256]{2,1,0:T(8,128)(2,1)S(1)}, u32[]{:S(2)}, u32[]{:S(2)}) collective-permute-start(bf16[2,512,256]{2,1,0:T(8,128)(2,1)S(1)} %get-tuple-element.21.act), channel_id=1, source_target_pairs={{2,0},{4,2},{6,4},{1,3},{3,5},{5,7},{7,6},{0,1},{10,8},{12,10},{14... | collective-permute-start | bytes 1572872 | tf_op jit(solution)/shard_map/ppermute | solution.py:364
  11.2 1.6 %collective-permute-start.3 = (bf16[8,4,16,256]{3,2,1,0:T(8,128)(2,1)S(1)}, bf16[8,4,16,256]{3,2,1,0:T(8,128)(2,1)S(1)}, u32[]{:S(2)}, u32[]{:S(2)}) collective-permute-start(bf16[8,4,16,256]{3,2,1,0:T(8,128)(2,1)S(1)} %bitcast.5), channel_id=1, source_target_pairs={{0,1},{1,0},{2,3},{3,2},{4,5},{5,4},{6,7},{7,6},{8,9},{9,8},{10,11... | collective-permute-start | bytes 786440 | tf_op jit(solution)/shard_map/ppermute | solution.py:380
  13.7 4.7 %collective-permute-start.5 = (bf16[144,256]{1,0:T(8,128)(2,1)S(1)}, bf16[144,256]{1,0:T(8,128)(2,1)S(1)}, u32[]{:S(2)}, u32[]{:S(2)}) collective-permute-start(bf16[144,256]{1,0:T(8,128)(2,1)S(1)} %get-tuple-element.20), channel_id=1, source_target_pairs={{0,2},{2,0},{4,6},{6,4},{1,3},{3,1},{5,7},{7,5},{8,10},{10,8},{12,... | collective-permute-start | bytes 221192 | tf_op jit(solution)/shard_map/ppermute | solution.py:400
  15.4 7.4 %collective-permute-start.8 = (bf16[144,256]{1,0:T(8,128)(2,1)S(1)}, bf16[144,256]{1,0:T(8,128)(2,1)S(1)}, u32[]{:S(2)}, u32[]{:S(2)}) collective-permute-start(bf16[144,256]{1,0:T(8,128)(2,1)S(1)} %get-tuple-element.22), channel_id=1, source_target_pairs={{0,2},{2,0},{4,6},{6,4},{1,3},{3,1},{5,7},{7,5},{8,10},{10,8},{12,... | collective-permute-start | bytes 221192 | tf_op jit(solution)/shard_map/ppermute | solution.py:401
  15.8 10.4 %collective-permute-start.4 = (bf16[288,256]{1,0:T(8,128)(2,1)S(1)}, bf16[288,256]{1,0:T(8,128)(2,1)S(1)}, u32[]{:S(2)}, u32[]{:S(2)}) collective-permute-start(bf16[288,256]{1,0:T(8,128)(2,1)S(1)} %get-tuple-element.18), channel_id=1, source_target_pairs={{0,2},{2,0},{4,6},{6,4},{1,3},{3,1},{5,7},{7,5},{8,10},{10,8},{12,... | collective-permute-start | bytes 442376 | tf_op jit(solution)/shard_map/ppermute | solution.py:402
  18.4 9.3 %collective-permute-start.7 = (bf16[144,256]{1,0:T(8,128)(2,1)S(1)}, bf16[144,256]{1,0:T(8,128)(2,1)S(1)}, u32[]{:S(2)}, u32[]{:S(2)}) collective-permute-start(bf16[144,256]{1,0:T(8,128)(2,1)S(1)} %shard_map.73.rest_0_), channel_id=1, source_target_pairs={{0,6},{2,4},{4,2},{6,0},{1,7},{3,5},{5,3},{7,1},{8,14},{10,12},{12... | collective-permute-start | bytes 221192 | tf_op jit(solution)/shard_map/ppermute | solution.py:410
  22.9 6.2 %collective-permute-start.9 = (bf16[144,256]{1,0:T(8,128)(2,1)S(1)}, bf16[144,256]{1,0:T(8,128)(2,1)S(1)}, u32[]{:S(2)}, u32[]{:S(2)}) collective-permute-start(bf16[144,256]{1,0:T(8,128)(2,1)S(1)} %shard_map.74._), channel_id=1, source_target_pairs={{0,6},{2,4},{4,2},{6,0},{1,7},{3,5},{5,3},{7,1},{8,14},{10,12},{12... | collective-permute-start | bytes 221192 | tf_op jit(solution)/shard_map/ppermute | solution.py:418
  24.5 3.2 %collective-permute-start.10 = (bf16[512,256]{1,0:T(8,128)(2,1)S(1)}, bf16[512,256]{1,0:T(8,128)(2,1)S(1)}, u32[]{:S(2)}, u32[]{:S(2)}) collective-permute-start(bf16[512,256]{1,0:T(8,128)(2,1)S(1)} %get-tuple-element.23), channel_id=1, source_target_pairs={{0,1},{1,0},{2,3},{3,2},{4,5},{5,4},{6,7},{7,6},{8,9},{9,8},{10,11... | collective-permute-start | bytes 786440 | tf_op jit(solution)/shard_map/ppermute | solution.py:422

commit v4 on v3

--- a/solution.py
+++ b/solution.py
@@ -196,7 +196,7 @@
     pre_ref[...] = pre_all[lax.axis_index("tile")]
 
 
-def split_kernel(arrived, _, mine_ref, other_ref):
+def split_kernel(arrived, mine_ref, other_ref):
     tile = lax.axis_index("tile")
     mine_ref[...] = arrived[tile]
     other_ref[...] = arrived[1 - tile]
@@ -209,12 +209,28 @@
     sum_ref[...] = (rows + came).astype(sum_ref.dtype)
 
 
-def last_sum_kernel(keep, near, last_a, last_b, block, out_ref, block_ref, *, scale):
-    block_ref[...] = block[...]
-    half = last_a.shape[0]
-    for first, last in ((0, last_a), (half, last_b)):
-        total = keep[first : first + half] + near[first : first + half].astype(jnp.float32)
-        out_ref[first : first + half] = (total + last[...].astype(jnp.float32)) * scale
+def share_rows(keep, near, last, first, scale):
+    count = last.shape[0]
+    total = keep[first : first + count] + near[first : first + count].astype(jnp.float32)
+    return (total + last[...].astype(jnp.float32)) * scale
+
+
+def first_rows_kernel(keep, near, last, block, _, out_hbm, block_hbm, rows, sems, *, scale):
+    block_copy = pltpu.make_async_copy(block, block_hbm, sems.at[0])
+    block_copy.start()
+    rows[...] = share_rows(keep, near, last, 0, scale)
+    copy = pltpu.make_async_copy(rows, out_hbm.at[pl.ds(0, last.shape[0])], sems.at[1])
+    copy.start()
+    block_copy.wait()
+    copy.wait()
+
+
+def other_rows_kernel(keep, near, last, _, out_hbm, rows, sems, *, scale):
+    first = keep.shape[0] - last.shape[0]
+    rows[...] = share_rows(keep, near, last, first, scale)
+    copy = pltpu.make_async_copy(rows, out_hbm.at[pl.ds(first, last.shape[0])], sems.at[0])
+    copy.start()
+    copy.wait()
 
 
 def transpose_kernel(own, other, _, out_ref, image):
@@ -265,7 +281,7 @@
     out_ref[...] = (act_grad * (sig * (1.0 + pre * (1.0 - sig)))).astype(jnp.bfloat16)
 
 
-def temporal_kernel(feats, act, first_in, second_in, weight, _, out_ref, ext):
+def temporal_kernel(feats, act, first_in, second_in, weight, out_ref, ext):
     count, channels = feats.shape
     own = act.at[lax.axis_index("tile")]
     frames = slabs(own, first_in, second_in, ext)
@@ -400,12 +416,17 @@
     far_in_a = lax.ppermute(far_a, "frame", beside)
     far_in_b = lax.ppermute(far_b, "frame", beside)
     near_in = lax.ppermute(near, "frame", beside)
+    act_second, act_pass = kernel_call(
+        split_kernel, [(flat, bf16)] * 2, [], 0, act_in
+    )
+    act_first = lax.ppermute(act_pass, "tile", swap)
+
     (sum_a,) = kernel_call(
         functools.partial(forward_sum_kernel, first=0),
         [(half, bf16)],
         [],
-        4 * product,
-        onward, far_in_a, act_in, anywhere=1,
+        20 * product,
+        onward, far_in_a, act_pass, anywhere=1,
     )
     last_a = lax.ppermute(sum_a, "frame", across)
     (sum_b,) = kernel_call(
@@ -413,14 +434,9 @@
         [(half, bf16)],
         [],
         0,
-        onward, far_in_b, sum_a, anywhere=1,
+        onward, far_in_b, sum_a, act_first, anywhere=2,
     )
     last_b = lax.ppermute(sum_b, "frame", across)
-    act_second, act_pass = kernel_call(
-        split_kernel, [(flat, bf16)] * 2, [], 0, act_in, sum_b, anywhere=1
-    )
-    act_first = lax.ppermute(act_pass, "tile", swap)
-
     input_grad, done = kernel_call(
         input_grad_kernel,
         [(flat, bf16), ((8, 128), f32)],
@@ -428,23 +444,36 @@
         product,
         grad_flat, pre_grad, pre_other, spatial_weight, sum_b, anywhere=1,
     )
-    (arrived,) = kernel_call(
-        order_kernel, [((8, 128), f32)], [], 20 * product, last_a, near_in, done, anywhere=3
-    )
     (block,) = kernel_call(
         temporal_kernel,
         [(flat, bf16)],
         [three],
         product,
-        feat_flat, act, act_first, act_second, temporal_weight, arrived, anywhere=1,
-    )
-    weight_grad, block_out = kernel_call(
-        functools.partial(last_sum_kernel, scale=scale),
-        [(share, f32), (flat, bf16)],
-        [],
-        0,
-        keep, near_in, last_a, last_b, block,
-    )
+        feat_flat, act, act_first, act_second, temporal_weight,
+    )
+    (arrived,) = kernel_call(
+        order_kernel, [((8, 128), f32)], [], 20 * product, last_a, near_in, done, block, anywhere=4
+    )
+    weight_grad, block_out = pl.pallas_call(
+        functools.partial(first_rows_kernel, scale=scale),
+        out_shape=(jax.ShapeDtypeStruct(share, f32), jax.ShapeDtypeStruct(flat, bf16)),
+        in_specs=[pl.BlockSpec(memory_space=pltpu.VMEM)] * 4 + [pl.BlockSpec(memory_space=pl.ANY)],
+        out_specs=(
+            pl.BlockSpec(memory_space=pltpu.HBM),
+            pl.BlockSpec(memory_space=pltpu.HBM),
+        ),
+        scratch_shapes=[pltpu.VMEM(half, f32), pltpu.SemaphoreType.DMA((2,))],
+        compiler_params=pltpu.CompilerParams(vmem_limit_bytes=VMEM_LIMIT),
+    )(keep, near_in, last_a, block, arrived)
+    weight_grad = pl.pallas_call(
+        functools.partial(other_rows_kernel, scale=scale),
+        out_shape=jax.ShapeDtypeStruct(share, f32),
+        in_specs=[pl.BlockSpec(memory_space=pltpu.VMEM)] * 3 + [pl.BlockSpec(memory_space=pltpu.HBM)],
+        out_specs=pl.BlockSpec(memory_space=pltpu.HBM),
+        scratch_shapes=[pltpu.VMEM(half, f32), pltpu.SemaphoreType.DMA((1,))],
+        input_output_aliases={3: 0},
+        compiler_params=pltpu.CompilerParams(vmem_limit_bytes=VMEM_LIMIT),
+    )(keep, near_in, last_b, weight_grad)
     return (
         block_out.reshape(clip_feats.shape),
         input_grad.reshape(clip_feats.shape),

time: 30.1 us -> 30 us (level)
  waiting for transfers between devices: 7.61 us -> 6.83 us
  Pallas kernels: 8.15 us -> 8.77 us
    pallas_call x0 -> x2, Pallas kernels: none -> 1.46 us  [the longest x1 0.76 us: per_device_pair(): pl.pallas_call(functools.partial(first_rows_kernel, scale=scale), out_sha...]
    pallas_call x13 -> x12, Pallas kernels: 8.15 us -> 7.31 us  [kernel_call(): pl.pallas_call(body, out_shape=tuple((jax.ShapeDtypeStruct(shape, kind) f...]
    ppermute x1, waiting for transfers between devices: 1.55 us -> 0.8 us  [per_device_pair(): last_a = lax.ppermute(sum_a, 'frame', across)]
  transfers between devices with their start and end apart: 11 -> 11, of which waited for: 7 -> 7; matrix products, arithmetic and copies ran while one was open for 0% -> 0% of each run, Pallas kernels for 24% -> 27%
where the time goes in v4:
time: 30 us; the launch traced here: 29.8 us
  starting transfers between devices  13.4 us (45%)
  Pallas kernels  8.77 us (29%)
  waiting for transfers between devices  6.83 us (23%)
  between operations  0.76 us (3%)
    pallas_call x12, Pallas kernels, kernel_call(): pl.pallas_call(body, out_shape=tuple((jax.ShapeDtypeStruct(shape, kind) f...  7.31 us
    ppermute x1, starting transfers between devices, per_device_pair(): last_a = lax.ppermute(sum_a, 'frame', across)  4.51 us
    ppermute x1, starting transfers between devices, per_device_pair(): grad_first = lax.ppermute(grad_flat, both, outward)  3.04 us
    ppermute x1, starting transfers between devices, per_device_pair(): far_in_a = lax.ppermute(far_a, 'frame', beside)  1.76 us
    ppermute x1, waiting for transfers between devices, per_device_pair(): feat_other = lax.ppermute(clip_feats, 'tile', swap)  1.74 us
    ppermute x1, starting transfers between devices, per_device_pair(): near_in = lax.ppermute(near, 'frame', beside)  1.7 us
    ppermute x1, starting transfers between devices, per_device_pair(): last_b = lax.ppermute(sum_b, 'frame', across)  1.56 us
    ppermute x1, waiting for transfers between devices, per_device_pair(): grad_first = lax.ppermute(grad_flat, both, outward)  1.47 us
  transfers between devices with their start and end apart: 11, of which 7 were waited for; matrix products, arithmetic and copies ran while one was open for 0% of the time, Pallas kernels for 27%

profile of v4, /device:TPU:0, one launch (start us, length us, event | category | flops | bytes accessed | tf_op | source)
XLA Modules:
  0.0 29.8 jit_solution(11406167078997332815)
XLA Ops:
  0.6 0.0 copy-start.1
  0.6 0.0 copy-start.3
  0.6 3.0 %collective-permute-start.1 = (bf16[512,256]{1,0:T(8,128)(2,1)}, bf16[512,256]{1,0:T(8,128)(2,1)S(1)}, u32[]{:S(2)}, u32[]{:S(2)}) collective-permute-start(bf16[512,256]{1,0:T(8,128)(2,1)} %bitcast.9), channel_id=1, source_target_pairs={{0,2},{2,4},{4,6},{3,1},{5,3},{7,5},{6,7},{1,0},{8,10},{10,12},{12... | collective-permute-start | bytes 786440 | tf_op jit(solution)/shard_map/ppermute | solution.py:368
  3.7 0.0 collective-permute-start.2
  3.7 0.0 collective-permute-start
  3.7 1.7 %collective-permute-done.other = bf16[8,4,16,256]{3,2,1,0:T(8,128)(2,1)S(1)} collective-permute-done((bf16[8,4,16,256]{3,2,1,0:T(8,128)(2,1)}, bf16[8,4,16,256]{3,2,1,0:T(8,128)(2,1)S(1)}, u32[]{:S(2)}, u32[]{:S(2)}) %collective-permute-start) | collective-permute-done | bytes 262176 | tf_op jit(solution)/shard_map/ppermute | solution.py:370
  5.4 0.0 copy-done.1
  5.4 0.0 copy-done.3
  5.4 1.7 %shard_map.68 = (f32[512,256]{1,0:T(8,128)S(1)}, bf16[2,512,256]{2,1,0:T(8,128)(2,1)S(1)}) custom-call(bf16[8,4,16,256]{3,2,1,0:T(8,128)(2,1)S(1)} %copy-done.1, bf16[2304,256]{1,0:T(8,128)(2,1)S(1)} %copy-done.3, bf16[8,4,16,256]{3,2,1,0:T(8,128)(2,1)S(1)} %collective-permute-done.other, f32[8,128]{1,0:T(8,128)S(1)} %shard_map.67._), custom_call_target="tpu_custom_call" | custom-call | flops 1207959552 | bytes 2756608 | tf_op jit(solution)/shard_map/pallas_call | solution.py:129
  7.2 0.0 copy-start
  7.2 0.0 copy-start.2
  7.2 0.4 %collective-permute-start.6 = (bf16[2,512,256]{2,1,0:T(8,128)(2,1)S(1)}, bf16[2,512,256]{2,1,0:T(8,128)(2,1)S(1)}, u32[]{:S(2)}, u32[]{:S(2)}) collective-permute-start(bf16[2,512,256]{2,1,0:T(8,128)(2,1)S(1)} %get-tuple-element.21.act), channel_id=1, source_target_pairs={{2,0},{4,2},{6,4},{1,3},{3,5},{5,7},{7,6},{0,1},{10,8},{12,10},{14... | collective-permute-start | bytes 1572872 | tf_op jit(solution)/shard_map/ppermute | solution.py:380
  7.6 0.5 %shard_map.69._.feats_t = bf16[2,768,512]{2,1,0:T(8,128)(2,1)S(1)} custom-call(bf16[8,4,16,256]{3,2,1,0:T(8,128)(2,1)S(1)} %copy-done.1, bf16[8,4,16,256]{3,2,1,0:T(8,128)(2,1)S(1)} %collective-permute-done.other, f32[512,256]{1,0:T(8,128)S(1)} %get-tuple-element.16._.pre_ref), custom_call_target="tpu_custom_call" | custom-call | bytes 2621440 | tf_op jit(solution)/shard_map/pallas_call | solution.py:129
  8.1 1.5 %collective-permute-done.1.first_in = bf16[512,256]{1,0:T(8,128)(2,1)S(1)} collective-permute-done((bf16[512,256]{1,0:T(8,128)(2,1)}, bf16[512,256]{1,0:T(8,128)(2,1)S(1)}, u32[]{:S(2)}, u32[]{:S(2)}) %collective-permute-start.1) | collective-permute-done | bytes 262176 | tf_op jit(solution)/shard_map/ppermute | solution.py:368
  9.6 0.7 %collective-permute-done.2.second_in = bf16[512,256]{1,0:T(8,128)(2,1)S(1)} collective-permute-done((bf16[512,256]{1,0:T(8,128)(2,1)}, bf16[512,256]{1,0:T(8,128)(2,1)S(1)}, u32[]{:S(2)}, u32[]{:S(2)}) %collective-permute-start.2) | collective-permute-done | bytes 262176 | tf_op jit(solution)/shard_map/ppermute | solution.py:369
  10.3 0.0 copy-done
  10.3 0.0 copy-done.2
  10.3 0.9 %shard_map.70 = bf16[512,256]{1,0:T(8,128)(2,1)S(1)} custom-call(bf16[512,256]{1,0:T(8,128)(2,1)S(1)} %bitcast.11, bf16[512,256]{1,0:T(8,128)(2,1)S(1)} %collective-permute-done.1.first_in, bf16[512,256]{1,0:T(8,128)(2,1)S(1)} %collective-permute-done.2.second_in, bf16[2304,256]{1,0:T(8,128)(2,1)S(1)} %copy-done, ...), custom_call_target="tpu_custom_call" | custom-call | flops 603979776 | bytes 4325376 | tf_op jit(solution)/shard_map/pallas_call | solution.py:129
  11.2 0.1 collective-permute-start.3
  11.3 0.8 %shard_map.71.term = f32[3,768,256]{2,1,0:T(8,128)S(1)} custom-call(bf16[2,768,512]{2,1,0:T(8,128)(2,1)S(1)} %shard_map.69._.feats_t, bf16[8,4,16,256]{3,2,1,0:T(8,128)(2,1)S(1)} %bitcast.6), custom_call_target="tpu_custom_call" | custom-call | flops 603979776 | bytes 4194304 | tf_op jit(solution)/shard_map/pallas_call | solution.py:129
  12.1 0.7 %collective-permute-done.3.other = bf16[8,4,16,256]{3,2,1,0:T(8,128)(2,1)S(1)} collective-permute-done((bf16[8,4,16,256]{3,2,1,0:T(8,128)(2,1)S(1)}, bf16[8,4,16,256]{3,2,1,0:T(8,128)(2,1)S(1)}, u32[]{:S(2)}, u32[]{:S(2)}) %collective-permute-start.3) | collective-permute-done | bytes 262176 | tf_op jit(solution)/shard_map/ppermute | solution.py:396
  12.8 0.9 %shard_map.72 = (bf16[144,256]{1,0:T(8,128)(2,1)S(1)}, bf16[144,256]{1,0:T(8,128)(2,1)S(1)}, f32[288,256]{1,0:T(8,128)S(1)}, bf16[288,256]{1,0:T(8,128)(2,1)S(1)}, f32[288,256]{1,0:T(8,128)S(1)}) custom-call(bf16[2,768,512]{2,1,0:T(8,128)(2,1)S(1)} %shard_map.69._.feats_t, bf16[8,4,16,256]{3,2,1,0:T(8,128)(2,1)S(1)} %collective-permute-done.3.other, ...), custom_call_target="tpu_custom_call" | custom-call | flops 603979776 | bytes 5079040 | tf_op jit(solution)/shard_map/pallas_call | solution.py:129
  13.7 1.8 %collective-permute-start.5 = (bf16[144,256]{1,0:T(8,128)(2,1)S(1)}, bf16[144,256]{1,0:T(8,128)(2,1)S(1)}, u32[]{:S(2)}, u32[]{:S(2)}) collective-permute-start(bf16[144,256]{1,0:T(8,128)(2,1)S(1)} %get-tuple-element.20), channel_id=1, source_target_pairs={{0,2},{2,0},{4,6},{6,4},{1,3},{3,1},{5,7},{7,5},{8,10},{10,8},{12,... | collective-permute-start | bytes 221192 | tf_op jit(solution)/shard_map/ppermute | solution.py:416
  15.4 0.3 %collective-permute-start.9 = (bf16[144,256]{1,0:T(8,128)(2,1)S(1)}, bf16[144,256]{1,0:T(8,128)(2,1)S(1)}, u32[]{:S(2)}, u32[]{:S(2)}) collective-permute-start(bf16[144,256]{1,0:T(8,128)(2,1)S(1)} %get-tuple-element.24), channel_id=1, source_target_pairs={{0,2},{2,0},{4,6},{6,4},{1,3},{3,1},{5,7},{7,5},{8,10},{10,8},{12,... | collective-permute-start | bytes 221192 | tf_op jit(solution)/shard_map/ppermute | solution.py:417
  15.8 1.7 %collective-permute-start.4 = (bf16[288,256]{1,0:T(8,128)(2,1)S(1)}, bf16[288,256]{1,0:T(8,128)(2,1)S(1)}, u32[]{:S(2)}, u32[]{:S(2)}) collective-permute-start(bf16[288,256]{1,0:T(8,128)(2,1)S(1)} %get-tuple-element.18), channel_id=1, source_target_pairs={{0,2},{2,0},{4,6},{6,4},{1,3},{3,1},{5,7},{7,5},{8,10},{10,8},{12,... | collective-permute-start | bytes 442376 | tf_op jit(solution)/shard_map/ppermute | solution.py:418
  17.5 0.0 collective-permute-done.6.arrived
  17.5 0.1 collective-permute-start.8
  17.6 0.8 %collective-permute-done.5.arrived = bf16[144,256]{1,0:T(8,128)(2,1)S(1)} collective-permute-done((bf16[144,256]{1,0:T(8,128)(2,1)S(1)}, bf16[144,256]{1,0:T(8,128)(2,1)S(1)}, u32[]{:S(2)}, u32[]{:S(2)}) %collective-permute-start.5) | collective-permute-done | bytes 73760 | tf_op jit(solution)/shard_map/ppermute | solution.py:416
  18.4 4.5 %collective-permute-start.7 = (bf16[144,256]{1,0:T(8,128)(2,1)S(1)}, bf16[144,256]{1,0:T(8,128)(2,1)S(1)}, u32[]{:S(2)}, u32[]{:S(2)}) collective-permute-start(bf16[144,256]{1,0:T(8,128)(2,1)S(1)} %shard_map.74.rest_0_), channel_id=1, source_target_pairs={{0,6},{2,4},{4,2},{6,0},{1,7},{3,5},{5,3},{7,1},{8,14},{10,12},{12... | collective-permute-start | bytes 221192 | tf_op jit(solution)/shard_map/ppermute | solution.py:431
  22.9 0.0 collective-permute-done.9.arrived
  22.9 0.0 collective-permute-done.8.first_in.rest_1_
  22.9 1.6 %collective-permute-start.10 = (bf16[144,256]{1,0:T(8,128)(2,1)S(1)}, bf16[144,256]{1,0:T(8,128)(2,1)S(1)}, u32[]{:S(2)}, u32[]{:S(2)}) collective-permute-start(bf16[144,256]{1,0:T(8,128)(2,1)S(1)} %shard_map.76._), channel_id=1, source_target_pairs={{0,6},{2,4},{4,2},{6,0},{1,7},{3,5},{5,3},{7,1},{8,14},{10,12},{12... | collective-permute-start | bytes 221192 | tf_op jit(solution)/shard_map/ppermute | solution.py:439
  24.5 1.5 %shard_map.77 = (bf16[512,256]{1,0:T(8,128)(2,1)}, f32[8,128]{1,0:T(8,128)S(1)}) custom-call(bf16[512,256]{1,0:T(8,128)(2,1)S(1)} %bitcast.12, bf16[8,4,16,256]{3,2,1,0:T(8,128)(2,1)S(1)} %bitcast.7, bf16[8,4,16,256]{3,2,1,0:T(8,128)(2,1)S(1)} %collective-permute-done.3.other, bf16[2304,256]{1,0:T(8,128)(2,1)S(1)} %copy-done.3, bf16[144,256]{1,0:T(8,128)(2,1)S(1)} %shard_map.76._), custom_call_target="tpu_custom_call" | custom-call | flops 603979776 | bytes 2306048 | tf_op jit(solution)/shard_map/pallas_call | solution.py:129
  26.0 0.9 %shard_map.75.refs_3_.block = bf16[512,256]{1,0:T(8,128)(2,1)S(1)} custom-call(bf16[512,256]{1,0:T(8,128)(2,1)S(1)} %bitcast.8, bf16[2,512,256]{2,1,0:T(8,128)(2,1)S(1)} %get-tuple-element.21.act, bf16[512,256]{1,0:T(8,128)(2,1)S(1)} %collective-permute-done.8.first_in.rest_1_, bf16[512,256]{1,0:T(8,128)(2,1)S(1)} %get-tuple-element.23.second_in, ...), custom_call_target="tpu_custom_call" | custom-call | flops 603979776 | bytes 2752512 | tf_op jit(solution)/shard_map/pallas_call | solution.py:129
  26.9 0.0 collective-permute-done.4.refs_1_.near
  26.9 0.8 %collective-permute-done.7.refs_0_.last = bf16[144,256]{1,0:T(8,128)(2,1)S(1)} collective-permute-done((bf16[144,256]{1,0:T(8,128)(2,1)S(1)}, bf16[144,256]{1,0:T(8,128)(2,1)S(1)}, u32[]{:S(2)}, u32[]{:S(2)}) %collective-permute-start.7) | collective-permute-done | bytes 73760 | tf_op jit(solution)/shard_map/ppermute | solution.py:431
  27.7 0.8 %shard_map.79 = (f32[288,256]{1,0:T(8,128)}, bf16[512,256]{1,0:T(8,128)(2,1)}) custom-call(f32[288,256]{1,0:T(8,128)S(1)} %get-tuple-element.17.keep, bf16[288,256]{1,0:T(8,128)(2,1)S(1)} %collective-permute-done.4.refs_1_.near, bf16[144,256]{1,0:T(8,128)(2,1)S(1)} %collective-permute-done.7.refs_0_.last, bf16[512,256]{1,0:T(8,128)(2,1)S(1)} %shard_map.75.refs_3_.block, ...), custom_call_target="tpu_custom_call" | custom-call | tf_op jit(solution)/shard_map/pallas_call | solution.py:457
  28.4 0.7 %collective-permute-done.10.last = bf16[144,256]{1,0:T(8,128)(2,1)S(1)} collective-permute-done((bf16[144,256]{1,0:T(8,128)(2,1)S(1)}, bf16[144,256]{1,0:T(8,128)(2,1)S(1)}, u32[]{:S(2)}, u32[]{:S(2)}) %collective-permute-start.10) | collective-permute-done | bytes 73760 | tf_op jit(solution)/shard_map/ppermute | solution.py:439
  29.1 0.7 %shard_map.80 = f32[288,256]{1,0:T(8,128)} custom-call(f32[288,256]{1,0:T(8,128)S(1)} %get-tuple-element.17.keep, bf16[288,256]{1,0:T(8,128)(2,1)S(1)} %collective-permute-done.4.refs_1_.near, bf16[144,256]{1,0:T(8,128)(2,1)S(1)} %collective-permute-done.10.last, f32[288,256]{1,0:T(8,128)} %get-tuple-element.28._), custom_call_target="tpu_custom_call", output_to_operand_aliasing={{}: (3, {})} | custom-call | tf_op jit(solution)/shard_map/pallas_call | solution.py:468
  (5 shorter events, 0.1 us)
Async XLA Ops:
  0.6 4.8 %copy-start.1 = (bf16[8,4,16,256]{3,2,1,0:T(8,128)(2,1)S(1)}, bf16[8,4,16,256]{3,2,1,0:T(8,128)(2,1)}, u32[]{:S(2)}) copy-start(bf16[8,4,16,256]{3,2,1,0:T(8,128)(2,1)} %own.3) | copy-start | bytes 786436
  0.6 4.8 %copy-start.3 = (bf16[2304,256]{1,0:T(8,128)(2,1)S(1)}, bf16[2304,256]{1,0:T(8,128)(2,1)}, u32[]{:S(2)}) copy-start(bf16[2304,256]{1,0:T(8,128)(2,1)} %weight.7) | copy-start | bytes 3538948
  0.6 9.0 %collective-permute-start.1 = (bf16[512,256]{1,0:T(8,128)(2,1)}, bf16[512,256]{1,0:T(8,128)(2,1)S(1)}, u32[]{:S(2)}, u32[]{:S(2)}) collective-permute-start(bf16[512,256]{1,0:T(8,128)(2,1)} %bitcast.9), channel_id=1, source_target_pairs={{0,2},{2,4},{4,6},{3,1},{5,3},{7,5},{6,7},{1,0},{8,10},{10,12},{12... | collective-permute-start | bytes 786440 | tf_op jit(solution)/shard_map/ppermute | solution.py:368
  3.7 6.6 %collective-permute-start.2 = (bf16[512,256]{1,0:T(8,128)(2,1)}, bf16[512,256]{1,0:T(8,128)(2,1)S(1)}, u32[]{:S(2)}, u32[]{:S(2)}) collective-permute-start(bf16[512,256]{1,0:T(8,128)(2,1)} %bitcast.10), channel_id=1, source_target_pairs={{2,0},{4,2},{6,4},{1,3},{3,5},{5,7},{7,6},{0,1},{10,8},{12,10},{14... | collective-permute-start | bytes 786440 | tf_op jit(solution)/shard_map/ppermute | solution.py:369
  3.7 1.7 %collective-permute-start = (bf16[8,4,16,256]{3,2,1,0:T(8,128)(2,1)}, bf16[8,4,16,256]{3,2,1,0:T(8,128)(2,1)S(1)}, u32[]{:S(2)}, u32[]{:S(2)}) collective-permute-start(bf16[8,4,16,256]{3,2,1,0:T(8,128)(2,1)} %own.3), channel_id=1, source_target_pairs={{0,1},{1,0},{2,3},{3,2},{4,5},{5,4},{6,7},{7,6},{8,9},{9,8},{10,11... | collective-permute-start | bytes 786440 | tf_op jit(solution)/shard_map/ppermute | solution.py:370
  7.2 3.1 %copy-start = (bf16[2304,256]{1,0:T(8,128)(2,1)S(1)}, bf16[2304,256]{1,0:T(8,128)(2,1)}, u32[]{:S(2)}) copy-start(bf16[2304,256]{1,0:T(8,128)(2,1)} %weight.6) | copy-start | bytes 3538948
  7.2 3.1 %copy-start.2 = (bf16[8,4,16,256]{3,2,1,0:T(8,128)(2,1)S(1)}, bf16[8,4,16,256]{3,2,1,0:T(8,128)(2,1)}, u32[]{:S(2)}) copy-start(bf16[8,4,16,256]{3,2,1,0:T(8,128)(2,1)} %param.5) | copy-start | bytes 786436
  7.2 10.3 %collective-permute-start.6 = (bf16[2,512,256]{2,1,0:T(8,128)(2,1)S(1)}, bf16[2,512,256]{2,1,0:T(8,128)(2,1)S(1)}, u32[]{:S(2)}, u32[]{:S(2)}) collective-permute-start(bf16[2,512,256]{2,1,0:T(8,128)(2,1)S(1)} %get-tuple-element.21.act), channel_id=1, source_target_pairs={{2,0},{4,2},{6,4},{1,3},{3,5},{5,7},{7,6},{0,1},{10,8},{12,10},{14... | collective-permute-start | bytes 1572872 | tf_op jit(solution)/shard_map/ppermute | solution.py:380
  11.2 1.6 %collective-permute-start.3 = (bf16[8,4,16,256]{3,2,1,0:T(8,128)(2,1)S(1)}, bf16[8,4,16,256]{3,2,1,0:T(8,128)(2,1)S(1)}, u32[]{:S(2)}, u32[]{:S(2)}) collective-permute-start(bf16[8,4,16,256]{3,2,1,0:T(8,128)(2,1)S(1)} %bitcast.5), channel_id=1, source_target_pairs={{0,1},{1,0},{2,3},{3,2},{4,5},{5,4},{6,7},{7,6},{8,9},{9,8},{10,11... | collective-permute-start | bytes 786440 | tf_op jit(solution)/shard_map/ppermute | solution.py:396
  13.7 4.7 %collective-permute-start.5 = (bf16[144,256]{1,0:T(8,128)(2,1)S(1)}, bf16[144,256]{1,0:T(8,128)(2,1)S(1)}, u32[]{:S(2)}, u32[]{:S(2)}) collective-permute-start(bf16[144,256]{1,0:T(8,128)(2,1)S(1)} %get-tuple-element.20), channel_id=1, source_target_pairs={{0,2},{2,0},{4,6},{6,4},{1,3},{3,1},{5,7},{7,5},{8,10},{10,8},{12,... | collective-permute-start | bytes 221192 | tf_op jit(solution)/shard_map/ppermute | solution.py:416
  15.4 7.4 %collective-permute-start.9 = (bf16[144,256]{1,0:T(8,128)(2,1)S(1)}, bf16[144,256]{1,0:T(8,128)(2,1)S(1)}, u32[]{:S(2)}, u32[]{:S(2)}) collective-permute-start(bf16[144,256]{1,0:T(8,128)(2,1)S(1)} %get-tuple-element.24), channel_id=1, source_target_pairs={{0,2},{2,0},{4,6},{6,4},{1,3},{3,1},{5,7},{7,5},{8,10},{10,8},{12,... | collective-permute-start | bytes 221192 | tf_op jit(solution)/shard_map/ppermute | solution.py:417
  15.8 11.1 %collective-permute-start.4 = (bf16[288,256]{1,0:T(8,128)(2,1)S(1)}, bf16[288,256]{1,0:T(8,128)(2,1)S(1)}, u32[]{:S(2)}, u32[]{:S(2)}) collective-permute-start(bf16[288,256]{1,0:T(8,128)(2,1)S(1)} %get-tuple-element.18), channel_id=1, source_target_pairs={{0,2},{2,0},{4,6},{6,4},{1,3},{3,1},{5,7},{7,5},{8,10},{10,8},{12,... | collective-permute-start | bytes 442376 | tf_op jit(solution)/shard_map/ppermute | solution.py:418
  17.5 5.4 %collective-permute-start.8 = (bf16[512,256]{1,0:T(8,128)(2,1)S(1)}, bf16[512,256]{1,0:T(8,128)(2,1)S(1)}, u32[]{:S(2)}, u32[]{:S(2)}) collective-permute-start(bf16[512,256]{1,0:T(8,128)(2,1)S(1)} %get-tuple-element.22.rest_0_), channel_id=1, source_target_pairs={{0,1},{1,0},{2,3},{3,2},{4,5},{5,4},{6,7},{7,6},{8,9},{9,8},{10,11... | collective-permute-start | bytes 786440 | tf_op jit(solution)/shard_map/ppermute | solution.py:422
  18.4 9.3 %collective-permute-start.7 = (bf16[144,256]{1,0:T(8,128)(2,1)S(1)}, bf16[144,256]{1,0:T(8,128)(2,1)S(1)}, u32[]{:S(2)}, u32[]{:S(2)}) collective-permute-start(bf16[144,256]{1,0:T(8,128)(2,1)S(1)} %shard_map.74.rest_0_), channel_id=1, source_target_pairs={{0,6},{2,4},{4,2},{6,0},{1,7},{3,5},{5,3},{7,1},{8,14},{10,12},{12... | collective-permute-start | bytes 221192 | tf_op jit(solution)/shard_map/ppermute | solution.py:431
  22.9 6.2 %collective-permute-start.10 = (bf16[144,256]{1,0:T(8,128)(2,1)S(1)}, bf16[144,256]{1,0:T(8,128)(2,1)S(1)}, u32[]{:S(2)}, u32[]{:S(2)}) collective-permute-start(bf16[144,256]{1,0:T(8,128)(2,1)S(1)} %shard_map.76._), channel_id=1, source_target_pairs={{0,6},{2,4},{4,2},{6,0},{1,7},{3,5},{5,3},{7,1},{8,14},{10,12},{12... | collective-permute-start | bytes 221192 | tf_op jit(solution)/shard_map/ppermute | solution.py:439

commit v5 on v4

--- a/solution.py
+++ b/solution.py
@@ -313,7 +313,7 @@
             tap = 3 * r + s
             total[tap * channels : (tap + 1) * channels] = both[r * channels : (r + 1) * channels]
     share = keep_ref.shape[0]
-    half = share // 2
+    half = far_a_ref.shape[0]
     for distance, skip, ref in (
         (2, 0, far_a_ref),
         (2, half, far_b_ref),
@@ -403,10 +403,11 @@
         product,
         feats_t, pre_grad,
     )
-    half = (share[0] // 2, channels)
+    part_a = (share[0] * 2 // 3, channels)
+    part_b = (share[0] - part_a[0], channels)
     far_a, far_b, onward, near, keep = kernel_call(
         kernel_grad_kernel,
-        [(half, bf16), (half, bf16), (share, f32), (share, bf16), (share, f32)],
+        [(part_a, bf16), (part_b, bf16), (share, f32), (share, bf16), (share, f32)],
         [((9 * channels, channels), f32)],
         product,
         feats_t, pre_other, term,
@@ -423,15 +424,15 @@
 
     (sum_a,) = kernel_call(
         functools.partial(forward_sum_kernel, first=0),
-        [(half, bf16)],
+        [(part_a, bf16)],
         [],
         20 * product,
         onward, far_in_a, act_pass, anywhere=1,
     )
     last_a = lax.ppermute(sum_a, "frame", across)
     (sum_b,) = kernel_call(
-        functools.partial(forward_sum_kernel, first=half[0]),
-        [(half, bf16)],
+        functools.partial(forward_sum_kernel, first=part_a[0]),
+        [(part_b, bf16)],
         [],
         0,
         onward, far_in_b, sum_a, act_first, anywhere=2,
@@ -462,7 +463,7 @@
             pl.BlockSpec(memory_space=pltpu.HBM),
             pl.BlockSpec(memory_space=pltpu.HBM),
         ),
-        scratch_shapes=[pltpu.VMEM(half, f32), pltpu.SemaphoreType.DMA((2,))],
+        scratch_shapes=[pltpu.VMEM(part_a, f32), pltpu.SemaphoreType.DMA((2,))],
         compiler_params=pltpu.CompilerParams(vmem_limit_bytes=VMEM_LIMIT),
     )(keep, near_in, last_a, block, arrived)
     weight_grad = pl.pallas_call(
@@ -470,7 +471,7 @@
         out_shape=jax.ShapeDtypeStruct(share, f32),
         in_specs=[pl.BlockSpec(memory_space=pltpu.VMEM)] * 3 + [pl.BlockSpec(memory_space=pltpu.HBM)],
         out_specs=pl.BlockSpec(memory_space=pltpu.HBM),
-        scratch_shapes=[pltpu.VMEM(half, f32), pltpu.SemaphoreType.DMA((1,))],
+        scratch_shapes=[pltpu.VMEM(part_b, f32), pltpu.SemaphoreType.DMA((1,))],
         input_output_aliases={3: 0},
         compiler_params=pltpu.CompilerParams(vmem_limit_bytes=VMEM_LIMIT),
     )(keep, near_in, last_b, weight_grad)

time: 30 us -> 30.2 us (level)
  waiting for transfers between devices: 6.83 us -> 8.05 us
  starting transfers between devices: 13.4 us -> 12.5 us
    ppermute x1, waiting for transfers between devices: 0.76 us -> 1.73 us  [per_device_pair(): far_in_a = lax.ppermute(far_a, 'frame', beside)]
    ppermute x1, starting transfers between devices: 1.56 us -> 1.02 us  [per_device_pair(): last_b = lax.ppermute(sum_b, 'frame', across)]
    ppermute x1, starting transfers between devices: 4.51 us -> 4.07 us  [per_device_pair(): last_a = lax.ppermute(sum_a, 'frame', across)]
where the time goes in v5:
time: 30.2 us; the launch traced here: 30.1 us
  starting transfers between devices  12.5 us (41%)
  Pallas kernels  8.75 us (29%)
  waiting for transfers between devices  8.05 us (27%)
  between operations  0.76 us (3%)
    pallas_call x12, Pallas kernels, kernel_call(): pl.pallas_call(body, out_shape=tuple((jax.ShapeDtypeStruct(shape, kind) f...  7.3 us
    ppermute x1, starting transfers between devices, per_device_pair(): last_a = lax.ppermute(sum_a, 'frame', across)  4.07 us
    ppermute x1, starting transfers between devices, per_device_pair(): grad_first = lax.ppermute(grad_flat, both, outward)  3.04 us
    ppermute x1, starting transfers between devices, per_device_pair(): far_in_a = lax.ppermute(far_a, 'frame', beside)  1.76 us
    ppermute x1, waiting for transfers between devices, per_device_pair(): feat_other = lax.ppermute(clip_feats, 'tile', swap)  1.74 us
    ppermute x1, waiting for transfers between devices, per_device_pair(): far_in_a = lax.ppermute(far_a, 'frame', beside)  1.73 us
    ppermute x1, starting transfers between devices, per_device_pair(): near_in = lax.ppermute(near, 'frame', beside)  1.7 us
    ppermute x1, waiting for transfers between devices, per_device_pair(): grad_first = lax.ppermute(grad_flat, both, outward)  1.47 us
  transfers between devices with their start and end apart: 11, of which 7 were waited for; matrix products, arithmetic and copies ran while one was open for 0% of the time, Pallas kernels for 27%

profile of v5, /device:TPU:0, one launch (start us, length us, event | category | flops | bytes accessed | tf_op | source)
XLA Modules:
  0.0 30.1 jit_solution(1916548263966669952)
XLA Ops:
  0.6 0.0 copy-start.1
  0.6 0.0 copy-start.3
  0.6 3.0 %collective-permute-start.1 = (bf16[512,256]{1,0:T(8,128)(2,1)}, bf16[512,256]{1,0:T(8,128)(2,1)S(1)}, u32[]{:S(2)}, u32[]{:S(2)}) collective-permute-start(bf16[512,256]{1,0:T(8,128)(2,1)} %bitcast.9), channel_id=1, source_target_pairs={{0,2},{2,4},{4,6},{3,1},{5,3},{7,5},{6,7},{1,0},{8,10},{10,12},{12... | collective-permute-start | bytes 786440 | tf_op jit(solution)/shard_map/ppermute | solution.py:368
  3.7 0.0 collective-permute-start.2
  3.7 0.0 collective-permute-start
  3.7 1.7 %collective-permute-done.other = bf16[8,4,16,256]{3,2,1,0:T(8,128)(2,1)S(1)} collective-permute-done((bf16[8,4,16,256]{3,2,1,0:T(8,128)(2,1)}, bf16[8,4,16,256]{3,2,1,0:T(8,128)(2,1)S(1)}, u32[]{:S(2)}, u32[]{:S(2)}) %collective-permute-start) | collective-permute-done | bytes 262176 | tf_op jit(solution)/shard_map/ppermute | solution.py:370
  5.4 0.0 copy-done.1
  5.4 0.0 copy-done.3
  5.4 1.7 %shard_map.68 = (f32[512,256]{1,0:T(8,128)S(1)}, bf16[2,512,256]{2,1,0:T(8,128)(2,1)S(1)}) custom-call(bf16[8,4,16,256]{3,2,1,0:T(8,128)(2,1)S(1)} %copy-done.1, bf16[2304,256]{1,0:T(8,128)(2,1)S(1)} %copy-done.3, bf16[8,4,16,256]{3,2,1,0:T(8,128)(2,1)S(1)} %collective-permute-done.other, f32[8,128]{1,0:T(8,128)S(1)} %shard_map.67._), custom_call_target="tpu_custom_call" | custom-call | flops 1207959552 | bytes 2756608 | tf_op jit(solution)/shard_map/pallas_call | solution.py:129
  7.2 0.0 copy-start
  7.2 0.0 copy-start.2
  7.2 0.4 %collective-permute-start.6 = (bf16[2,512,256]{2,1,0:T(8,128)(2,1)S(1)}, bf16[2,512,256]{2,1,0:T(8,128)(2,1)S(1)}, u32[]{:S(2)}, u32[]{:S(2)}) collective-permute-start(bf16[2,512,256]{2,1,0:T(8,128)(2,1)S(1)} %get-tuple-element.21.act), channel_id=1, source_target_pairs={{2,0},{4,2},{6,4},{1,3},{3,5},{5,7},{7,6},{0,1},{10,8},{12,10},{14... | collective-permute-start | bytes 1572872 | tf_op jit(solution)/shard_map/ppermute | solution.py:380
  7.6 0.5 %shard_map.69._.feats_t = bf16[2,768,512]{2,1,0:T(8,128)(2,1)S(1)} custom-call(bf16[8,4,16,256]{3,2,1,0:T(8,128)(2,1)S(1)} %copy-done.1, bf16[8,4,16,256]{3,2,1,0:T(8,128)(2,1)S(1)} %collective-permute-done.other, f32[512,256]{1,0:T(8,128)S(1)} %get-tuple-element.16._.pre_ref), custom_call_target="tpu_custom_call" | custom-call | bytes 2621440 | tf_op jit(solution)/shard_map/pallas_call | solution.py:129
  8.1 1.5 %collective-permute-done.1.first_in = bf16[512,256]{1,0:T(8,128)(2,1)S(1)} collective-permute-done((bf16[512,256]{1,0:T(8,128)(2,1)}, bf16[512,256]{1,0:T(8,128)(2,1)S(1)}, u32[]{:S(2)}, u32[]{:S(2)}) %collective-permute-start.1) | collective-permute-done | bytes 262176 | tf_op jit(solution)/shard_map/ppermute | solution.py:368
  9.6 0.7 %collective-permute-done.2.second_in = bf16[512,256]{1,0:T(8,128)(2,1)S(1)} collective-permute-done((bf16[512,256]{1,0:T(8,128)(2,1)}, bf16[512,256]{1,0:T(8,128)(2,1)S(1)}, u32[]{:S(2)}, u32[]{:S(2)}) %collective-permute-start.2) | collective-permute-done | bytes 262176 | tf_op jit(solution)/shard_map/ppermute | solution.py:369
  10.3 0.0 copy-done
  10.3 0.0 copy-done.2
  10.3 0.9 %shard_map.70 = bf16[512,256]{1,0:T(8,128)(2,1)S(1)} custom-call(bf16[512,256]{1,0:T(8,128)(2,1)S(1)} %bitcast.11, bf16[512,256]{1,0:T(8,128)(2,1)S(1)} %collective-permute-done.1.first_in, bf16[512,256]{1,0:T(8,128)(2,1)S(1)} %collective-permute-done.2.second_in, bf16[2304,256]{1,0:T(8,128)(2,1)S(1)} %copy-done, ...), custom_call_target="tpu_custom_call" | custom-call | flops 603979776 | bytes 4325376 | tf_op jit(solution)/shard_map/pallas_call | solution.py:129
  11.2 0.1 collective-permute-start.3
  11.3 0.8 %shard_map.71.term = f32[3,768,256]{2,1,0:T(8,128)S(1)} custom-call(bf16[2,768,512]{2,1,0:T(8,128)(2,1)S(1)} %shard_map.69._.feats_t, bf16[8,4,16,256]{3,2,1,0:T(8,128)(2,1)S(1)} %bitcast.6), custom_call_target="tpu_custom_call" | custom-call | flops 603979776 | bytes 4194304 | tf_op jit(solution)/shard_map/pallas_call | solution.py:129
  12.1 0.7 %collective-permute-done.3.other = bf16[8,4,16,256]{3,2,1,0:T(8,128)(2,1)S(1)} collective-permute-done((bf16[8,4,16,256]{3,2,1,0:T(8,128)(2,1)S(1)}, bf16[8,4,16,256]{3,2,1,0:T(8,128)(2,1)S(1)}, u32[]{:S(2)}, u32[]{:S(2)}) %collective-permute-start.3) | collective-permute-done | bytes 262176 | tf_op jit(solution)/shard_map/ppermute | solution.py:396
  12.8 0.9 %shard_map.72 = (bf16[192,256]{1,0:T(8,128)(2,1)S(1)}, bf16[96,256]{1,0:T(8,128)(2,1)S(1)}, f32[288,256]{1,0:T(8,128)S(1)}, bf16[288,256]{1,0:T(8,128)(2,1)S(1)}, f32[288,256]{1,0:T(8,128)S(1)}) custom-call(bf16[2,768,512]{2,1,0:T(8,128)(2,1)S(1)} %shard_map.69._.feats_t, bf16[8,4,16,256]{3,2,1,0:T(8,128)(2,1)S(1)} %collective-permute-done.3.other, ...), custom_call_target="tpu_custom_call" | custom-call | flops 603979776 | bytes 5079040 | tf_op jit(solution)/shard_map/pallas_call | solution.py:129
  13.7 1.8 %collective-permute-start.5 = (bf16[192,256]{1,0:T(8,128)(2,1)S(1)}, bf16[192,256]{1,0:T(8,128)(2,1)S(1)}, u32[]{:S(2)}, u32[]{:S(2)}) collective-permute-start(bf16[192,256]{1,0:T(8,128)(2,1)S(1)} %get-tuple-element.20), channel_id=1, source_target_pairs={{0,2},{2,0},{4,6},{6,4},{1,3},{3,1},{5,7},{7,5},{8,10},{10,8},{12,... | collective-permute-start | bytes 294920 | tf_op jit(solution)/shard_map/ppermute | solution.py:417
  15.4 0.3 %collective-permute-start.9 = (bf16[96,256]{1,0:T(8,128)(2,1)S(1)}, bf16[96,256]{1,0:T(8,128)(2,1)S(1)}, u32[]{:S(2)}, u32[]{:S(2)}) collective-permute-start(bf16[96,256]{1,0:T(8,128)(2,1)S(1)} %get-tuple-element.24), channel_id=1, source_target_pairs={{0,2},{2,0},{4,6},{6,4},{1,3},{3,1},{5,7},{7,5},{8,10},{10,8},{12,... | collective-permute-start | bytes 147464 | tf_op jit(solution)/shard_map/ppermute | solution.py:418
  15.8 1.7 %collective-permute-start.4 = (bf16[288,256]{1,0:T(8,128)(2,1)S(1)}, bf16[288,256]{1,0:T(8,128)(2,1)S(1)}, u32[]{:S(2)}, u32[]{:S(2)}) collective-permute-start(bf16[288,256]{1,0:T(8,128)(2,1)S(1)} %get-tuple-element.18), channel_id=1, source_target_pairs={{0,2},{2,0},{4,6},{6,4},{1,3},{3,1},{5,7},{7,5},{8,10},{10,8},{12,... | collective-permute-start | bytes 442376 | tf_op jit(solution)/shard_map/ppermute | solution.py:419
  17.5 0.0 collective-permute-done.6.arrived
  17.5 0.1 collective-permute-start.8
  17.6 1.7 %collective-permute-done.5.arrived = bf16[192,256]{1,0:T(8,128)(2,1)S(1)} collective-permute-done((bf16[192,256]{1,0:T(8,128)(2,1)S(1)}, bf16[192,256]{1,0:T(8,128)(2,1)S(1)}, u32[]{:S(2)}, u32[]{:S(2)}) %collective-permute-start.5) | collective-permute-done | bytes 98336 | tf_op jit(solution)/shard_map/ppermute | solution.py:417
  19.3 4.1 %collective-permute-start.7 = (bf16[192,256]{1,0:T(8,128)(2,1)S(1)}, bf16[192,256]{1,0:T(8,128)(2,1)S(1)}, u32[]{:S(2)}, u32[]{:S(2)}) collective-permute-start(bf16[192,256]{1,0:T(8,128)(2,1)S(1)} %shard_map.74.rest_0_), channel_id=1, source_target_pairs={{0,6},{2,4},{4,2},{6,0},{1,7},{3,5},{5,3},{7,1},{8,14},{10,12},{12... | collective-permute-start | bytes 294920 | tf_op jit(solution)/shard_map/ppermute | solution.py:432
  23.4 0.0 collective-permute-done.9.arrived
  23.4 0.0 collective-permute-done.8.first_in.rest_1_
  23.4 1.0 %collective-permute-start.10 = (bf16[96,256]{1,0:T(8,128)(2,1)S(1)}, bf16[96,256]{1,0:T(8,128)(2,1)S(1)}, u32[]{:S(2)}, u32[]{:S(2)}) collective-permute-start(bf16[96,256]{1,0:T(8,128)(2,1)S(1)} %shard_map.76._), channel_id=1, source_target_pairs={{0,6},{2,4},{4,2},{6,0},{1,7},{3,5},{5,3},{7,1},{8,14},{10,12},{12... | collective-permute-start | bytes 147464 | tf_op jit(solution)/shard_map/ppermute | solution.py:440
  24.5 1.5 %shard_map.77 = (bf16[512,256]{1,0:T(8,128)(2,1)}, f32[8,128]{1,0:T(8,128)S(1)}) custom-call(bf16[512,256]{1,0:T(8,128)(2,1)S(1)} %bitcast.12, bf16[8,4,16,256]{3,2,1,0:T(8,128)(2,1)S(1)} %bitcast.7, bf16[8,4,16,256]{3,2,1,0:T(8,128)(2,1)S(1)} %collective-permute-done.3.other, bf16[2304,256]{1,0:T(8,128)(2,1)S(1)} %copy-done.3, bf16[96,256]{1,0:T(8,128)(2,1)S(1)} %shard_map.76._), custom_call_target="tpu_custom_call" | custom-call | flops 603979776 | bytes 2281472 | tf_op jit(solution)/shard_map/pallas_call | solution.py:129
  26.0 0.9 %shard_map.75.refs_3_.block = bf16[512,256]{1,0:T(8,128)(2,1)S(1)} custom-call(bf16[512,256]{1,0:T(8,128)(2,1)S(1)} %bitcast.8, bf16[2,512,256]{2,1,0:T(8,128)(2,1)S(1)} %get-tuple-element.21.act, bf16[512,256]{1,0:T(8,128)(2,1)S(1)} %collective-permute-done.8.first_in.rest_1_, bf16[512,256]{1,0:T(8,128)(2,1)S(1)} %get-tuple-element.23.second_in, ...), custom_call_target="tpu_custom_call" | custom-call | flops 603979776 | bytes 2752512 | tf_op jit(solution)/shard_map/pallas_call | solution.py:129
  26.9 0.0 collective-permute-done.4.refs_1_.near
  26.9 1.1 %collective-permute-done.7.refs_0_.last = bf16[192,256]{1,0:T(8,128)(2,1)S(1)} collective-permute-done((bf16[192,256]{1,0:T(8,128)(2,1)S(1)}, bf16[192,256]{1,0:T(8,128)(2,1)S(1)}, u32[]{:S(2)}, u32[]{:S(2)}) %collective-permute-start.7) | collective-permute-done | bytes 98336 | tf_op jit(solution)/shard_map/ppermute | solution.py:432
  27.9 0.8 %shard_map.79 = (f32[288,256]{1,0:T(8,128)}, bf16[512,256]{1,0:T(8,128)(2,1)}) custom-call(f32[288,256]{1,0:T(8,128)S(1)} %get-tuple-element.17.keep, bf16[288,256]{1,0:T(8,128)(2,1)S(1)} %collective-permute-done.4.refs_1_.near, bf16[192,256]{1,0:T(8,128)(2,1)S(1)} %collective-permute-done.7.refs_0_.last, bf16[512,256]{1,0:T(8,128)(2,1)S(1)} %shard_map.75.refs_3_.block, ...), custom_call_target="tpu_custom_call" | custom-call | tf_op jit(solution)/shard_map/pallas_call | solution.py:458
  28.7 0.7 %collective-permute-done.10.last = bf16[96,256]{1,0:T(8,128)(2,1)S(1)} collective-permute-done((bf16[96,256]{1,0:T(8,128)(2,1)S(1)}, bf16[96,256]{1,0:T(8,128)(2,1)S(1)}, u32[]{:S(2)}, u32[]{:S(2)}) %collective-permute-start.10) | collective-permute-done | bytes 49184 | tf_op jit(solution)/shard_map/ppermute | solution.py:440
  29.4 0.7 %shard_map.80 = f32[288,256]{1,0:T(8,128)} custom-call(f32[288,256]{1,0:T(8,128)S(1)} %get-tuple-element.17.keep, bf16[288,256]{1,0:T(8,128)(2,1)S(1)} %collective-permute-done.4.refs_1_.near, bf16[96,256]{1,0:T(8,128)(2,1)S(1)} %collective-permute-done.10.last, f32[288,256]{1,0:T(8,128)} %get-tuple-element.28._), custom_call_target="tpu_custom_call", output_to_operand_aliasing={{}: (3, {})} | custom-call | tf_op jit(solution)/shard_map/pallas_call | solution.py:469
  (5 shorter events, 0.1 us)
Async XLA Ops:
  0.6 4.8 %copy-start.1 = (bf16[8,4,16,256]{3,2,1,0:T(8,128)(2,1)S(1)}, bf16[8,4,16,256]{3,2,1,0:T(8,128)(2,1)}, u32[]{:S(2)}) copy-start(bf16[8,4,16,256]{3,2,1,0:T(8,128)(2,1)} %own.3) | copy-start | bytes 786436
  0.6 4.8 %copy-start.3 = (bf16[2304,256]{1,0:T(8,128)(2,1)S(1)}, bf16[2304,256]{1,0:T(8,128)(2,1)}, u32[]{:S(2)}) copy-start(bf16[2304,256]{1,0:T(8,128)(2,1)} %weight.7) | copy-start | bytes 3538948
  0.6 9.0 %collective-permute-start.1 = (bf16[512,256]{1,0:T(8,128)(2,1)}, bf16[512,256]{1,0:T(8,128)(2,1)S(1)}, u32[]{:S(2)}, u32[]{:S(2)}) collective-permute-start(bf16[512,256]{1,0:T(8,128)(2,1)} %bitcast.9), channel_id=1, source_target_pairs={{0,2},{2,4},{4,6},{3,1},{5,3},{7,5},{6,7},{1,0},{8,10},{10,12},{12... | collective-permute-start | bytes 786440 | tf_op jit(solution)/shard_map/ppermute | solution.py:368
  3.7 6.6 %collective-permute-start.2 = (bf16[512,256]{1,0:T(8,128)(2,1)}, bf16[512,256]{1,0:T(8,128)(2,1)S(1)}, u32[]{:S(2)}, u32[]{:S(2)}) collective-permute-start(bf16[512,256]{1,0:T(8,128)(2,1)} %bitcast.10), channel_id=1, source_target_pairs={{2,0},{4,2},{6,4},{1,3},{3,5},{5,7},{7,6},{0,1},{10,8},{12,10},{14... | collective-permute-start | bytes 786440 | tf_op jit(solution)/shard_map/ppermute | solution.py:369
  3.7 1.7 %collective-permute-start = (bf16[8,4,16,256]{3,2,1,0:T(8,128)(2,1)}, bf16[8,4,16,256]{3,2,1,0:T(8,128)(2,1)S(1)}, u32[]{:S(2)}, u32[]{:S(2)}) collective-permute-start(bf16[8,4,16,256]{3,2,1,0:T(8,128)(2,1)} %own.3), channel_id=1, source_target_pairs={{0,1},{1,0},{2,3},{3,2},{4,5},{5,4},{6,7},{7,6},{8,9},{9,8},{10,11... | collective-permute-start | bytes 786440 | tf_op jit(solution)/shard_map/ppermute | solution.py:370
  7.2 3.1 %copy-start = (bf16[2304,256]{1,0:T(8,128)(2,1)S(1)}, bf16[2304,256]{1,0:T(8,128)(2,1)}, u32[]{:S(2)}) copy-start(bf16[2304,256]{1,0:T(8,128)(2,1)} %weight.6) | copy-start | bytes 3538948
  7.2 3.1 %copy-start.2 = (bf16[8,4,16,256]{3,2,1,0:T(8,128)(2,1)S(1)}, bf16[8,4,16,256]{3,2,1,0:T(8,128)(2,1)}, u32[]{:S(2)}) copy-start(bf16[8,4,16,256]{3,2,1,0:T(8,128)(2,1)} %param.5) | copy-start | bytes 786436
  7.2 10.3 %collective-permute-start.6 = (bf16[2,512,256]{2,1,0:T(8,128)(2,1)S(1)}, bf16[2,512,256]{2,1,0:T(8,128)(2,1)S(1)}, u32[]{:S(2)}, u32[]{:S(2)}) collective-permute-start(bf16[2,512,256]{2,1,0:T(8,128)(2,1)S(1)} %get-tuple-element.21.act), channel_id=1, source_target_pairs={{2,0},{4,2},{6,4},{1,3},{3,5},{5,7},{7,6},{0,1},{10,8},{12,10},{14... | collective-permute-start | bytes 1572872 | tf_op jit(solution)/shard_map/ppermute | solution.py:380
  11.2 1.6 %collective-permute-start.3 = (bf16[8,4,16,256]{3,2,1,0:T(8,128)(2,1)S(1)}, bf16[8,4,16,256]{3,2,1,0:T(8,128)(2,1)S(1)}, u32[]{:S(2)}, u32[]{:S(2)}) collective-permute-start(bf16[8,4,16,256]{3,2,1,0:T(8,128)(2,1)S(1)} %bitcast.5), channel_id=1, source_target_pairs={{0,1},{1,0},{2,3},{3,2},{4,5},{5,4},{6,7},{7,6},{8,9},{9,8},{10,11... | collective-permute-start | bytes 786440 | tf_op jit(solution)/shard_map/ppermute | solution.py:396
  13.7 5.6 %collective-permute-start.5 = (bf16[192,256]{1,0:T(8,128)(2,1)S(1)}, bf16[192,256]{1,0:T(8,128)(2,1)S(1)}, u32[]{:S(2)}, u32[]{:S(2)}) collective-permute-start(bf16[192,256]{1,0:T(8,128)(2,1)S(1)} %get-tuple-element.20), channel_id=1, source_target_pairs={{0,2},{2,0},{4,6},{6,4},{1,3},{3,1},{5,7},{7,5},{8,10},{10,8},{12,... | collective-permute-start | bytes 294920 | tf_op jit(solution)/shard_map/ppermute | solution.py:417
  15.4 8.0 %collective-permute-start.9 = (bf16[96,256]{1,0:T(8,128)(2,1)S(1)}, bf16[96,256]{1,0:T(8,128)(2,1)S(1)}, u32[]{:S(2)}, u32[]{:S(2)}) collective-permute-start(bf16[96,256]{1,0:T(8,128)(2,1)S(1)} %get-tuple-element.24), channel_id=1, source_target_pairs={{0,2},{2,0},{4,6},{6,4},{1,3},{3,1},{5,7},{7,5},{8,10},{10,8},{12,... | collective-permute-start | bytes 147464 | tf_op jit(solution)/shard_map/ppermute | solution.py:418
  15.8 11.1 %collective-permute-start.4 = (bf16[288,256]{1,0:T(8,128)(2,1)S(1)}, bf16[288,256]{1,0:T(8,128)(2,1)S(1)}, u32[]{:S(2)}, u32[]{:S(2)}) collective-permute-start(bf16[288,256]{1,0:T(8,128)(2,1)S(1)} %get-tuple-element.18), channel_id=1, source_target_pairs={{0,2},{2,0},{4,6},{6,4},{1,3},{3,1},{5,7},{7,5},{8,10},{10,8},{12,... | collective-permute-start | bytes 442376 | tf_op jit(solution)/shard_map/ppermute | solution.py:419
  17.5 5.9 %collective-permute-start.8 = (bf16[512,256]{1,0:T(8,128)(2,1)S(1)}, bf16[512,256]{1,0:T(8,128)(2,1)S(1)}, u32[]{:S(2)}, u32[]{:S(2)}) collective-permute-start(bf16[512,256]{1,0:T(8,128)(2,1)S(1)} %get-tuple-element.22.rest_0_), channel_id=1, source_target_pairs={{0,1},{1,0},{2,3},{3,2},{4,5},{5,4},{6,7},{7,6},{8,9},{9,8},{10,11... | collective-permute-start | bytes 786440 | tf_op jit(solution)/shard_map/ppermute | solution.py:423
  19.3 8.6 %collective-permute-start.7 = (bf16[192,256]{1,0:T(8,128)(2,1)S(1)}, bf16[192,256]{1,0:T(8,128)(2,1)S(1)}, u32[]{:S(2)}, u32[]{:S(2)}) collective-permute-start(bf16[192,256]{1,0:T(8,128)(2,1)S(1)} %shard_map.74.rest_0_), channel_id=1, source_target_pairs={{0,6},{2,4},{4,2},{6,0},{1,7},{3,5},{5,3},{7,1},{8,14},{10,12},{12... | collective-permute-start | bytes 294920 | tf_op jit(solution)/shard_map/ppermute | solution.py:432
  23.4 6.0 %collective-permute-start.10 = (bf16[96,256]{1,0:T(8,128)(2,1)S(1)}, bf16[96,256]{1,0:T(8,128)(2,1)S(1)}, u32[]{:S(2)}, u32[]{:S(2)}) collective-permute-start(bf16[96,256]{1,0:T(8,128)(2,1)S(1)} %shard_map.76._), channel_id=1, source_target_pairs={{0,6},{2,4},{4,2},{6,0},{1,7},{3,5},{5,3},{7,1},{8,14},{10,12},{12... | collective-permute-start | bytes 147464 | tf_op jit(solution)/shard_map/ppermute | solution.py:440

commit v6 on v4

--- a/solution.py
+++ b/solution.py
@@ -315,9 +315,9 @@
     share = keep_ref.shape[0]
     half = share // 2
     for distance, skip, ref in (
-        (2, 0, far_a_ref),
-        (2, half, far_b_ref),
-        (3, 0, pass_ref),
+        (3, 0, far_a_ref),
+        (3, half, far_b_ref),
+        (2, 0, pass_ref),
         (1, 0, near_ref),
         (0, 0, keep_ref),
     ):
@@ -412,7 +412,7 @@
         feats_t, pre_other, term,
     )
     beside = [(z, z ^ 1) for z in range(chips)]
-    across = [(z, z ^ 3) for z in range(chips)]
+    across = [(z, z ^ 2) for z in range(chips)]
     far_in_a = lax.ppermute(far_a, "frame", beside)
     far_in_b = lax.ppermute(far_b, "frame", beside)
     near_in = lax.ppermute(near, "frame", beside)

time: 30 us -> 30 us (level)
  waiting for transfers between devices: 6.83 us -> 7.8 us
  starting transfers between devices: 13.4 us -> 12.5 us
    ppermute x1, waiting for transfers between devices: 0.68 us -> 2.45 us  [per_device_pair(): last_b = lax.ppermute(sum_b, 'frame', across)]
    ppermute x1, starting transfers between devices: 4.51 us -> 3.13 us  [per_device_pair(): last_a = lax.ppermute(sum_a, 'frame', across)]
    ppermute x1, waiting for transfers between devices: 0.8 us -> 0.01 us  [per_device_pair(): last_a = lax.ppermute(sum_a, 'frame', across)]
    ppermute x1, starting transfers between devices: 1.56 us -> 1.96 us  [per_device_pair(): last_b = lax.ppermute(sum_b, 'frame', across)]
  transfers between devices with their start and end apart: 11 -> 11, of which waited for: 7 -> 6; matrix products, arithmetic and copies ran while one was open for 0% -> 0% of each run, Pallas kernels for 27% -> 27%
where the time goes in v6:
time: 30 us; the launch traced here: 29.8 us
  starting transfers between devices  12.5 us (42%)
  Pallas kernels  8.78 us (29%)
  waiting for transfers between devices  7.8 us (26%)
  between operations  0.77 us (3%)
    pallas_call x12, Pallas kernels, kernel_call(): pl.pallas_call(body, out_shape=tuple((jax.ShapeDtypeStruct(shape, kind) f...  7.31 us
    ppermute x1, starting transfers between devices, per_device_pair(): last_a = lax.ppermute(sum_a, 'frame', across)  3.13 us
    ppermute x1, starting transfers between devices, per_device_pair(): grad_first = lax.ppermute(grad_flat, both, outward)  3.04 us
    ppermute x1, waiting for transfers between devices, per_device_pair(): last_b = lax.ppermute(sum_b, 'frame', across)  2.45 us
    ppermute x1, starting transfers between devices, per_device_pair(): last_b = lax.ppermute(sum_b, 'frame', across)  1.96 us
    ppermute x1, starting transfers between devices, per_device_pair(): far_in_a = lax.ppermute(far_a, 'frame', beside)  1.76 us
    ppermute x1, waiting for transfers between devices, per_device_pair(): feat_other = lax.ppermute(clip_feats, 'tile', swap)  1.74 us
    ppermute x1, starting transfers between devices, per_device_pair(): near_in = lax.ppermute(near, 'frame', beside)  1.7 us
  transfers between devices with their start and end apart: 11, of which 6 were waited for; matrix products, arithmetic and copies ran while one was open for 0% of the time, Pallas kernels for 27%

profile of v6, /device:TPU:0, one launch (start us, length us, event | category | flops | bytes accessed | tf_op | source)
XLA Modules:
  0.0 29.8 jit_solution(2935630720048828321)
XLA Ops:
  0.6 0.0 copy-start.1
  0.6 0.0 copy-start.3
  0.6 3.0 %collective-permute-start.1 = (bf16[512,256]{1,0:T(8,128)(2,1)}, bf16[512,256]{1,0:T(8,128)(2,1)S(1)}, u32[]{:S(2)}, u32[]{:S(2)}) collective-permute-start(bf16[512,256]{1,0:T(8,128)(2,1)} %bitcast.9), channel_id=1, source_target_pairs={{0,2},{2,4},{4,6},{3,1},{5,3},{7,5},{6,7},{1,0},{8,10},{10,12},{12... | collective-permute-start | bytes 786440 | tf_op jit(solution)/shard_map/ppermute | solution.py:368
  3.7 0.0 collective-permute-start.2
  3.7 0.0 collective-permute-start
  3.7 1.7 %collective-permute-done.other = bf16[8,4,16,256]{3,2,1,0:T(8,128)(2,1)S(1)} collective-permute-done((bf16[8,4,16,256]{3,2,1,0:T(8,128)(2,1)}, bf16[8,4,16,256]{3,2,1,0:T(8,128)(2,1)S(1)}, u32[]{:S(2)}, u32[]{:S(2)}) %collective-permute-start) | collective-permute-done | bytes 262176 | tf_op jit(solution)/shard_map/ppermute | solution.py:370
  5.4 0.0 copy-done.1
  5.4 0.0 copy-done.3
  5.4 1.7 %shard_map.68 = (f32[512,256]{1,0:T(8,128)S(1)}, bf16[2,512,256]{2,1,0:T(8,128)(2,1)S(1)}) custom-call(bf16[8,4,16,256]{3,2,1,0:T(8,128)(2,1)S(1)} %copy-done.1, bf16[2304,256]{1,0:T(8,128)(2,1)S(1)} %copy-done.3, bf16[8,4,16,256]{3,2,1,0:T(8,128)(2,1)S(1)} %collective-permute-done.other, f32[8,128]{1,0:T(8,128)S(1)} %shard_map.67._), custom_call_target="tpu_custom_call" | custom-call | flops 1207959552 | bytes 2756608 | tf_op jit(solution)/shard_map/pallas_call | solution.py:129
  7.2 0.0 copy-start
  7.2 0.0 copy-start.2
  7.2 0.4 %collective-permute-start.6 = (bf16[2,512,256]{2,1,0:T(8,128)(2,1)S(1)}, bf16[2,512,256]{2,1,0:T(8,128)(2,1)S(1)}, u32[]{:S(2)}, u32[]{:S(2)}) collective-permute-start(bf16[2,512,256]{2,1,0:T(8,128)(2,1)S(1)} %get-tuple-element.21.act), channel_id=1, source_target_pairs={{2,0},{4,2},{6,4},{1,3},{3,5},{5,7},{7,6},{0,1},{10,8},{12,10},{14... | collective-permute-start | bytes 1572872 | tf_op jit(solution)/shard_map/ppermute | solution.py:380
  7.6 0.5 %shard_map.69._.feats_t = bf16[2,768,512]{2,1,0:T(8,128)(2,1)S(1)} custom-call(bf16[8,4,16,256]{3,2,1,0:T(8,128)(2,1)S(1)} %copy-done.1, bf16[8,4,16,256]{3,2,1,0:T(8,128)(2,1)S(1)} %collective-permute-done.other, f32[512,256]{1,0:T(8,128)S(1)} %get-tuple-element.16._.pre_ref), custom_call_target="tpu_custom_call" | custom-call | bytes 2621440 | tf_op jit(solution)/shard_map/pallas_call | solution.py:129
  8.1 1.5 %collective-permute-done.1.first_in = bf16[512,256]{1,0:T(8,128)(2,1)S(1)} collective-permute-done((bf16[512,256]{1,0:T(8,128)(2,1)}, bf16[512,256]{1,0:T(8,128)(2,1)S(1)}, u32[]{:S(2)}, u32[]{:S(2)}) %collective-permute-start.1) | collective-permute-done | bytes 262176 | tf_op jit(solution)/shard_map/ppermute | solution.py:368
  9.6 0.7 %collective-permute-done.2.second_in = bf16[512,256]{1,0:T(8,128)(2,1)S(1)} collective-permute-done((bf16[512,256]{1,0:T(8,128)(2,1)}, bf16[512,256]{1,0:T(8,128)(2,1)S(1)}, u32[]{:S(2)}, u32[]{:S(2)}) %collective-permute-start.2) | collective-permute-done | bytes 262176 | tf_op jit(solution)/shard_map/ppermute | solution.py:369
  10.3 0.0 copy-done
  10.3 0.0 copy-done.2
  10.3 0.9 %shard_map.70 = bf16[512,256]{1,0:T(8,128)(2,1)S(1)} custom-call(bf16[512,256]{1,0:T(8,128)(2,1)S(1)} %bitcast.11, bf16[512,256]{1,0:T(8,128)(2,1)S(1)} %collective-permute-done.1.first_in, bf16[512,256]{1,0:T(8,128)(2,1)S(1)} %collective-permute-done.2.second_in, bf16[2304,256]{1,0:T(8,128)(2,1)S(1)} %copy-done, ...), custom_call_target="tpu_custom_call" | custom-call | flops 603979776 | bytes 4325376 | tf_op jit(solution)/shard_map/pallas_call | solution.py:129
  11.2 0.1 collective-permute-start.3
  11.3 0.8 %shard_map.71.term = f32[3,768,256]{2,1,0:T(8,128)S(1)} custom-call(bf16[2,768,512]{2,1,0:T(8,128)(2,1)S(1)} %shard_map.69._.feats_t, bf16[8,4,16,256]{3,2,1,0:T(8,128)(2,1)S(1)} %bitcast.6), custom_call_target="tpu_custom_call" | custom-call | flops 603979776 | bytes 4194304 | tf_op jit(solution)/shard_map/pallas_call | solution.py:129
  12.1 0.7 %collective-permute-done.3.other = bf16[8,4,16,256]{3,2,1,0:T(8,128)(2,1)S(1)} collective-permute-done((bf16[8,4,16,256]{3,2,1,0:T(8,128)(2,1)S(1)}, bf16[8,4,16,256]{3,2,1,0:T(8,128)(2,1)S(1)}, u32[]{:S(2)}, u32[]{:S(2)}) %collective-permute-start.3) | collective-permute-done | bytes 262176 | tf_op jit(solution)/shard_map/ppermute | solution.py:396
  12.8 0.9 %shard_map.72 = (bf16[144,256]{1,0:T(8,128)(2,1)S(1)}, bf16[144,256]{1,0:T(8,128)(2,1)S(1)}, f32[288,256]{1,0:T(8,128)S(1)}, bf16[288,256]{1,0:T(8,128)(2,1)S(1)}, f32[288,256]{1,0:T(8,128)S(1)}) custom-call(bf16[2,768,512]{2,1,0:T(8,128)(2,1)S(1)} %shard_map.69._.feats_t, bf16[8,4,16,256]{3,2,1,0:T(8,128)(2,1)S(1)} %collective-permute-done.3.other, ...), custom_call_target="tpu_custom_call" | custom-call | flops 603979776 | bytes 5079040 | tf_op jit(solution)/shard_map/pallas_call | solution.py:129
  13.7 1.8 %collective-permute-start.5 = (bf16[144,256]{1,0:T(8,128)(2,1)S(1)}, bf16[144,256]{1,0:T(8,128)(2,1)S(1)}, u32[]{:S(2)}, u32[]{:S(2)}) collective-permute-start(bf16[144,256]{1,0:T(8,128)(2,1)S(1)} %get-tuple-element.20), channel_id=1, source_target_pairs={{0,2},{2,0},{4,6},{6,4},{1,3},{3,1},{5,7},{7,5},{8,10},{10,8},{12,... | collective-permute-start | bytes 221192 | tf_op jit(solution)/shard_map/ppermute | solution.py:416
  15.4 0.3 %collective-permute-start.9 = (bf16[144,256]{1,0:T(8,128)(2,1)S(1)}, bf16[144,256]{1,0:T(8,128)(2,1)S(1)}, u32[]{:S(2)}, u32[]{:S(2)}) collective-permute-start(bf16[144,256]{1,0:T(8,128)(2,1)S(1)} %get-tuple-element.24), channel_id=1, source_target_pairs={{0,2},{2,0},{4,6},{6,4},{1,3},{3,1},{5,7},{7,5},{8,10},{10,8},{12,... | collective-permute-start | bytes 221192 | tf_op jit(solution)/shard_map/ppermute | solution.py:417
  15.8 1.7 %collective-permute-start.4 = (bf16[288,256]{1,0:T(8,128)(2,1)S(1)}, bf16[288,256]{1,0:T(8,128)(2,1)S(1)}, u32[]{:S(2)}, u32[]{:S(2)}) collective-permute-start(bf16[288,256]{1,0:T(8,128)(2,1)S(1)} %get-tuple-element.18), channel_id=1, source_target_pairs={{0,2},{2,0},{4,6},{6,4},{1,3},{3,1},{5,7},{7,5},{8,10},{10,8},{12,... | collective-permute-start | bytes 442376 | tf_op jit(solution)/shard_map/ppermute | solution.py:418
  17.5 0.0 collective-permute-done.6.arrived
  17.5 0.1 collective-permute-start.8
  17.6 0.8 %collective-permute-done.5.arrived = bf16[144,256]{1,0:T(8,128)(2,1)S(1)} collective-permute-done((bf16[144,256]{1,0:T(8,128)(2,1)S(1)}, bf16[144,256]{1,0:T(8,128)(2,1)S(1)}, u32[]{:S(2)}, u32[]{:S(2)}) %collective-permute-start.5) | collective-permute-done | bytes 73760 | tf_op jit(solution)/shard_map/ppermute | solution.py:416
  18.4 3.1 %collective-permute-start.7 = (bf16[144,256]{1,0:T(8,128)(2,1)S(1)}, bf16[144,256]{1,0:T(8,128)(2,1)S(1)}, u32[]{:S(2)}, u32[]{:S(2)}) collective-permute-start(bf16[144,256]{1,0:T(8,128)(2,1)S(1)} %shard_map.74.rest_0_), channel_id=1, source_target_pairs={{0,4},{2,6},{4,0},{6,2},{1,5},{3,7},{5,1},{7,3},{8,12},{10,14},{12... | collective-permute-start | bytes 221192 | tf_op jit(solution)/shard_map/ppermute | solution.py:431
  21.5 0.0 collective-permute-done.9.arrived
  21.5 0.0 collective-permute-done.8.first_in.rest_1_
  21.5 2.0 %collective-permute-start.10 = (bf16[144,256]{1,0:T(8,128)(2,1)S(1)}, bf16[144,256]{1,0:T(8,128)(2,1)S(1)}, u32[]{:S(2)}, u32[]{:S(2)}) collective-permute-start(bf16[144,256]{1,0:T(8,128)(2,1)S(1)} %shard_map.76._), channel_id=1, source_target_pairs={{0,4},{2,6},{4,0},{6,2},{1,5},{3,7},{5,1},{7,3},{8,12},{10,14},{12... | collective-permute-start | bytes 221192 | tf_op jit(solution)/shard_map/ppermute | solution.py:439
  23.5 1.5 %shard_map.77 = (bf16[512,256]{1,0:T(8,128)(2,1)}, f32[8,128]{1,0:T(8,128)S(1)}) custom-call(bf16[512,256]{1,0:T(8,128)(2,1)S(1)} %bitcast.12, bf16[8,4,16,256]{3,2,1,0:T(8,128)(2,1)S(1)} %bitcast.7, bf16[8,4,16,256]{3,2,1,0:T(8,128)(2,1)S(1)} %collective-permute-done.3.other, bf16[2304,256]{1,0:T(8,128)(2,1)S(1)} %copy-done.3, bf16[144,256]{1,0:T(8,128)(2,1)S(1)} %shard_map.76._), custom_call_target="tpu_custom_call" | custom-call | flops 603979776 | bytes 2306048 | tf_op jit(solution)/shard_map/pallas_call | solution.py:129
  25.0 0.9 %shard_map.75.refs_3_.block = bf16[512,256]{1,0:T(8,128)(2,1)S(1)} custom-call(bf16[512,256]{1,0:T(8,128)(2,1)S(1)} %bitcast.8, bf16[2,512,256]{2,1,0:T(8,128)(2,1)S(1)} %get-tuple-element.21.act, bf16[512,256]{1,0:T(8,128)(2,1)S(1)} %collective-permute-done.8.first_in.rest_1_, bf16[512,256]{1,0:T(8,128)(2,1)S(1)} %get-tuple-element.23.second_in, ...), custom_call_target="tpu_custom_call" | custom-call | flops 603979776 | bytes 2752512 | tf_op jit(solution)/shard_map/pallas_call | solution.py:129
  25.9 0.0 collective-permute-done.4.refs_1_.near
  25.9 0.0 collective-permute-done.7.refs_0_.last
  25.9 0.8 %shard_map.79 = (f32[288,256]{1,0:T(8,128)}, bf16[512,256]{1,0:T(8,128)(2,1)}) custom-call(f32[288,256]{1,0:T(8,128)S(1)} %get-tuple-element.17.keep, bf16[288,256]{1,0:T(8,128)(2,1)S(1)} %collective-permute-done.4.refs_1_.near, bf16[144,256]{1,0:T(8,128)(2,1)S(1)} %collective-permute-done.7.refs_0_.last, bf16[512,256]{1,0:T(8,128)(2,1)S(1)} %shard_map.75.refs_3_.block, ...), custom_call_target="tpu_custom_call" | custom-call | tf_op jit(solution)/shard_map/pallas_call | solution.py:457
  26.7 2.4 %collective-permute-done.10.last = bf16[144,256]{1,0:T(8,128)(2,1)S(1)} collective-permute-done((bf16[144,256]{1,0:T(8,128)(2,1)S(1)}, bf16[144,256]{1,0:T(8,128)(2,1)S(1)}, u32[]{:S(2)}, u32[]{:S(2)}) %collective-permute-start.10) | collective-permute-done | bytes 73760 | tf_op jit(solution)/shard_map/ppermute | solution.py:439
  29.1 0.7 %shard_map.80 = f32[288,256]{1,0:T(8,128)} custom-call(f32[288,256]{1,0:T(8,128)S(1)} %get-tuple-element.17.keep, bf16[288,256]{1,0:T(8,128)(2,1)S(1)} %collective-permute-done.4.refs_1_.near, bf16[144,256]{1,0:T(8,128)(2,1)S(1)} %collective-permute-done.10.last, f32[288,256]{1,0:T(8,128)} %get-tuple-element.28._), custom_call_target="tpu_custom_call", output_to_operand_aliasing={{}: (3, {})} | custom-call | tf_op jit(solution)/shard_map/pallas_call | solution.py:468
  (5 shorter events, 0.1 us)
Async XLA Ops:
  0.6 4.8 %copy-start.1 = (bf16[8,4,16,256]{3,2,1,0:T(8,128)(2,1)S(1)}, bf16[8,4,16,256]{3,2,1,0:T(8,128)(2,1)}, u32[]{:S(2)}) copy-start(bf16[8,4,16,256]{3,2,1,0:T(8,128)(2,1)} %own.3) | copy-start | bytes 786436
  0.6 4.8 %copy-start.3 = (bf16[2304,256]{1,0:T(8,128)(2,1)S(1)}, bf16[2304,256]{1,0:T(8,128)(2,1)}, u32[]{:S(2)}) copy-start(bf16[2304,256]{1,0:T(8,128)(2,1)} %weight.7) | copy-start | bytes 3538948
  0.6 9.0 %collective-permute-start.1 = (bf16[512,256]{1,0:T(8,128)(2,1)}, bf16[512,256]{1,0:T(8,128)(2,1)S(1)}, u32[]{:S(2)}, u32[]{:S(2)}) collective-permute-start(bf16[512,256]{1,0:T(8,128)(2,1)} %bitcast.9), channel_id=1, source_target_pairs={{0,2},{2,4},{4,6},{3,1},{5,3},{7,5},{6,7},{1,0},{8,10},{10,12},{12... | collective-permute-start | bytes 786440 | tf_op jit(solution)/shard_map/ppermute | solution.py:368
  3.7 6.6 %collective-permute-start.2 = (bf16[512,256]{1,0:T(8,128)(2,1)}, bf16[512,256]{1,0:T(8,128)(2,1)S(1)}, u32[]{:S(2)}, u32[]{:S(2)}) collective-permute-start(bf16[512,256]{1,0:T(8,128)(2,1)} %bitcast.10), channel_id=1, source_target_pairs={{2,0},{4,2},{6,4},{1,3},{3,5},{5,7},{7,6},{0,1},{10,8},{12,10},{14... | collective-permute-start | bytes 786440 | tf_op jit(solution)/shard_map/ppermute | solution.py:369
  3.7 1.7 %collective-permute-start = (bf16[8,4,16,256]{3,2,1,0:T(8,128)(2,1)}, bf16[8,4,16,256]{3,2,1,0:T(8,128)(2,1)S(1)}, u32[]{:S(2)}, u32[]{:S(2)}) collective-permute-start(bf16[8,4,16,256]{3,2,1,0:T(8,128)(2,1)} %own.3), channel_id=1, source_target_pairs={{0,1},{1,0},{2,3},{3,2},{4,5},{5,4},{6,7},{7,6},{8,9},{9,8},{10,11... | collective-permute-start | bytes 786440 | tf_op jit(solution)/shard_map/ppermute | solution.py:370
  7.2 3.1 %copy-start = (bf16[2304,256]{1,0:T(8,128)(2,1)S(1)}, bf16[2304,256]{1,0:T(8,128)(2,1)}, u32[]{:S(2)}) copy-start(bf16[2304,256]{1,0:T(8,128)(2,1)} %weight.6) | copy-start | bytes 3538948
  7.2 3.1 %copy-start.2 = (bf16[8,4,16,256]{3,2,1,0:T(8,128)(2,1)S(1)}, bf16[8,4,16,256]{3,2,1,0:T(8,128)(2,1)}, u32[]{:S(2)}) copy-start(bf16[8,4,16,256]{3,2,1,0:T(8,128)(2,1)} %param.5) | copy-start | bytes 786436
  7.2 10.3 %collective-permute-start.6 = (bf16[2,512,256]{2,1,0:T(8,128)(2,1)S(1)}, bf16[2,512,256]{2,1,0:T(8,128)(2,1)S(1)}, u32[]{:S(2)}, u32[]{:S(2)}) collective-permute-start(bf16[2,512,256]{2,1,0:T(8,128)(2,1)S(1)} %get-tuple-element.21.act), channel_id=1, source_target_pairs={{2,0},{4,2},{6,4},{1,3},{3,5},{5,7},{7,6},{0,1},{10,8},{12,10},{14... | collective-permute-start | bytes 1572872 | tf_op jit(solution)/shard_map/ppermute | solution.py:380
  11.2 1.6 %collective-permute-start.3 = (bf16[8,4,16,256]{3,2,1,0:T(8,128)(2,1)S(1)}, bf16[8,4,16,256]{3,2,1,0:T(8,128)(2,1)S(1)}, u32[]{:S(2)}, u32[]{:S(2)}) collective-permute-start(bf16[8,4,16,256]{3,2,1,0:T(8,128)(2,1)S(1)} %bitcast.5), channel_id=1, source_target_pairs={{0,1},{1,0},{2,3},{3,2},{4,5},{5,4},{6,7},{7,6},{8,9},{9,8},{10,11... | collective-permute-start | bytes 786440 | tf_op jit(solution)/shard_map/ppermute | solution.py:396
  13.7 4.7 %collective-permute-start.5 = (bf16[144,256]{1,0:T(8,128)(2,1)S(1)}, bf16[144,256]{1,0:T(8,128)(2,1)S(1)}, u32[]{:S(2)}, u32[]{:S(2)}) collective-permute-start(bf16[144,256]{1,0:T(8,128)(2,1)S(1)} %get-tuple-element.20), channel_id=1, source_target_pairs={{0,2},{2,0},{4,6},{6,4},{1,3},{3,1},{5,7},{7,5},{8,10},{10,8},{12,... | collective-permute-start | bytes 221192 | tf_op jit(solution)/shard_map/ppermute | solution.py:416
  15.4 6.1 %collective-permute-start.9 = (bf16[144,256]{1,0:T(8,128)(2,1)S(1)}, bf16[144,256]{1,0:T(8,128)(2,1)S(1)}, u32[]{:S(2)}, u32[]{:S(2)}) collective-permute-start(bf16[144,256]{1,0:T(8,128)(2,1)S(1)} %get-tuple-element.24), channel_id=1, source_target_pairs={{0,2},{2,0},{4,6},{6,4},{1,3},{3,1},{5,7},{7,5},{8,10},{10,8},{12,... | collective-permute-start | bytes 221192 | tf_op jit(solution)/shard_map/ppermute | solution.py:417
  15.8 10.1 %collective-permute-start.4 = (bf16[288,256]{1,0:T(8,128)(2,1)S(1)}, bf16[288,256]{1,0:T(8,128)(2,1)S(1)}, u32[]{:S(2)}, u32[]{:S(2)}) collective-permute-start(bf16[288,256]{1,0:T(8,128)(2,1)S(1)} %get-tuple-element.18), channel_id=1, source_target_pairs={{0,2},{2,0},{4,6},{6,4},{1,3},{3,1},{5,7},{7,5},{8,10},{10,8},{12,... | collective-permute-start | bytes 442376 | tf_op jit(solution)/shard_map/ppermute | solution.py:418
  17.5 4.0 %collective-permute-start.8 = (bf16[512,256]{1,0:T(8,128)(2,1)S(1)}, bf16[512,256]{1,0:T(8,128)(2,1)S(1)}, u32[]{:S(2)}, u32[]{:S(2)}) collective-permute-start(bf16[512,256]{1,0:T(8,128)(2,1)S(1)} %get-tuple-element.22.rest_0_), channel_id=1, source_target_pairs={{0,1},{1,0},{2,3},{3,2},{4,5},{5,4},{6,7},{7,6},{8,9},{9,8},{10,11... | collective-permute-start | bytes 786440 | tf_op jit(solution)/shard_map/ppermute | solution.py:422
  18.4 7.5 %collective-permute-start.7 = (bf16[144,256]{1,0:T(8,128)(2,1)S(1)}, bf16[144,256]{1,0:T(8,128)(2,1)S(1)}, u32[]{:S(2)}, u32[]{:S(2)}) collective-permute-start(bf16[144,256]{1,0:T(8,128)(2,1)S(1)} %shard_map.74.rest_0_), channel_id=1, source_target_pairs={{0,4},{2,6},{4,0},{6,2},{1,5},{3,7},{5,1},{7,3},{8,12},{10,14},{12... | collective-permute-start | bytes 221192 | tf_op jit(solution)/shard_map/ppermute | solution.py:431
  21.5 7.6 %collective-permute-start.10 = (bf16[144,256]{1,0:T(8,128)(2,1)S(1)}, bf16[144,256]{1,0:T(8,128)(2,1)S(1)}, u32[]{:S(2)}, u32[]{:S(2)}) collective-permute-start(bf16[144,256]{1,0:T(8,128)(2,1)S(1)} %shard_map.76._), channel_id=1, source_target_pairs={{0,4},{2,6},{4,0},{6,2},{1,5},{3,7},{5,1},{7,3},{8,12},{10,14},{12... | collective-permute-start | bytes 221192 | tf_op jit(solution)/shard_map/ppermute | solution.py:439

commit v7 on v5

--- a/solution.py
+++ b/solution.py
@@ -403,7 +403,7 @@
         product,
         feats_t, pre_grad,
     )
-    part_a = (share[0] * 2 // 3, channels)
+    part_a = (share[0] // 3, channels)
     part_b = (share[0] - part_a[0], channels)
     far_a, far_b, onward, near, keep = kernel_call(
         kernel_grad_kernel,

time: 30.2 us -> 29.8 us (0.987)
  waiting for transfers between devices: 8.05 us -> 6.12 us
  starting transfers between devices: 12.5 us -> 14 us
    ppermute x1, waiting for transfers between devices: 1.73 us -> 0.24 us  [per_device_pair(): far_in_a = lax.ppermute(far_a, 'frame', beside)]
    ppermute x1, starting transfers between devices: 1.02 us -> 2.09 us  [per_device_pair(): last_b = lax.ppermute(sum_b, 'frame', across)]
    ppermute x1, starting transfers between devices: 4.07 us -> 4.5 us  [per_device_pair(): last_a = lax.ppermute(sum_a, 'frame', across)]
where the time goes in v7:
time: 29.8 us; the launch traced here: 29.6 us
  starting transfers between devices  14 us (47%)
  Pallas kernels  8.77 us (29%)
  waiting for transfers between devices  6.12 us (21%)
  between operations  0.76 us (3%)
    pallas_call x12, Pallas kernels, kernel_call(): pl.pallas_call(body, out_shape=tuple((jax.ShapeDtypeStruct(shape, kind) f...  7.3 us
    ppermute x1, starting transfers between devices, per_device_pair(): last_a = lax.ppermute(sum_a, 'frame', across)  4.5 us
    ppermute x1, starting transfers between devices, per_device_pair(): grad_first = lax.ppermute(grad_flat, both, outward)  3.04 us
    ppermute x1, starting transfers between devices, per_device_pair(): last_b = lax.ppermute(sum_b, 'frame', across)  2.09 us
    ppermute x1, starting transfers between devices, per_device_pair(): far_in_a = lax.ppermute(far_a, 'frame', beside)  1.76 us
    ppermute x1, waiting for transfers between devices, per_device_pair(): feat_other = lax.ppermute(clip_feats, 'tile', swap)  1.74 us
    ppermute x1, starting transfers between devices, per_device_pair(): near_in = lax.ppermute(near, 'frame', beside)  1.7 us
    ppermute x1, waiting for transfers between devices, per_device_pair(): grad_first = lax.ppermute(grad_flat, both, outward)  1.47 us
  transfers between devices with their start and end apart: 11, of which 7 were waited for; matrix products, arithmetic and copies ran while one was open for 0% of the time, Pallas kernels for 27%

profile of v7, /device:TPU:0, one launch (start us, length us, event | category | flops | bytes accessed | tf_op | source)
XLA Modules:
  0.0 29.6 jit_solution(16868048962983909693)
XLA Ops:
  0.6 0.0 copy-start.1
  0.6 0.0 copy-start.3
  0.6 3.0 %collective-permute-start.1 = (bf16[512,256]{1,0:T(8,128)(2,1)}, bf16[512,256]{1,0:T(8,128)(2,1)S(1)}, u32[]{:S(2)}, u32[]{:S(2)}) collective-permute-start(bf16[512,256]{1,0:T(8,128)(2,1)} %bitcast.9), channel_id=1, source_target_pairs={{0,2},{2,4},{4,6},{3,1},{5,3},{7,5},{6,7},{1,0},{8,10},{10,12},{12... | collective-permute-start | bytes 786440 | tf_op jit(solution)/shard_map/ppermute | solution.py:368
  3.7 0.0 collective-permute-start.2
  3.7 0.0 collective-permute-start
  3.7 1.7 %collective-permute-done.other = bf16[8,4,16,256]{3,2,1,0:T(8,128)(2,1)S(1)} collective-permute-done((bf16[8,4,16,256]{3,2,1,0:T(8,128)(2,1)}, bf16[8,4,16,256]{3,2,1,0:T(8,128)(2,1)S(1)}, u32[]{:S(2)}, u32[]{:S(2)}) %collective-permute-start) | collective-permute-done | bytes 262176 | tf_op jit(solution)/shard_map/ppermute | solution.py:370
  5.4 0.0 copy-done.1
  5.4 0.0 copy-done.3
  5.4 1.7 %shard_map.68 = (f32[512,256]{1,0:T(8,128)S(1)}, bf16[2,512,256]{2,1,0:T(8,128)(2,1)S(1)}) custom-call(bf16[8,4,16,256]{3,2,1,0:T(8,128)(2,1)S(1)} %copy-done.1, bf16[2304,256]{1,0:T(8,128)(2,1)S(1)} %copy-done.3, bf16[8,4,16,256]{3,2,1,0:T(8,128)(2,1)S(1)} %collective-permute-done.other, f32[8,128]{1,0:T(8,128)S(1)} %shard_map.67._), custom_call_target="tpu_custom_call" | custom-call | flops 1207959552 | bytes 2756608 | tf_op jit(solution)/shard_map/pallas_call | solution.py:129
  7.2 0.0 copy-start
  7.2 0.0 copy-start.2
  7.2 0.4 %collective-permute-start.6 = (bf16[2,512,256]{2,1,0:T(8,128)(2,1)S(1)}, bf16[2,512,256]{2,1,0:T(8,128)(2,1)S(1)}, u32[]{:S(2)}, u32[]{:S(2)}) collective-permute-start(bf16[2,512,256]{2,1,0:T(8,128)(2,1)S(1)} %get-tuple-element.21.act), channel_id=1, source_target_pairs={{2,0},{4,2},{6,4},{1,3},{3,5},{5,7},{7,6},{0,1},{10,8},{12,10},{14... | collective-permute-start | bytes 1572872 | tf_op jit(solution)/shard_map/ppermute | solution.py:380
  7.6 0.5 %shard_map.69._.feats_t = bf16[2,768,512]{2,1,0:T(8,128)(2,1)S(1)} custom-call(bf16[8,4,16,256]{3,2,1,0:T(8,128)(2,1)S(1)} %copy-done.1, bf16[8,4,16,256]{3,2,1,0:T(8,128)(2,1)S(1)} %collective-permute-done.other, f32[512,256]{1,0:T(8,128)S(1)} %get-tuple-element.16._.pre_ref), custom_call_target="tpu_custom_call" | custom-call | bytes 2621440 | tf_op jit(solution)/shard_map/pallas_call | solution.py:129
  8.1 1.5 %collective-permute-done.1.first_in = bf16[512,256]{1,0:T(8,128)(2,1)S(1)} collective-permute-done((bf16[512,256]{1,0:T(8,128)(2,1)}, bf16[512,256]{1,0:T(8,128)(2,1)S(1)}, u32[]{:S(2)}, u32[]{:S(2)}) %collective-permute-start.1) | collective-permute-done | bytes 262176 | tf_op jit(solution)/shard_map/ppermute | solution.py:368
  9.6 0.7 %collective-permute-done.2.second_in = bf16[512,256]{1,0:T(8,128)(2,1)S(1)} collective-permute-done((bf16[512,256]{1,0:T(8,128)(2,1)}, bf16[512,256]{1,0:T(8,128)(2,1)S(1)}, u32[]{:S(2)}, u32[]{:S(2)}) %collective-permute-start.2) | collective-permute-done | bytes 262176 | tf_op jit(solution)/shard_map/ppermute | solution.py:369
  10.3 0.0 copy-done
  10.3 0.0 copy-done.2
  10.3 0.9 %shard_map.70 = bf16[512,256]{1,0:T(8,128)(2,1)S(1)} custom-call(bf16[512,256]{1,0:T(8,128)(2,1)S(1)} %bitcast.11, bf16[512,256]{1,0:T(8,128)(2,1)S(1)} %collective-permute-done.1.first_in, bf16[512,256]{1,0:T(8,128)(2,1)S(1)} %collective-permute-done.2.second_in, bf16[2304,256]{1,0:T(8,128)(2,1)S(1)} %copy-done, ...), custom_call_target="tpu_custom_call" | custom-call | flops 603979776 | bytes 4325376 | tf_op jit(solution)/shard_map/pallas_call | solution.py:129
  11.2 0.1 collective-permute-start.3
  11.3 0.8 %shard_map.71.term = f32[3,768,256]{2,1,0:T(8,128)S(1)} custom-call(bf16[2,768,512]{2,1,0:T(8,128)(2,1)S(1)} %shard_map.69._.feats_t, bf16[8,4,16,256]{3,2,1,0:T(8,128)(2,1)S(1)} %bitcast.6), custom_call_target="tpu_custom_call" | custom-call | flops 603979776 | bytes 4194304 | tf_op jit(solution)/shard_map/pallas_call | solution.py:129
  12.1 0.7 %collective-permute-done.3.other = bf16[8,4,16,256]{3,2,1,0:T(8,128)(2,1)S(1)} collective-permute-done((bf16[8,4,16,256]{3,2,1,0:T(8,128)(2,1)S(1)}, bf16[8,4,16,256]{3,2,1,0:T(8,128)(2,1)S(1)}, u32[]{:S(2)}, u32[]{:S(2)}) %collective-permute-start.3) | collective-permute-done | bytes 262176 | tf_op jit(solution)/shard_map/ppermute | solution.py:396
  12.8 0.9 %shard_map.72 = (bf16[96,256]{1,0:T(8,128)(2,1)S(1)}, bf16[192,256]{1,0:T(8,128)(2,1)S(1)}, f32[288,256]{1,0:T(8,128)S(1)}, bf16[288,256]{1,0:T(8,128)(2,1)S(1)}, f32[288,256]{1,0:T(8,128)S(1)}) custom-call(bf16[2,768,512]{2,1,0:T(8,128)(2,1)S(1)} %shard_map.69._.feats_t, bf16[8,4,16,256]{3,2,1,0:T(8,128)(2,1)S(1)} %collective-permute-done.3.other, ...), custom_call_target="tpu_custom_call" | custom-call | flops 603979776 | bytes 5079040 | tf_op jit(solution)/shard_map/pallas_call | solution.py:129
  13.7 1.8 %collective-permute-start.5 = (bf16[96,256]{1,0:T(8,128)(2,1)S(1)}, bf16[96,256]{1,0:T(8,128)(2,1)S(1)}, u32[]{:S(2)}, u32[]{:S(2)}) collective-permute-start(bf16[96,256]{1,0:T(8,128)(2,1)S(1)} %get-tuple-element.20), channel_id=1, source_target_pairs={{0,2},{2,0},{4,6},{6,4},{1,3},{3,1},{5,7},{7,5},{8,10},{10,8},{12,... | collective-permute-start | bytes 147464 | tf_op jit(solution)/shard_map/ppermute | solution.py:417
  15.4 0.3 %collective-permute-start.9 = (bf16[192,256]{1,0:T(8,128)(2,1)S(1)}, bf16[192,256]{1,0:T(8,128)(2,1)S(1)}, u32[]{:S(2)}, u32[]{:S(2)}) collective-permute-start(bf16[192,256]{1,0:T(8,128)(2,1)S(1)} %get-tuple-element.24), channel_id=1, source_target_pairs={{0,2},{2,0},{4,6},{6,4},{1,3},{3,1},{5,7},{7,5},{8,10},{10,8},{12,... | collective-permute-start | bytes 294920 | tf_op jit(solution)/shard_map/ppermute | solution.py:418
  15.8 1.7 %collective-permute-start.4 = (bf16[288,256]{1,0:T(8,128)(2,1)S(1)}, bf16[288,256]{1,0:T(8,128)(2,1)S(1)}, u32[]{:S(2)}, u32[]{:S(2)}) collective-permute-start(bf16[288,256]{1,0:T(8,128)(2,1)S(1)} %get-tuple-element.18), channel_id=1, source_target_pairs={{0,2},{2,0},{4,6},{6,4},{1,3},{3,1},{5,7},{7,5},{8,10},{10,8},{12,... | collective-permute-start | bytes 442376 | tf_op jit(solution)/shard_map/ppermute | solution.py:419
  17.5 0.0 collective-permute-done.6.arrived
  17.5 0.1 collective-permute-start.8
  17.6 0.2 collective-permute-done.5.arrived
  17.8 4.5 %collective-permute-start.7 = (bf16[96,256]{1,0:T(8,128)(2,1)S(1)}, bf16[96,256]{1,0:T(8,128)(2,1)S(1)}, u32[]{:S(2)}, u32[]{:S(2)}) collective-permute-start(bf16[96,256]{1,0:T(8,128)(2,1)S(1)} %shard_map.74.rest_0_), channel_id=1, source_target_pairs={{0,6},{2,4},{4,2},{6,0},{1,7},{3,5},{5,3},{7,1},{8,14},{10,12},{12... | collective-permute-start | bytes 147464 | tf_op jit(solution)/shard_map/ppermute | solution.py:432
  22.3 0.0 collective-permute-done.9.arrived
  22.3 0.0 collective-permute-done.8.first_in.rest_1_
  22.4 2.1 %collective-permute-start.10 = (bf16[192,256]{1,0:T(8,128)(2,1)S(1)}, bf16[192,256]{1,0:T(8,128)(2,1)S(1)}, u32[]{:S(2)}, u32[]{:S(2)}) collective-permute-start(bf16[192,256]{1,0:T(8,128)(2,1)S(1)} %shard_map.76._), channel_id=1, source_target_pairs={{0,6},{2,4},{4,2},{6,0},{1,7},{3,5},{5,3},{7,1},{8,14},{10,12},{12... | collective-permute-start | bytes 294920 | tf_op jit(solution)/shard_map/ppermute | solution.py:440
  24.5 1.5 %shard_map.77 = (bf16[512,256]{1,0:T(8,128)(2,1)}, f32[8,128]{1,0:T(8,128)S(1)}) custom-call(bf16[512,256]{1,0:T(8,128)(2,1)S(1)} %bitcast.12, bf16[8,4,16,256]{3,2,1,0:T(8,128)(2,1)S(1)} %bitcast.7, bf16[8,4,16,256]{3,2,1,0:T(8,128)(2,1)S(1)} %collective-permute-done.3.other, bf16[2304,256]{1,0:T(8,128)(2,1)S(1)} %copy-done.3, bf16[192,256]{1,0:T(8,128)(2,1)S(1)} %shard_map.76._), custom_call_target="tpu_custom_call" | custom-call | flops 603979776 | bytes 2330624 | tf_op jit(solution)/shard_map/pallas_call | solution.py:129
  26.0 0.9 %shard_map.75.refs_3_.block = bf16[512,256]{1,0:T(8,128)(2,1)S(1)} custom-call(bf16[512,256]{1,0:T(8,128)(2,1)S(1)} %bitcast.8, bf16[2,512,256]{2,1,0:T(8,128)(2,1)S(1)} %get-tuple-element.21.act, bf16[512,256]{1,0:T(8,128)(2,1)S(1)} %collective-permute-done.8.first_in.rest_1_, bf16[512,256]{1,0:T(8,128)(2,1)S(1)} %get-tuple-element.23.second_in, ...), custom_call_target="tpu_custom_call" | custom-call | flops 603979776 | bytes 2752512 | tf_op jit(solution)/shard_map/pallas_call | solution.py:129
  26.9 0.0 collective-permute-done.4.refs_1_.near
  26.9 0.8 %collective-permute-done.7.refs_0_.last = bf16[96,256]{1,0:T(8,128)(2,1)S(1)} collective-permute-done((bf16[96,256]{1,0:T(8,128)(2,1)S(1)}, bf16[96,256]{1,0:T(8,128)(2,1)S(1)}, u32[]{:S(2)}, u32[]{:S(2)}) %collective-permute-start.7) | collective-permute-done | bytes 49184 | tf_op jit(solution)/shard_map/ppermute | solution.py:432
  27.7 0.7 %shard_map.79 = (f32[288,256]{1,0:T(8,128)}, bf16[512,256]{1,0:T(8,128)(2,1)}) custom-call(f32[288,256]{1,0:T(8,128)S(1)} %get-tuple-element.17.keep, bf16[288,256]{1,0:T(8,128)(2,1)S(1)} %collective-permute-done.4.refs_1_.near, bf16[96,256]{1,0:T(8,128)(2,1)S(1)} %collective-permute-done.7.refs_0_.last, bf16[512,256]{1,0:T(8,128)(2,1)S(1)} %shard_map.75.refs_3_.block, ...), custom_call_target="tpu_custom_call" | custom-call | tf_op jit(solution)/shard_map/pallas_call | solution.py:458
  28.4 0.5 %collective-permute-done.10.last = bf16[192,256]{1,0:T(8,128)(2,1)S(1)} collective-permute-done((bf16[192,256]{1,0:T(8,128)(2,1)S(1)}, bf16[192,256]{1,0:T(8,128)(2,1)S(1)}, u32[]{:S(2)}, u32[]{:S(2)}) %collective-permute-start.10) | collective-permute-done | bytes 98336 | tf_op jit(solution)/shard_map/ppermute | solution.py:440
  28.9 0.7 %shard_map.80 = f32[288,256]{1,0:T(8,128)} custom-call(f32[288,256]{1,0:T(8,128)S(1)} %get-tuple-element.17.keep, bf16[288,256]{1,0:T(8,128)(2,1)S(1)} %collective-permute-done.4.refs_1_.near, bf16[192,256]{1,0:T(8,128)(2,1)S(1)} %collective-permute-done.10.last, f32[288,256]{1,0:T(8,128)} %get-tuple-element.28._), custom_call_target="tpu_custom_call", output_to_operand_aliasing={{}: (3, {})} | custom-call | tf_op jit(solution)/shard_map/pallas_call | solution.py:469
  (5 shorter events, 0.1 us)
Async XLA Ops:
  0.6 4.8 %copy-start.1 = (bf16[8,4,16,256]{3,2,1,0:T(8,128)(2,1)S(1)}, bf16[8,4,16,256]{3,2,1,0:T(8,128)(2,1)}, u32[]{:S(2)}) copy-start(bf16[8,4,16,256]{3,2,1,0:T(8,128)(2,1)} %own.3) | copy-start | bytes 786436
  0.6 4.8 %copy-start.3 = (bf16[2304,256]{1,0:T(8,128)(2,1)S(1)}, bf16[2304,256]{1,0:T(8,128)(2,1)}, u32[]{:S(2)}) copy-start(bf16[2304,256]{1,0:T(8,128)(2,1)} %weight.7) | copy-start | bytes 3538948
  0.6 9.0 %collective-permute-start.1 = (bf16[512,256]{1,0:T(8,128)(2,1)}, bf16[512,256]{1,0:T(8,128)(2,1)S(1)}, u32[]{:S(2)}, u32[]{:S(2)}) collective-permute-start(bf16[512,256]{1,0:T(8,128)(2,1)} %bitcast.9), channel_id=1, source_target_pairs={{0,2},{2,4},{4,6},{3,1},{5,3},{7,5},{6,7},{1,0},{8,10},{10,12},{12... | collective-permute-start | bytes 786440 | tf_op jit(solution)/shard_map/ppermute | solution.py:368
  3.7 6.6 %collective-permute-start.2 = (bf16[512,256]{1,0:T(8,128)(2,1)}, bf16[512,256]{1,0:T(8,128)(2,1)S(1)}, u32[]{:S(2)}, u32[]{:S(2)}) collective-permute-start(bf16[512,256]{1,0:T(8,128)(2,1)} %bitcast.10), channel_id=1, source_target_pairs={{2,0},{4,2},{6,4},{1,3},{3,5},{5,7},{7,6},{0,1},{10,8},{12,10},{14... | collective-permute-start | bytes 786440 | tf_op jit(solution)/shard_map/ppermute | solution.py:369
  3.7 1.7 %collective-permute-start = (bf16[8,4,16,256]{3,2,1,0:T(8,128)(2,1)}, bf16[8,4,16,256]{3,2,1,0:T(8,128)(2,1)S(1)}, u32[]{:S(2)}, u32[]{:S(2)}) collective-permute-start(bf16[8,4,16,256]{3,2,1,0:T(8,128)(2,1)} %own.3), channel_id=1, source_target_pairs={{0,1},{1,0},{2,3},{3,2},{4,5},{5,4},{6,7},{7,6},{8,9},{9,8},{10,11... | collective-permute-start | bytes 786440 | tf_op jit(solution)/shard_map/ppermute | solution.py:370
  7.2 3.1 %copy-start = (bf16[2304,256]{1,0:T(8,128)(2,1)S(1)}, bf16[2304,256]{1,0:T(8,128)(2,1)}, u32[]{:S(2)}) copy-start(bf16[2304,256]{1,0:T(8,128)(2,1)} %weight.6) | copy-start | bytes 3538948
  7.2 3.1 %copy-start.2 = (bf16[8,4,16,256]{3,2,1,0:T(8,128)(2,1)S(1)}, bf16[8,4,16,256]{3,2,1,0:T(8,128)(2,1)}, u32[]{:S(2)}) copy-start(bf16[8,4,16,256]{3,2,1,0:T(8,128)(2,1)} %param.5) | copy-start | bytes 786436
  7.2 10.3 %collective-permute-start.6 = (bf16[2,512,256]{2,1,0:T(8,128)(2,1)S(1)}, bf16[2,512,256]{2,1,0:T(8,128)(2,1)S(1)}, u32[]{:S(2)}, u32[]{:S(2)}) collective-permute-start(bf16[2,512,256]{2,1,0:T(8,128)(2,1)S(1)} %get-tuple-element.21.act), channel_id=1, source_target_pairs={{2,0},{4,2},{6,4},{1,3},{3,5},{5,7},{7,6},{0,1},{10,8},{12,10},{14... | collective-permute-start | bytes 1572872 | tf_op jit(solution)/shard_map/ppermute | solution.py:380
  11.2 1.6 %collective-permute-start.3 = (bf16[8,4,16,256]{3,2,1,0:T(8,128)(2,1)S(1)}, bf16[8,4,16,256]{3,2,1,0:T(8,128)(2,1)S(1)}, u32[]{:S(2)}, u32[]{:S(2)}) collective-permute-start(bf16[8,4,16,256]{3,2,1,0:T(8,128)(2,1)S(1)} %bitcast.5), channel_id=1, source_target_pairs={{0,1},{1,0},{2,3},{3,2},{4,5},{5,4},{6,7},{7,6},{8,9},{9,8},{10,11... | collective-permute-start | bytes 786440 | tf_op jit(solution)/shard_map/ppermute | solution.py:396
  13.7 4.2 %collective-permute-start.5 = (bf16[96,256]{1,0:T(8,128)(2,1)S(1)}, bf16[96,256]{1,0:T(8,128)(2,1)S(1)}, u32[]{:S(2)}, u32[]{:S(2)}) collective-permute-start(bf16[96,256]{1,0:T(8,128)(2,1)S(1)} %get-tuple-element.20), channel_id=1, source_target_pairs={{0,2},{2,0},{4,6},{6,4},{1,3},{3,1},{5,7},{7,5},{8,10},{10,8},{12,... | collective-permute-start | bytes 147464 | tf_op jit(solution)/shard_map/ppermute | solution.py:417
  15.4 6.9 %collective-permute-start.9 = (bf16[192,256]{1,0:T(8,128)(2,1)S(1)}, bf16[192,256]{1,0:T(8,128)(2,1)S(1)}, u32[]{:S(2)}, u32[]{:S(2)}) collective-permute-start(bf16[192,256]{1,0:T(8,128)(2,1)S(1)} %get-tuple-element.24), channel_id=1, source_target_pairs={{0,2},{2,0},{4,6},{6,4},{1,3},{3,1},{5,7},{7,5},{8,10},{10,8},{12,... | collective-permute-start | bytes 294920 | tf_op jit(solution)/shard_map/ppermute | solution.py:418
  15.8 11.1 %collective-permute-start.4 = (bf16[288,256]{1,0:T(8,128)(2,1)S(1)}, bf16[288,256]{1,0:T(8,128)(2,1)S(1)}, u32[]{:S(2)}, u32[]{:S(2)}) collective-permute-start(bf16[288,256]{1,0:T(8,128)(2,1)S(1)} %get-tuple-element.18), channel_id=1, source_target_pairs={{0,2},{2,0},{4,6},{6,4},{1,3},{3,1},{5,7},{7,5},{8,10},{10,8},{12,... | collective-permute-start | bytes 442376 | tf_op jit(solution)/shard_map/ppermute | solution.py:419
  17.5 4.8 %collective-permute-start.8 = (bf16[512,256]{1,0:T(8,128)(2,1)S(1)}, bf16[512,256]{1,0:T(8,128)(2,1)S(1)}, u32[]{:S(2)}, u32[]{:S(2)}) collective-permute-start(bf16[512,256]{1,0:T(8,128)(2,1)S(1)} %get-tuple-element.22.rest_0_), channel_id=1, source_target_pairs={{0,1},{1,0},{2,3},{3,2},{4,5},{5,4},{6,7},{7,6},{8,9},{9,8},{10,11... | collective-permute-start | bytes 786440 | tf_op jit(solution)/shard_map/ppermute | solution.py:423
  17.8 9.8 %collective-permute-start.7 = (bf16[96,256]{1,0:T(8,128)(2,1)S(1)}, bf16[96,256]{1,0:T(8,128)(2,1)S(1)}, u32[]{:S(2)}, u32[]{:S(2)}) collective-permute-start(bf16[96,256]{1,0:T(8,128)(2,1)S(1)} %shard_map.74.rest_0_), channel_id=1, source_target_pairs={{0,6},{2,4},{4,2},{6,0},{1,7},{3,5},{5,3},{7,1},{8,14},{10,12},{12... | collective-permute-start | bytes 147464 | tf_op jit(solution)/shard_map/ppermute | solution.py:432
  22.4 6.5 %collective-permute-start.10 = (bf16[192,256]{1,0:T(8,128)(2,1)S(1)}, bf16[192,256]{1,0:T(8,128)(2,1)S(1)}, u32[]{:S(2)}, u32[]{:S(2)}) collective-permute-start(bf16[192,256]{1,0:T(8,128)(2,1)S(1)} %shard_map.76._), channel_id=1, source_target_pairs={{0,6},{2,4},{4,2},{6,0},{1,7},{3,5},{5,3},{7,1},{8,14},{10,12},{12... | collective-permute-start | bytes 294920 | tf_op jit(solution)/shard_map/ppermute | solution.py:440
